TPU v7x, 256 devices: a whole 4x4x8 slice. The times are simulated.
256 devices in a mesh: section: 4 (over x_hi, core), dp: 64 (over z, y, x_lo).
Axes of the slice: x: 4 (x_hi: 2, x_lo: 2; x = x_hi * 2 + x_lo), y: 4, z: 8, core: 2. Of those that a mesh axis runs over, the one named last changes fastest.
Arguments:
- partials: bfloat16 [4, 256, 64, 1280], P('section', 'dp'), may hold values from -6 to 6
- latents: bfloat16 [256, 64, 1280], P('dp'), may hold values from -6 to 6
- features: bfloat16 [256, 257, 1280], P('dp'), may hold values from -6 to 6
- feature_gain: float32 [1280], replicated, may hold values from 0.1 to 1.9
- latent_gain: float32 [1280], replicated, may hold values from 0.1 to 1.9
- query_weight: bfloat16 [1280, 768], replicated, may hold values from -6 to 6
- kv_weight: bfloat16 [1280, 1536], replicated, may hold values from -6 to 6
- out_weight: bfloat16 [768, 1280], replicated, may hold values from -0.21875 to 0.21875
- sample_of: int32 [64, 4], P('dp'), may hold values from 0 to 1, never falling along the last dimension, each value on 1 to 3 neighbouring positions
- owner: int32 [256, 1], P('dp'), may hold values from 0 to 3; in each aligned block of 4 rows (0 to 3, 4 to 7, ...) at most 2 rows name the same one
Outputs:
- latent_grad: bfloat16 [4, 128, 64, 1280], P('section', 'dp')
- kv_grad: float32 [1280, 1536], P('dp', 'section')
Inputs may be any that keep to these rules, and one draw needn't show every extreme that they name: `owner`: in each aligned block of 4 rows (the images of one index of dp) at most 2 rows name one section, a bound that some block reaches. `sample_of`: each row numbers the samples of its images in order, never falling, each sample having 1 to 3 images.
All inputs are finite; a program needn't handle non-finite values.
Results may differ from a plain program's by a relative error of at most 0.015.
The roundings to bfloat16 on the way count: a program that leaves them out, or rounds other values in their place, can miss the bound.
Values may be sent and summed in bfloat16 or wider, within the bound.
No kernel may reach another device: no remote copies, remote signals or barrier semaphores. Data moves between devices by JAX's collectives and lax.ppermute only.
A program may use at most 64 MiB of HBM per device.

v0:
```python
import jax
import jax.numpy as jnp
from jax import lax
from jax.sharding import PartitionSpec as P

HEAD_DIM = 96
IMG_DEV = 4
CAP = 2


norm_epsilon = 1e-05


def product(form, left, right):
    return jnp.einsum(form, left, right, preferred_element_type=jnp.float32)


def layer_stats(values):
    centred = values - jnp.mean(values, axis=-1, keepdims=True)
    inverse = lax.rsqrt(jnp.mean(centred * centred, axis=-1, keepdims=True) + norm_epsilon)
    return (centred * inverse, inverse)


def resampler_backward(
    upstream,
    latent_rows,
    patch_rows,
    feature_gain,
    latent_gain,
    query_weight,
    kv_weight,
    out_weight,
):
    count = upstream.shape[0]
    patches = patch_rows.shape[1]
    latent_count = latent_rows.shape[1]
    inner_width = query_weight.shape[1]
    heads_total = inner_width // HEAD_DIM
    factor = HEAD_DIM ** (-0.5)
    patch_hat, _ = layer_stats(patch_rows.astype(jnp.float32))
    normed_patches = (patch_hat * feature_gain).astype(jnp.bfloat16)
    latent_hat, latent_inverse = layer_stats(latent_rows.astype(jnp.float32))
    normed_latents = (latent_hat * latent_gain).astype(jnp.bfloat16)
    context = jnp.concatenate([normed_patches, normed_latents], axis=1)
    context_len = patches + latent_count
    queries = product("nld,de->nle", normed_latents, query_weight).astype(jnp.bfloat16)
    keyvals = product("ncd,de->nce", context, kv_weight).astype(jnp.bfloat16)
    query_heads = queries.reshape(count, latent_count, heads_total, HEAD_DIM)
    key_heads = keyvals[..., :inner_width].reshape(count, context_len, heads_total, HEAD_DIM)
    value_heads = keyvals[..., inner_width:].reshape(count, context_len, heads_total, HEAD_DIM)
    scores = product("nqhd,nkhd->nhqk", query_heads, key_heads) * factor
    shifted = jnp.exp(scores - jnp.max(scores, axis=-1, keepdims=True))
    probs = shifted / jnp.sum(shifted, axis=-1, keepdims=True)
    probs_low = probs.astype(jnp.bfloat16)
    attn_grad = product("nld,ed->nle", upstream, out_weight).astype(jnp.bfloat16)
    attn_heads = attn_grad.reshape(count, latent_count, heads_total, HEAD_DIM)
    prob_grad = product("nqhd,nkhd->nhqk", attn_heads, value_heads)
    value_grad = product("nhqk,nqhd->nkhd", probs_low, attn_heads)
    score_grad = (
        probs * (prob_grad - jnp.sum(probs * prob_grad, axis=-1, keepdims=True)) * factor
    ).astype(jnp.bfloat16)
    query_grad = (
        product("nhqk,nkhd->nqhd", score_grad, key_heads)
        .astype(jnp.bfloat16)
        .reshape(count, latent_count, inner_width)
    )
    key_grad = product("nhqk,nqhd->nkhd", score_grad, query_heads).reshape(
        count, context_len, inner_width
    )
    keyval_grad = jnp.concatenate(
        [key_grad, value_grad.reshape(count, context_len, inner_width)], axis=-1
    ).astype(jnp.bfloat16)
    weight_term = product("ncd,nce->de", context, keyval_grad)
    normed_grad = product("nle,de->nld", query_grad, query_weight) + product(
        "nle,de->nld", keyval_grad[:, patches:], kv_weight
    )
    dy_rows = normed_grad * latent_gain
    centred = (
        dy_rows
        - jnp.mean(dy_rows, axis=-1, keepdims=True)
        - latent_hat * jnp.mean(dy_rows * latent_hat, axis=-1, keepdims=True)
    )
    image_grad = (upstream.astype(jnp.float32) + latent_inverse * centred).astype(jnp.bfloat16)
    return (image_grad, weight_term)


def select_rows(picker, values):
    return product("ci,ild->cld", picker.astype(jnp.bfloat16), values).astype(jnp.bfloat16)


def per_device(
    partials,
    latents,
    features,
    feature_gain,
    latent_gain,
    query_weight,
    kv_weight,
    out_weight,
    sample_of,
    owner,
):
    sections = lax.axis_size("section")
    here = lax.axis_index("section")
    groups = sample_of[0]
    same = (groups[:, None] == groups[None, :]).astype(jnp.float32)
    scale = 1.0 / jnp.sum(same, axis=-1)
    owners = owner[:, 0]
    positions = jnp.arange(IMG_DEV, dtype=jnp.int32)
    before = (owners[None, :] == owners[:, None]) & (positions[None, :] < positions[:, None])
    ranking = jnp.sum(before.astype(jnp.int32), axis=-1)
    section_ids = jnp.arange(sections, dtype=jnp.int32)
    slot_ids = jnp.arange(CAP, dtype=jnp.int32)
    placing = (
        (owners[None, None, :] == section_ids[:, None, None])
        & (ranking[None, None, :] == slot_ids[None, :, None])
    ).astype(jnp.float32)
    partial_wide = partials[0].astype(jnp.float32)
    mine = lax.dynamic_index_in_dim(placing, here, 0, keepdims=False)
    summed = lax.psum(partial_wide.astype(jnp.bfloat16), "section").astype(jnp.float32)
    upstream = jnp.einsum("ci,ild->cld", mine, summed * scale[:, None, None]).astype(jnp.bfloat16)
    image_grad, weight_term = resampler_backward(
        upstream,
        select_rows(mine, latents),
        select_rows(mine, features),
        feature_gain,
        latent_gain,
        query_weight,
        kv_weight,
        out_weight,
    )
    row_share = lax.psum_scatter(weight_term, "dp", scatter_dimension=0, tiled=True)
    kv_share = lax.psum_scatter(row_share, "section", scatter_dimension=1, tiled=True)
    kv_grad = kv_share * (1.0 / (IMG_DEV * lax.axis_size("dp")))
    return (image_grad[None], kv_grad)


def solution(mesh):
    return jax.shard_map(
        per_device,
        mesh=mesh,
        in_specs=(
            P("section", "dp", None, None),
            P("dp", None, None),
            P("dp", None, None),
            P(),
            P(),
            P(),
            P(),
            P(),
            P("dp", None),
            P("dp", None),
        ),
        out_specs=(P("section", "dp", None, None), P("dp", "section")),
        check_vma=False,
    )
```

profile of v0, /device:TPU:8, one launch (start us, length us, event | category | flops | bytes accessed | tf_op | source)
XLA Modules:
  0.0 435.5 jit_solution(12244995519078873243)
XLA Ops:
  7.2 0.7 all-reduce.4.cloned.1.call-update
  7.9 0.0 reduce-scatter.4.cloned.1.call-start
  8.0 0.9 convert_reduce_fusion.2
  8.9 0.7 iota_compare_fusion.1
  9.6 1.8 fusion.86
  11.4 0.5 multiply_reduce_fusion.2
  11.9 1.7 convert_reduce_fusion
  13.6 1.9 fusion.12
  15.5 0.5 multiply_convert_fusion.1
  16.0 2.3 fusion.14
  18.3 2.1 pad_maximum_fusion
  20.4 3.0 fusion.7
  23.4 1.4 fusion.85
  24.8 0.9 copy-done.1
  25.7 1.1 fusion.41
  26.8 2.4 copy.69
  29.2 1.3 reshape.120
  30.5 2.4 copy.73
  32.8 1.3 dynamic-slice.4
  34.7 0.9 convert_reduce_fusion.1
  35.7 0.5 broadcast_divide_fusion.1
  36.2 3.6 fusion.87
  39.8 21.7 %all-reduce.4.cloned.1.call-done = bf16[4,64,1280]{2,1,0:T(8,128)(2,1)} async-done(((bf16[4,64,1280]{2,1,0:T(8,128)(2,1)}), bf16[4,64,1280]{2,1,0:T(8,128)(2,1)}) %all-reduce.4.cloned.1.call-update) | async-done | bytes 655376 | tf_op jit(solution)/shard_map/psum | solution.py:120
  61.6 1.4 convert_multiply_fusion
  63.0 0.6 convolution_convert_fusion.2
  63.6 0.7 copy-done.10
  64.3 1.5 fusion.44
  65.8 2.0 reshape.121
  67.8 3.0 fusion.62
  70.8 1.6 convolution_convert_fusion.3
  72.4 9.5 %convolution_convert_fusion.4 = bf16[2,8,96,321]{3,2,1,0:T(8,128)(2,1)} fusion(f32[2,8,64,321]{3,2,1,0:T(8,128)} %fusion.62, bf16[2,64,8,96]{3,2,1,0:T(8,128)(2,1)S(1)} %reshape.120, f32[2,8,64,321]{3,2,1,0:T(8,128)} %get-tuple-element.20, f32[2,8,64]{2,1,0:T(8,128)} %get-tuple-element.19), kind=kOutput, calls=%fused_computation.34 | convolution fusion | flops 65906496 | bytes 3816448 | tf_op jit(solution)/shard_map/nhqk,nqhd->nkhd/dot_general | solution.py:15
  81.9 9.4 %fusion.47 = bf16[2,64,8,96]{3,1,2,0:T(8,128)(2,1)} fusion(bf16[2,321,8,96]{1,3,2,0:T(8,128)(2,1)} %bitcast.60, f32[2,8,64,321]{3,2,1,0:T(8,128)} %fusion.62, f32[2,8,64,321]{3,2,1,0:T(8,128)} %get-tuple-element.20, f32[2,8,64]{2,1,0:T(8,128)} %get-tuple-element.19), kind=kOutput, calls=%fused_computation.45 | convolution fusion | flops 65511744 | bytes 3816448 | tf_op jit(solution)/shard_map/nhqk,nkhd->nqhd/dot_general | solution.py:15
  91.4 2.3 copy.79
  93.7 2.3 copy.78
  96.0 4.7 %fusion.3 = f32[2,64,1280]{2,1,0:T(8,128)} fusion(bf16[1280,1536]{1,0:T(8,128)(2,1)} %param.16, bf16[2,321,768]{2,1,0:T(8,128)(2,1)} %copy.79, bf16[2,321,768]{2,1,0:T(8,128)(2,1)} %copy.78), kind=kOutput, calls=%fused_computation.3 | convolution fusion | flops 504102912 | bytes 6559744 | tf_op jit(solution)/shard_map/nle,de->nld/dot_general | solution.py:15
  100.8 5.6 %convolution_bitcast_fusion = f32[1280,1536]{1,0:T(8,128)} fusion(bf16[2,321,768]{2,1,0:T(8,128)(2,1)S(1)} %copy-done.2, bf16[2,321,768]{2,1,0:T(8,128)(2,1)S(1)} %copy-done.3, bf16[2,321,1280]{2,0,1:T(2,128)(2,1)S(1)} %copy-done.8), kind=kOutput, calls=%fused_computation.2 | convolution fusion | flops 2528391168 | bytes 11480064 | tf_op jit(solution)/shard_map/ncd,nce->de/dot_general | solution.py:15
  106.4 211.0 %fusion = f32[24,1536]{1,0:T(8,128)} fusion(f32[1280,1536]{1,0:T(8,128)} %convolution_bitcast_fusion), kind=kCustom, calls=%all-reduce-scatter | all-reduce-scatter fusion | flops 2359297 | bytes 8012800
  317.4 1.5 slice.14
  318.9 3.8 collective-permute-start.9
  322.7 1.9 collective-permute-start.8
  324.7 4.8 %collective-permute-start.7 = (f32[24,1536]{1,0:T(8,128)}, f32[24,1536]{1,0:T(8,128)}, u32[]{:S(2)}, u32[]{:S(2)}) collective-permute-start(f32[24,1536]{1,0:T(8,128)} %fusion), channel_id=1, source_target_pairs={{0,8},{1,9},{2,10},{3,11},{4,12},{5,13},{6,14},{7,15},{8,16},{9,17... | collective-permute-start | bytes 442376
  329.4 5.3 %collective-permute-start.6 = (f32[24,1536]{1,0:T(8,128)}, f32[24,1536]{1,0:T(8,128)}, u32[]{:S(2)}, u32[]{:S(2)}) collective-permute-start(f32[24,1536]{1,0:T(8,128)} %fusion), channel_id=1, source_target_pairs={{0,7},{1,8},{2,9},{3,10},{4,11},{5,12},{6,13},{7,14},{8,15},{9,16}... | collective-permute-start | bytes 442376
  334.7 1.1 copy.75
  335.9 0.9 reshape.123
  336.8 4.3 collective-permute-start.10
  341.1 2.4 fusion.21
  343.5 0.1 collective-permute-done.10
  343.6 0.6 copy-done.16
  344.2 2.6 collective-permute-start.5
  346.8 2.0 fusion.83
  348.8 8.3 %collective-permute-start.4 = (f32[24,1536]{1,0:T(8,128)}, f32[24,1536]{1,0:T(8,128)}, u32[]{:S(2)}, u32[]{:S(2)}) collective-permute-start(f32[24,1536]{1,0:T(8,128)} %fusion), channel_id=1, source_target_pairs={{0,5},{1,6},{2,7},{3,8},{4,9},{5,10},{6,11},{7,12},{8,13},{9,14},{... | collective-permute-start | bytes 442376
  357.1 4.8 %collective-permute-start.3 = (f32[24,1536]{1,0:T(8,128)}, f32[24,1536]{1,0:T(8,128)}, u32[]{:S(2)}, u32[]{:S(2)}) collective-permute-start(f32[24,1536]{1,0:T(8,128)} %fusion), channel_id=1, source_target_pairs={{0,4},{1,5},{2,6},{3,7},{4,8},{5,9},{6,10},{7,11},{8,12},{9,13},{1... | collective-permute-start | bytes 442376
  361.9 5.0 %collective-permute-start.2 = (f32[24,1536]{1,0:T(8,128)}, f32[24,1536]{1,0:T(8,128)}, u32[]{:S(2)}, u32[]{:S(2)}) collective-permute-start(f32[24,1536]{1,0:T(8,128)} %fusion), channel_id=1, source_target_pairs={{0,3},{1,4},{2,5},{3,6},{4,7},{5,8},{6,9},{7,10},{8,11},{9,12},{10... | collective-permute-start | bytes 442376
  366.9 2.4 collective-permute-start.1
  369.3 2.3 collective-permute-start
  371.7 0.6 broadcast_multiply_fusion.2
  372.3 2.5 collective-permute-done.1
  374.8 2.8 collective-permute-done
  377.6 19.6 %concatenate.9 = f32[276,1536]{1,0:T(8,128)} concatenate(f32[12,1536]{1,0:T(8,128)} %copy-done.16, f32[24,1536]{1,0:T(8,128)} %collective-permute-done.9, f32[24,1536]{1,0:T(8,128)} %collective-permute-done.8, f32[24,1536]{1,0:T(8,128)} %collective-permute-done.7, f32[24,1536]{1,0:T(8,128)} %collective-permute-done.6, f32[24,1536]{1,0:T(8,128)S(1)} %collective-permute-done.5, ...), dimensions={0} | concatenate | bytes 3391488
  397.1 1.6 constant_dynamic-slice_fusion
  398.7 2.1 fusion.60
  400.8 0.8 copy.83
  401.6 25.7 %reduce-scatter.4.cloned.1.call-done = f32[20,384]{1,0:T(8,128)} async-done(((f32[20,1536]{1,0:T(8,128)}), f32[20,384]{1,0:T(8,128)}) %reduce-scatter.4.cloned.1.call-update) | async-done | bytes 30736 | tf_op jit(solution)/shard_map/reduce_scatter | solution.py:133
  427.3 1.4 broadcast_multiply_fusion.1
  (55 shorter events, 0.2 us)
Async XLA Ops:
  7.2 4.7 %copy-start = (bf16[4,257,1280]{2,0,1:T(4,128)(2,1)S(1)}, bf16[4,257,1280]{2,0,1:T(4,128)(2,1)}, u32[]{:S(2)}) copy-start(bf16[4,257,1280]{2,0,1:T(4,128)(2,1)} %param.12) | copy-start | bytes 7895044
  7.2 54.4 %all-reduce.4.cloned.1.call-start = ((), (), s32[]{:S(2)}) async-start(), calls=%async_computation.1 | async-start | bytes 1310720 | tf_op jit(solution)/shard_map/psum | solution.py:120
  7.9 419.4 %reduce-scatter.4.cloned.1.call-start = ((), (), s32[]{:S(2)}) async-start(), calls=%async_computation.2 | async-start | bytes 184320 | tf_op jit(solution)/shard_map/reduce_scatter | solution.py:133
  11.4 4.1 copy-start.12
  11.9 3.6 copy-start.14
  13.5 2.0 copy-start.17
  13.5 2.4 copy-start.19
  16.0 4.4 %copy-start.4 = (bf16[1280,1536]{1,0:T(8,128)(2,1)S(1)}, bf16[1280,1536]{1,0:T(8,128)(2,1)}, u32[]{:S(2)}) copy-start(bf16[1280,1536]{1,0:T(8,128)(2,1)} %param.16) | copy-start | bytes 11796484
  20.4 3.0 copy-start.7
  23.4 2.3 copy-start.1
  61.6 2.8 copy-start.6
  63.6 0.7 copy-start.10
  67.8 3.0 copy-start.9
  67.8 3.0 copy-start.11
  67.8 3.0 copy-start.20
  96.0 4.7 %copy-start.2 = (bf16[2,321,768]{2,1,0:T(8,128)(2,1)S(1)}, bf16[2,321,768]{2,1,0:T(8,128)(2,1)}, u32[]{:S(2)}) copy-start(bf16[2,321,768]{2,1,0:T(8,128)(2,1)} %copy.79) | copy-start | bytes 2958340
  96.0 4.7 %copy-start.3 = (bf16[2,321,768]{2,1,0:T(8,128)(2,1)S(1)}, bf16[2,321,768]{2,1,0:T(8,128)(2,1)}, u32[]{:S(2)}) copy-start(bf16[2,321,768]{2,1,0:T(8,128)(2,1)} %copy.78) | copy-start | bytes 2958340
  96.0 4.7 %copy-start.8 = (bf16[2,321,1280]{2,0,1:T(2,128)(2,1)S(1)}, bf16[2,321,1280]{2,0,1:T(2,128)(2,1)}, u32[]{:S(2)}) copy-start(bf16[2,321,1280]{2,0,1:T(2,128)(2,1)} %copy-done.7) | copy-start | bytes 4930564
  318.9 29.9 %collective-permute-start.9 = (f32[24,1536]{1,0:T(8,128)}, f32[24,1536]{1,0:T(8,128)}, u32[]{:S(2)}, u32[]{:S(2)}) collective-permute-start(f32[24,1536]{1,0:T(8,128)} %fusion), channel_id=1, source_target_pairs={{0,10},{1,11},{2,12},{3,13},{4,14},{5,15},{6,16},{7,17},{8,18},{9,... | collective-permute-start | bytes 442376
  322.7 34.4 %collective-permute-start.8 = (f32[24,1536]{1,0:T(8,128)}, f32[24,1536]{1,0:T(8,128)}, u32[]{:S(2)}, u32[]{:S(2)}) collective-permute-start(f32[24,1536]{1,0:T(8,128)} %fusion), channel_id=1, source_target_pairs={{0,9},{1,10},{2,11},{3,12},{4,13},{5,14},{6,15},{7,16},{8,17},{9,1... | collective-permute-start | bytes 442376
  324.7 37.3 %collective-permute-start.7 = (f32[24,1536]{1,0:T(8,128)}, f32[24,1536]{1,0:T(8,128)}, u32[]{:S(2)}, u32[]{:S(2)}) collective-permute-start(f32[24,1536]{1,0:T(8,128)} %fusion), channel_id=1, source_target_pairs={{0,8},{1,9},{2,10},{3,11},{4,12},{5,13},{6,14},{7,15},{8,16},{9,17... | collective-permute-start | bytes 442376
  329.4 37.5 %collective-permute-start.6 = (f32[24,1536]{1,0:T(8,128)}, f32[24,1536]{1,0:T(8,128)}, u32[]{:S(2)}, u32[]{:S(2)}) collective-permute-start(f32[24,1536]{1,0:T(8,128)} %fusion), channel_id=1, source_target_pairs={{0,7},{1,8},{2,9},{3,10},{4,11},{5,12},{6,13},{7,14},{8,15},{9,16}... | collective-permute-start | bytes 442376
  336.8 10.0 %copy-start.5 = (f32[2,64,1280]{2,1,0:T(8,128)S(1)}, f32[2,64,1280]{2,1,0:T(8,128)}, u32[]{:S(2)}) copy-start(f32[2,64,1280]{2,1,0:T(8,128)} %fusion.3) | copy-start | bytes 1966084
  336.8 10.0 %copy-start.13 = (f32[2,64]{0,1:T(8,128)S(1)}, f32[2,64]{0,1:T(8,128)}, u32[]{:S(2)}) copy-start(f32[2,64]{0,1:T(8,128)} %copy-done.12) | copy-start | bytes 1540
  336.8 10.0 %copy-start.15 = (f32[2,64]{0,1:T(8,128)S(1)}, f32[2,64]{0,1:T(8,128)}, u32[]{:S(2)}) copy-start(f32[2,64]{0,1:T(8,128)} %copy-done.14) | copy-start | bytes 1540
  336.8 10.1 %copy-start.18 = (f32[1280]{0:T(1024)S(1)}, f32[1280]{0:T(1024)}, u32[]{:S(2)}) copy-start(f32[1280]{0:T(1024)} %param.14) | copy-start | bytes 15364
  336.8 6.8 %collective-permute-start.10 = (f32[12,1536]{1,0:T(8,128)}, f32[12,1536]{1,0:T(8,128)S(1)}, u32[]{:S(2)}, u32[]{:S(2)}) collective-permute-start(f32[12,1536]{1,0:T(8,128)} %slice.14), channel_id=1, source_target_pairs={{0,11},{1,12},{2,13},{3,14},{4,15},{5,16},{6,17},{7,18},{8,19},{9,... | collective-permute-start | bytes 221192
  343.6 0.6 copy-start.16
  344.2 25.1 %collective-permute-start.5 = (f32[24,1536]{1,0:T(8,128)}, f32[24,1536]{1,0:T(8,128)S(1)}, u32[]{:S(2)}, u32[]{:S(2)}) collective-permute-start(f32[24,1536]{1,0:T(8,128)} %fusion), channel_id=1, source_target_pairs={{0,6},{1,7},{2,8},{3,9},{4,10},{5,11},{6,12},{7,13},{8,14},{9,15},... | collective-permute-start | bytes 442376
  348.8 23.4 %collective-permute-start.4 = (f32[24,1536]{1,0:T(8,128)}, f32[24,1536]{1,0:T(8,128)}, u32[]{:S(2)}, u32[]{:S(2)}) collective-permute-start(f32[24,1536]{1,0:T(8,128)} %fusion), channel_id=1, source_target_pairs={{0,5},{1,6},{2,7},{3,8},{4,9},{5,10},{6,11},{7,12},{8,13},{9,14},{... | collective-permute-start | bytes 442376
  357.1 15.2 %collective-permute-start.3 = (f32[24,1536]{1,0:T(8,128)}, f32[24,1536]{1,0:T(8,128)}, u32[]{:S(2)}, u32[]{:S(2)}) collective-permute-start(f32[24,1536]{1,0:T(8,128)} %fusion), channel_id=1, source_target_pairs={{0,4},{1,5},{2,6},{3,7},{4,8},{5,9},{6,10},{7,11},{8,12},{9,13},{1... | collective-permute-start | bytes 442376
  361.9 10.3 %collective-permute-start.2 = (f32[24,1536]{1,0:T(8,128)}, f32[24,1536]{1,0:T(8,128)}, u32[]{:S(2)}, u32[]{:S(2)}) collective-permute-start(f32[24,1536]{1,0:T(8,128)} %fusion), channel_id=1, source_target_pairs={{0,3},{1,4},{2,5},{3,6},{4,7},{5,8},{6,9},{7,10},{8,11},{9,12},{10... | collective-permute-start | bytes 442376
  366.9 7.9 %collective-permute-start.1 = (f32[24,1536]{1,0:T(8,128)}, f32[24,1536]{1,0:T(8,128)}, u32[]{:S(2)}, u32[]{:S(2)}) collective-permute-start(f32[24,1536]{1,0:T(8,128)} %fusion), channel_id=1, source_target_pairs={{0,2},{1,3},{2,4},{3,5},{4,6},{5,7},{6,8},{7,9},{8,10},{9,11},{10,... | collective-permute-start | bytes 442376
  369.3 8.3 %collective-permute-start = (f32[24,1536]{1,0:T(8,128)}, f32[24,1536]{1,0:T(8,128)}, u32[]{:S(2)}, u32[]{:S(2)}) collective-permute-start(f32[24,1536]{1,0:T(8,128)} %fusion), channel_id=1, source_target_pairs={{0,1},{1,2},{2,3},{3,4},{4,5},{5,6},{6,7},{7,8},{8,9},{9,10},{10,1... | collective-permute-start | bytes 442376
Sparse Core Ops, SparseCore 0:
  10.7 50.8 all-reduce.3
  398.9 28.3 reduce-scatter.3
where the time goes:
time: 437 us; the launch traced here: 435 us
  blocking collectives  211 us (48%)
  waiting for transfers between devices  53.5 us (12%)
  matrix products  49.7 us (11%)
  starting transfers between devices  45.5 us (10%)
  local copies, waits for them, and re-layouts  43 us (10%)
  other arithmetic  17.8 us (4%)
  between operations  15 us (3%)
    unnamed x1, blocking collectives  211 us
    unnamed x11, starting transfers between devices  45.5 us
    dot_general x12, matrix products, product(): return jnp.einsum(form, left, right, preferred_element_type=jnp.float32)  45.4 us
    unnamed x47, local copies, waits for them, and re-layouts  27 us
    reduce_scatter x1, waiting for transfers between devices, per_device(): lax.psum_scatter(row_share, 'section', scatter_dimension=1, tiled=True)  25.7 us
    psum x1, waiting for transfers between devices, per_device(): lax.psum(partial_wide.astype(jnp.bfloat16), 'section').astype(jnp.float32)  21.7 us
  transfers between devices with their start and end apart: 13, of which 5 were waited for; matrix products, arithmetic and copies ran while one was open for 9% of the time, Pallas kernels for 0%

commit v1 on v0

v1 whole, which is shorter than its diff:
```python
import functools
import jax
import jax.numpy as jnp
from jax import lax
from jax.experimental import pallas as pl
from jax.experimental.pallas import tpu as pltpu
from jax.sharding import Mesh, PartitionSpec as P

HEAD = 96
IMGS = 4
LAT = 64
PATCH = 257
TOK = 321
ROWS = 336
D = 1280
INNER = 768
EPS = 1e-05
BF = jnp.bfloat16
F32 = jnp.float32
FACTOR = HEAD ** (-0.5)
SHARE = 20


def dot(a, b, ca, cb):
    return lax.dot_general(a, b, (((ca,), (cb,)), ((), ())), preferred_element_type=F32)


def pair_of(xh, co):
    return co * 2 + xh


def window_of(pair):
    return (pair // 2) * 384 + (pair % 2) * 128


def spread(pair):
    src = lax.broadcasted_iota(jnp.int32, (256, 256), 0)
    dst = lax.broadcasted_iota(jnp.int32, (256, 256), 1)
    lane = dst % 128
    hit = (lane < HEAD) & (src == (pair % 2) * 64 + (dst // 128) * HEAD + lane)
    return jnp.where(hit, 1.0, 0.0).astype(BF)


def layer_stats(x):
    centred = x - jnp.mean(x, axis=-1, keepdims=True)
    inverse = lax.rsqrt(jnp.mean(centred * centred, axis=-1, keepdims=True) + EPS)
    return centred * inverse, inverse


def slot_image(owner_ref, section, slot):
    found = jnp.int32(0)
    index = jnp.int32(0)
    seen = jnp.int32(0)
    for i in range(IMGS):
        mine = (owner_ref[i, 0] == section).astype(jnp.int32)
        take = (mine == 1) & (seen == slot)
        index = jnp.where(take, i, index)
        found = jnp.where(take, 1, found)
        seen = seen + mine
    return index, found


def scale_of(sample_ref, i):
    count = jnp.int32(0)
    for k in range(IMGS):
        count = count + (sample_ref[0, k] == sample_ref[0, i]).astype(jnp.int32)
    return count


def attn_kernel(owner_ref, part_ref, ow_ref, a0, a1, a2, a3, u1, u2, u3, prod):
    xh = lax.axis_index("xh")
    co = lax.axis_index("co")
    rows = part_ref[...].reshape(IMGS * LAT, D)
    prod[...] = dot(rows, ow_ref[...], 1, 1).astype(BF)
    for out, (dx, dc) in zip((a0, a1, a2, a3), ((0, 0), (0, 1), (1, 0), (1, 1))):
        pair = pair_of(xh ^ dx, co ^ dc)
        start = pl.multiple_of(window_of(pair), 128)
        out[...] = dot(prod[:, pl.ds(start, 256)], spread(pair), 1, 0).astype(BF)
    for out, (dx, dc) in zip((u1, u2, u3), ((0, 1), (1, 0), (1, 1))):
        section = (xh ^ dx) * 2 + (co ^ dc)
        for slot in range(2):
            index, _ = slot_image(owner_ref, section, slot)
            out[slot] = part_ref[index]


def forward_kernel(feat_ref, lat_ref, fg_ref, lg_ref, qw_hbm, kvw_hbm, ctx_ref, kv_ref, q_ref, pr_ref,
                   win, wp, sems):
    i = pl.program_id(0)

    @pl.when(i == 0)
    def _():
        xh = lax.axis_index("xh")
        co = lax.axis_index("co")
        pair = pair_of(xh, co)
        start = pl.multiple_of(window_of(pair), 128)
        copies = [
            pltpu.make_async_copy(qw_hbm.at[:, pl.ds(start, 256)], win.at[0], sems.at[0]),
            pltpu.make_async_copy(kvw_hbm.at[:, pl.ds(start, 256)], win.at[1], sems.at[1]),
            pltpu.make_async_copy(kvw_hbm.at[:, pl.ds(pl.multiple_of(start + INNER, 128), 256)], win.at[2], sems.at[2]),
        ]
        for c in copies:
            c.start()
        table = spread(pair)
        for k, c in enumerate(copies):
            c.wait()
            wp[:, 256 * k:256 * (k + 1)] = dot(win[k], table, 1, 0).astype(BF)

    patch_hat, _ = layer_stats(feat_ref[0].astype(F32))
    lat_hat, _ = layer_stats(lat_ref[0].astype(F32))
    normed = (lat_hat * lg_ref[...]).astype(BF)
    ctx_ref[0, 320:ROWS] = jnp.zeros((ROWS - 320, D), BF)
    ctx_ref[0, LAT:TOK] = (patch_hat * fg_ref[...]).astype(BF)
    ctx_ref[0, 0:LAT] = normed
    kv_ref[0] = dot(ctx_ref[0], wp[:, 256:], 1, 0).astype(BF)
    q_ref[0] = dot(normed, wp[:, :256], 1, 0).astype(BF)
    live = lax.broadcasted_iota(jnp.int32, (LAT, ROWS), 1) < TOK
    for h in range(2):
        lanes = slice(128 * h, 128 * (h + 1))
        scores = dot(q_ref[0, :, lanes], kv_ref[0, :, lanes], 1, 1) * FACTOR
        scores = jnp.where(live, scores, -1e30)
        shifted = jnp.exp(scores - jnp.max(scores, axis=-1, keepdims=True))
        shifted = jnp.where(live, shifted, 0.0)
        pr_ref[0, h] = shifted / jnp.sum(shifted, axis=-1, keepdims=True)


def backward_kernel(owner_ref, sample_ref, a0, a1, a2, a3, ctx_ref, kv_ref, q_ref, pr_ref,
                    w_ref, g0, g1, g2, g3, kvg, wide, order, lat):
    xh = lax.axis_index("xh")
    co = lax.axis_index("co")
    for i in range(IMGS):
        rows = slice(LAT * i, LAT * (i + 1))
        count = scale_of(sample_ref, i).astype(F32)
        total = (a0[rows].astype(F32) + a1[rows].astype(F32)) + (a2[rows].astype(F32) + a3[rows].astype(F32))
        attn = (total / count).astype(BF)
        grads = []
        for h in range(2):
            lanes = slice(128 * h, 128 * (h + 1))
            vlanes = slice(256 + 128 * h, 256 + 128 * (h + 1))
            probs = pr_ref[i, h]
            a = attn[:, lanes]
            value_grad = dot(probs.astype(BF), a, 0, 0)
            prob_grad = dot(a, kv_ref[i, :, vlanes], 1, 1)
            inner = jnp.sum(probs * prob_grad, axis=-1, keepdims=True)
            score_grad = (probs * (prob_grad - inner) * FACTOR).astype(BF)
            query_grad = dot(score_grad, kv_ref[i, :, lanes], 1, 0)
            key_grad = dot(score_grad, q_ref[i, :, lanes], 0, 0)
            lat[rows, lanes] = query_grad.astype(BF)
            lat[rows, 256 + 128 * h:256 + 128 * (h + 1)] = key_grad[:LAT].astype(BF)
            lat[rows, 512 + 128 * h:512 + 128 * (h + 1)] = value_grad[:LAT].astype(BF)
            grads.append((key_grad[:, :HEAD], value_grad[:, :HEAD]))
        kvg[ROWS * i:ROWS * (i + 1)] = jnp.concatenate(
            [grads[0][0], grads[1][0], grads[0][1], grads[1][1]], axis=1).astype(BF)
    table = spread(pair_of(xh, co))
    for k in range(3):
        lanes = slice(256 * k, 256 * (k + 1))
        lat[:, lanes] = dot(lat[:, lanes], table, 1, 1).astype(BF)
    for out, (dx, dc) in zip((g0, g1, g2, g3), ((0, 0), (0, 1), (1, 0), (1, 1))):
        section = (xh ^ dx) * 2 + (co ^ dc)
        for slot in range(2):
            index, _ = slot_image(owner_ref, section, slot)
            out[LAT * slot:LAT * (slot + 1)] = lat[pl.ds(pl.multiple_of(index * LAT, LAT), LAT)]
    ctx = ctx_ref[...].reshape(IMGS * ROWS, D)
    for c in range(5):
        wide[256 * c:256 * (c + 1)] = dot(ctx[:, 256 * c:256 * (c + 1)], kvg[...], 0, 0)
    for y in range(4):
        for xl in range(2):
            piece = xl * 4 + y
            for z in range(8):
                first = ((z * 4 + y) * 2 + xl) * SHARE
                block = wide[first:first + SHARE]
                to = z * SHARE
                order[piece, to:to + SHARE, :] = block
            whole = order[piece]
            keys = whole[:, :128], whole[:, 128:192]
            vals = whole[:, 256:], whole[:, 192:256]
            for k, (main, tail) in enumerate((keys, vals)):
                w_ref[8 * k + piece, 0:160] = main.astype(BF)
                w_ref[8 * k + piece, 160:240] = jnp.concatenate([tail[:80], tail[80:]], axis=1).astype(BF)


def first_sum_kernel(r_ref, out_ref, full):
    halves = []
    for k in range(2):
        total = r_ref[8 * k].astype(F32)
        for p in range(1, 8):
            total = total + r_ref[8 * k + p].astype(F32)
        main, tail = total[:160], total[160:]
        tail = jnp.concatenate([tail[:, :64], tail[:, 64:]], axis=0)
        halves.append((main, tail))
    return halves


def stage_kernel(r_ref, out_ref, full):
    here = lax.axis_index("xh")
    halves = first_sum_kernel(r_ref, out_ref, full)

    @pl.when(here == 0)
    def _():
        for k, (main, tail) in enumerate(halves):
            full[:, 192 * k:192 * (k + 1)] = jnp.concatenate([main, tail], axis=1)

    @pl.when(here == 1)
    def _():
        for k, (main, tail) in enumerate(halves):
            full[:, 192 * k:192 * (k + 1)] = jnp.concatenate([tail, main], axis=1)

    for z in range(8):
        out_ref[z, 0:SHARE] = full[SHARE * z:SHARE * (z + 1)].astype(BF)


def last_kernel(r_ref, out_ref):
    total = r_ref[0].astype(F32)
    for z in range(1, 8):
        total = total + r_ref[z].astype(F32)
    out_ref[...] = total[:SHARE] * (1.0 / 256.0)


def latent_kernel(owner_ref, sample_ref, part_ref, lat_ref, lg_ref, qw_ref, kvw_ref,
                  u1, u2, u3, g0, g1, g2, g3, out_ref):
    xh = lax.axis_index("xh")
    co = lax.axis_index("co")
    section = xh * 2 + co
    grad = jnp.zeros((2 * LAT, D), F32)
    for g, (dx, dc) in zip((g0, g1, g2, g3), ((0, 0), (0, 1), (1, 0), (1, 1))):
        start = pl.multiple_of(window_of(pair_of(xh ^ dx, co ^ dc)), 128)
        grad = grad + dot(g[:, 0:256], qw_ref[:, pl.ds(start, 256)], 1, 1)
        grad = grad + dot(g[:, 256:512], kvw_ref[:, pl.ds(start, 256)], 1, 1)
        grad = grad + dot(g[:, 512:768], kvw_ref[:, pl.ds(pl.multiple_of(start + INNER, 128), 256)], 1, 1)
    for slot in range(2):
        index, found = slot_image(owner_ref, section, slot)
        count = scale_of(sample_ref, index).astype(F32)
        summed = (part_ref[index].astype(F32) + u1[slot].astype(F32)) + (u2[slot].astype(F32) + u3[slot].astype(F32))
        upstream = (summed / count).astype(BF).astype(F32)
        hat, inverse = layer_stats(lat_ref[index].astype(F32))
        dy = grad[LAT * slot:LAT * (slot + 1)] * lg_ref[...]
        centred = dy - jnp.mean(dy, axis=-1, keepdims=True) - hat * jnp.mean(dy * hat, axis=-1, keepdims=True)
        out = (upstream + inverse * centred).astype(BF)
        out_ref[slot] = jnp.where(found == 1, out, jnp.zeros_like(out))


def call(body, outs, ins, scratch, flops=0, size=0, limit=40, grid=None, name=None):
    vm = pl.BlockSpec(memory_space=pltpu.VMEM)
    return pl.pallas_call(
        body,
        out_shape=outs,
        in_specs=ins,
        out_specs=jax.tree.map(lambda _: vm, outs),
        scratch_shapes=scratch,
        cost_estimate=pl.CostEstimate(flops=flops, bytes_accessed=size, transcendentals=0),
        compiler_params=pltpu.CompilerParams(vmem_limit_bytes=limit * 2**20),
        name=name,
    )


SMEM = pl.BlockSpec(memory_space=pltpu.SMEM)
VMEM = pl.BlockSpec(memory_space=pltpu.VMEM)
CORE = [(0, 1), (1, 0), (2, 3), (3, 2)]
FAR = [(0, 2), (2, 0), (1, 3), (3, 1)]
DIAGONAL = [(0, 3), (3, 0), (1, 2), (2, 1)]
SECTION = ("xh", "co")


def swap(x, pairs):
    return lax.ppermute(x, SECTION, pairs)


def per_device(partials, latents, features, feature_gain, latent_gain, query_weight, kv_weight, out_weight,
               sample_of, owner):
    part = partials[0]
    fg = feature_gain.reshape(1, D)
    lg = latent_gain.reshape(1, D)
    sd = jax.ShapeDtypeStruct
    a0, a1, a2, a3, u1, u2, u3 = call(
        attn_kernel,
        [sd((256, 256), BF)] * 4 + [sd((2, LAT, D), BF)] * 3,
        [SMEM, VMEM, VMEM],
        [pltpu.VMEM((256, INNER), BF)],
        flops=600_000_000, size=3_000_000, name="attn_part",
    )(owner, part, out_weight)
    a3 = swap(a3, DIAGONAL)
    a2 = swap(a2, FAR)
    a1 = swap(a1, CORE)
    whole = lambda *shape: pl.BlockSpec(shape, lambda i: (0,) * len(shape))
    image = lambda *shape: pl.BlockSpec((1,) + shape, lambda i: (i,) + (0,) * len(shape))
    ctx, kv, q, probs = pl.pallas_call(
        forward_kernel,
        grid=(IMGS,),
        out_shape=[sd((IMGS, ROWS, D), BF), sd((IMGS, ROWS, 512), BF), sd((IMGS, LAT, 256), BF),
                   sd((IMGS, 2, LAT, ROWS), F32)],
        in_specs=[image(PATCH, D), image(LAT, D), whole(1, D), whole(1, D),
                  pl.BlockSpec(memory_space=pl.ANY), pl.BlockSpec(memory_space=pl.ANY)],
        out_specs=[image(ROWS, D), image(ROWS, 512), image(LAT, 256), image(2, LAT, ROWS)],
        scratch_shapes=[pltpu.VMEM((3, D, 256), BF), pltpu.VMEM((D, 768), BF), pltpu.SemaphoreType.DMA((3,))],
        cost_estimate=pl.CostEstimate(flops=4_000_000_000, bytes_accessed=12_000_000, transcendentals=0),
        compiler_params=pltpu.CompilerParams(vmem_limit_bytes=40 * 2**20),
        name="forward_part",
    )(features, latents, fg, lg, query_weight, kv_weight)
    w, g0, g1, g2, g3 = call(
        backward_kernel,
        [sd((16, 240, 128), BF)] + [sd((2 * LAT, 768), BF)] * 4,
        [SMEM, SMEM] + [VMEM] * 8,
        [pltpu.VMEM((IMGS * ROWS, 384), BF), pltpu.VMEM((D, 384), F32), pltpu.VMEM((8, 160, 384), F32),
         pltpu.VMEM((256, 768), BF)],
        flops=4_000_000_000, size=10_000_000, name="backward_part",
    )(owner, sample_of, a0, a1, a2, a3, ctx, kv, q, probs)
    w = lax.all_to_all(w, ("xh", "xl", "y"), 0, 0, tiled=True)
    w = call(stage_kernel, sd((8, 32, 384), BF), [VMEM], [pltpu.VMEM((160, 384), F32)],
             size=1_000_000, name="first_sum")(w)
    u3 = swap(u3, DIAGONAL)
    u2 = swap(u2, FAR)
    u1 = swap(u1, CORE)
    g3 = swap(g3, DIAGONAL)
    g2 = swap(g2, FAR)
    g1 = swap(g1, CORE)
    w = lax.all_to_all(w, "z", 0, 0, tiled=True)
    kv_grad = call(last_kernel, sd((SHARE, 384), F32), [VMEM], [], size=300_000, name="last_sum")(w)
    latent_grad = call(
        latent_kernel, sd((2, LAT, D), BF), [SMEM, SMEM] + [VMEM] * 12, [],
        flops=1_000_000_000, size=9_000_000, name="latent_part",
    )(owner, sample_of, part, latents, lg, query_weight, kv_weight, u1, u2, u3, g0, g1, g2, g3)
    return latent_grad[None], kv_grad


def solution(mesh):
    fine = Mesh(mesh.devices.reshape(2, 2, 8, 4, 2), ("xh", "co", "z", "y", "xl"))
    dp = ("z", "y", "xl")
    return jax.shard_map(
        per_device,
        mesh=fine,
        in_specs=(
            P(SECTION, dp, None, None),
            P(dp, None, None),
            P(dp, None, None),
            P(),
            P(),
            P(),
            P(),
            P(),
            P(dp, None),
            P(dp, None),
        ),
        out_specs=(P(SECTION, dp, None, None), P(dp, SECTION)),
        check_vma=False,
    )
```

time: 437 us -> 95.7 us (0.22)
  the two profiles are of different devices: /device:TPU:8 before, /device:TPU:61 now
where the time goes in v1:
time: 95.7 us; the launch traced here: 95.2 us
  starting transfers between devices  40.7 us (43%)
  Pallas kernels  24 us (25%)
  waiting for transfers between devices  17.7 us (18%)
  local copies, waits for them, and re-layouts  12.2 us (13%)
    ppermute x9, starting transfers between devices, swap(): return lax.ppermute(x, SECTION, pairs)  26 us
    unnamed x30, local copies, waits for them, and re-layouts  11.5 us
    ppermute x9, waiting for transfers between devices, swap(): return lax.ppermute(x, SECTION, pairs)  9.45 us
    all_to_all x1, waiting for transfers between devices, per_device(): w = lax.all_to_all(w, ('xh', 'xl', 'y'), 0, 0, tiled=True)  8.25 us
    pallas_call x1, Pallas kernels, per_device(): pl.pallas_call(forward_kernel, grid=(IMGS,), out_shape=[sd((IMGS, ROWS, D...  8.19 us
    all_to_all x1, starting transfers between devices, per_device(): w = lax.all_to_all(w, 'z', 0, 0, tiled=True)  8.02 us
    pallas_call x1, Pallas kernels, per_device(): call(backward_kernel, [sd((16, 240, 128), BF)] + [sd((2 * LAT, 768), BF)]...  7.15 us
    all_to_all x1, starting transfers between devices, per_device(): w = lax.all_to_all(w, ('xh', 'xl', 'y'), 0, 0, tiled=True)  6.68 us
  transfers between devices with their start and end apart: 11, of which 3 were waited for; matrix products, arithmetic and copies ran while one was open for 1% of the time, Pallas kernels for 14%

profile of v1, /device:TPU:61, one launch (start us, length us, event | category | flops | bytes accessed | tf_op | source)
XLA Modules:
  0.0 95.2 jit_solution(4680612950345831213)
XLA Ops:
  0.6 0.7 copy.15.owner_ref
  1.4 0.0 copy-start.1
  1.4 1.1 %copy-done.1 = bf16[1,4,64,1280]{3,2,1,0:T(8,128)(2,1)S(1)} copy-done((bf16[1,4,64,1280]{3,2,1,0:T(8,128)(2,1)S(1)}, bf16[1,4,64,1280]{3,2,1,0:T(8,128)(2,1)}, u32[]{:S(2)}) %copy-start.1) | copy-done | bytes 655384
  2.5 0.0 copy-start.5
  2.5 1.5 %copy-done.5 = bf16[768,1280]{1,0:T(8,128)(2,1)S(1)} copy-done((bf16[768,1280]{1,0:T(8,128)(2,1)S(1)}, bf16[768,1280]{1,0:T(8,128)(2,1)}, u32[]{:S(2)}) %copy-start.5) | copy-done | bytes 1966104
  4.0 0.0 copy-start.13
  4.0 0.0 copy-start.12
  4.0 2.6 %attn_part.1 = (bf16[256,256]{1,0:T(8,128)(2,1)S(1)}, bf16[256,256]{1,0:T(8,128)(2,1)S(1)}, bf16[256,256]{1,0:T(8,128)(2,1)S(1)}, bf16[256,256]{1,0:T(8,128)(2,1...) custom-call(s32[4,1]{1,0:T(4,128)S(1)} %copy.15.owner_ref, ...), custom_call_target="tpu_custom_call" | custom-call | flops 600000000 | bytes 3000000 | tf_op jit(solution)/shard_map/attn_part/pallas_call | solution.py:273
  6.6 0.0 copy-start.8
  6.6 0.7 copy-done.8
  7.3 0.7 collective-permute-start.3
  8.0 0.2 collective-permute-start.4
  8.2 2.9 %collective-permute-start.5 = (bf16[256,256]{1,0:T(8,128)(2,1)S(1)}, bf16[256,256]{1,0:T(8,128)(2,1)S(1)}, u32[]{:S(2)}, u32[]{:S(2)}) collective-permute-start(bf16[256,256]{1,0:T(8,128)(2,1)S(1)} %get-tuple-element.24), channel_id=1, source_target_pairs={{0,192},{192,0},{64,128},{128,64},{1,193},{193,1},{65,129},{129,65... | collective-permute-start | bytes 393224 | tf_op jit(solution)/shard_map/ppermute | solution.py:264
  11.1 0.7 reshape.10.lg_ref
  11.8 0.0 copy-done.13
  11.8 0.0 copy-done.12
  11.8 0.0 copy-start.3
  11.9 0.0 copy-start.6
  11.9 0.3 copy.13.feat_ref
  12.2 1.2 %copy-done.3 = bf16[1280,768]{1,0:T(8,128)(2,1)S(1)} copy-done((bf16[1280,768]{1,0:T(8,128)(2,1)S(1)}, bf16[1280,768]{1,0:T(8,128)(2,1)}, u32[]{:S(2)}) %copy-start.3) | copy-done | bytes 1966104
  13.4 0.1 copy-done.6
  13.5 0.0 copy-start.7
  13.5 8.2 %forward_part.1 = (bf16[4,336,1280]{2,1,0:T(8,128)(2,1)S(1)}, bf16[4,336,512]{2,1,0:T(8,128)(2,1)S(1)}, bf16[4,64,256]{2,1,0:T(8,128)(2,1)S(1)}, f32[4,2,64,336]{3,2,1,0:T(8,128)S(1)}) custom-call(bf16[4,257,1280]{2,1,0:T(8,128)(2,1)S(1)} %copy.13.feat_ref, bf16[4,64,1280]{2,1,0:T(8,128)(2,1)S(1)} %copy-done.6, f32[1,1280]{1,0:T(1,128)S(1)} %reshape.11.fg_ref, ...), custom_call_target="tpu_custom_call" | custom-call | flops 4000000000 | bytes 12000000 | tf_op jit(solution)/shard_map/forward_part/pallas_call | solution.py:285
  21.7 0.0 collective-permute-done.3.a1
  21.7 0.0 collective-permute-done.4.a2
  21.7 0.0 collective-permute-done.5.a3
  21.8 0.0 copy-done.7
  21.8 7.1 %backward_part.1 = (bf16[16,240,128]{2,1,0:T(8,128)(2,1)}, bf16[128,768]{1,0:T(8,128)(2,1)S(1)}, bf16[128,768]{1,0:T(8,128)(2,1)S(1)}, bf16[128,768]{1,0:T(8,128)(2,1)S(1)}, bf16[128,768]{1,0:T(8,128)(2,1)S(1)}) custom-call(s32[4,1]{1,0:T(4,128)S(1)} %copy.15.owner_ref, s32[1,4]{1,0:T(1,128)S(1)} %copy-done.7, bf16[256,256]{1,0:T(8,128)(2,1)S(1)} %get-tuple-element.21.a0, ...), custom_call_target="tpu_custom_call" | custom-call | flops 4000000000 | bytes 10000000 | tf_op jit(solution)/shard_map/backward_part/pallas_call | solution.py:298
  28.9 0.0 copy-start.9
  28.9 0.7 copy-done.9
  29.6 0.0 copy-start.10
  29.6 0.7 copy-done.10
  30.3 0.0 copy-start.11
  30.3 0.7 copy-done.11
  31.0 0.0 copy-start.2
  31.0 6.7 %all-to-all-start = ((bf16[16,240,128]{2,1,0:T(8,128)(2,1)}), bf16[16,240,128]{2,1,0:T(8,128)(2,1)S(1)}, u32[]{:S(2)}, u32[]{:S(2)}) async-start(bf16[16,240,128]{2,1,0:T(8,128)(2,1)} %get-tuple-element.33), calls=%async_computation | async-start | bytes 1966080 | tf_op jit(solution)/shard_map/all_to_all | solution.py:306
  37.6 0.8 collective-permute-start
  38.4 0.3 collective-permute-start.1
  38.7 2.9 %collective-permute-start.2 = (bf16[2,64,1280]{2,1,0:T(8,128)(2,1)}, bf16[2,64,1280]{2,1,0:T(8,128)(2,1)S(1)}, u32[]{:S(2)}, u32[]{:S(2)}) collective-permute-start(bf16[2,64,1280]{2,1,0:T(8,128)(2,1)} %copy-done.8), channel_id=1, source_target_pairs={{0,192},{192,0},{64,128},{128,64},{1,193},{193,1},{65,129},{129,65... | collective-permute-start | bytes 983048 | tf_op jit(solution)/shard_map/ppermute | solution.py:264
  41.7 8.2 %all-to-all-done.r_ref = bf16[16,240,128]{2,1,0:T(8,128)(2,1)S(1)} async-done(((bf16[16,240,128]{2,1,0:T(8,128)(2,1)}), bf16[16,240,128]{2,1,0:T(8,128)(2,1)S(1)}, u32[]{:S(2)}, u32[]{:S(2)}) %all-to-all-start) | async-done | bytes 983072 | tf_op jit(solution)/shard_map/all_to_all | solution.py:306
  49.9 1.0 %first_sum.1 = bf16[8,32,384]{2,1,0:T(8,128)(2,1)} custom-call(bf16[16,240,128]{2,1,0:T(8,128)(2,1)S(1)} %all-to-all-done.r_ref), custom_call_target="tpu_custom_call" | custom-call | bytes 1000000 | tf_op jit(solution)/shard_map/first_sum/pallas_call | solution.py:307
  50.9 8.0 %all-to-all-start.1 = ((bf16[8,32,384]{2,1,0:T(8,128)(2,1)}), bf16[8,32,384]{2,1,0:T(8,128)(2,1)S(1)}, u32[]{:S(2)}, u32[]{:S(2)}) async-start(bf16[8,32,384]{2,1,0:T(8,128)(2,1)} %first_sum.1), calls=%async_computation.1 | async-start | bytes 393216 | tf_op jit(solution)/shard_map/all_to_all | solution.py:315
  59.0 15.0 %collective-permute-start.6 = (bf16[128,768]{1,0:T(8,128)(2,1)}, bf16[128,768]{1,0:T(8,128)(2,1)S(1)}, u32[]{:S(2)}, u32[]{:S(2)}) collective-permute-start(bf16[128,768]{1,0:T(8,128)(2,1)} %copy-done.11), channel_id=1, source_target_pairs={{0,64},{64,0},{128,192},{192,128},{1,65},{65,1},{129,193},{193,129... | collective-permute-start | bytes 589832 | tf_op jit(solution)/shard_map/ppermute | solution.py:264
  73.9 0.0 collective-permute-start.7
  73.9 0.0 collective-permute-done.u1
  73.9 3.1 %collective-permute-start.8 = (bf16[128,768]{1,0:T(8,128)(2,1)}, bf16[128,768]{1,0:T(8,128)(2,1)S(1)}, u32[]{:S(2)}, u32[]{:S(2)}) collective-permute-start(bf16[128,768]{1,0:T(8,128)(2,1)} %copy-done.9), channel_id=1, source_target_pairs={{0,192},{192,0},{64,128},{128,64},{1,193},{193,1},{65,129},{129,65... | collective-permute-start | bytes 589832 | tf_op jit(solution)/shard_map/ppermute | solution.py:264
  77.1 0.0 collective-permute-done.1.u2
  77.1 0.0 collective-permute-done.2.u3
  77.1 0.0 collective-permute-done.6.g1
  77.1 5.2 %collective-permute-done.7.g2 = bf16[128,768]{1,0:T(8,128)(2,1)S(1)} collective-permute-done((bf16[128,768]{1,0:T(8,128)(2,1)}, bf16[128,768]{1,0:T(8,128)(2,1)S(1)}, u32[]{:S(2)}, u32[]{:S(2)}) %collective-permute-start.7) | collective-permute-done | bytes 196640 | tf_op jit(solution)/shard_map/ppermute | solution.py:264
  82.2 4.3 %collective-permute-done.8.g3 = bf16[128,768]{1,0:T(8,128)(2,1)S(1)} collective-permute-done((bf16[128,768]{1,0:T(8,128)(2,1)}, bf16[128,768]{1,0:T(8,128)(2,1)S(1)}, u32[]{:S(2)}, u32[]{:S(2)}) %collective-permute-start.8) | collective-permute-done | bytes 196640 | tf_op jit(solution)/shard_map/ppermute | solution.py:264
  86.5 0.0 copy-done.2
  86.5 0.0 copy-start
  86.5 2.1 %copy-done = bf16[1280,1536]{1,0:T(8,128)(2,1)S(1)} copy-done((bf16[1280,1536]{1,0:T(8,128)(2,1)S(1)}, bf16[1280,1536]{1,0:T(8,128)(2,1)}, u32[]{:S(2)}) %copy-start) | copy-done | bytes 3932184
  88.6 0.0 copy-start.4
  88.6 1.5 %copy-done.4 = bf16[1280,768]{1,0:T(8,128)(2,1)S(1)} copy-done((bf16[1280,768]{1,0:T(8,128)(2,1)S(1)}, bf16[1280,768]{1,0:T(8,128)(2,1)}, u32[]{:S(2)}) %copy-start.4) | copy-done | bytes 1966104
  90.2 4.4 %latent_part.1 = bf16[2,64,1280]{2,1,0:T(8,128)(2,1)} custom-call(s32[4,1]{1,0:T(4,128)S(1)} %copy.15.owner_ref, s32[1,4]{1,0:T(1,128)S(1)} %copy-done.7, bf16[4,64,1280]{2,1,0:T(8,128)(2,1)S(1)} %bitcast.3, bf16[4,64,1280]{2,1,0:T(8,128)(2,1)S(1)} %copy-done.6, f32[1,1280]{1,0:T(1,128)S(1)} %reshape.10.lg_ref, bf16[1280,768]{1,0:T(8,128)(2,1)S(1)} %copy-done.4, ...), custom_call_target="tpu_custom_call" | custom-call | flops 1000000000 | bytes 9000000 | tf_op jit(solution)/shard_map/latent_part/pallas_call | solution.py:317
  94.6 0.0 all-to-all-done.1.r_ref
  94.6 0.6 last_sum.1
  (1 shorter events, 0.0 us)
Async XLA Ops:
  1.4 1.1 %copy-start.1 = (bf16[1,4,64,1280]{3,2,1,0:T(8,128)(2,1)S(1)}, bf16[1,4,64,1280]{3,2,1,0:T(8,128)(2,1)}, u32[]{:S(2)}) copy-start(bf16[1,4,64,1280]{3,2,1,0:T(8,128)(2,1)} %param.10) | copy-start | bytes 1966084
  2.5 1.5 %copy-start.5 = (bf16[768,1280]{1,0:T(8,128)(2,1)S(1)}, bf16[768,1280]{1,0:T(8,128)(2,1)}, u32[]{:S(2)}) copy-start(bf16[768,1280]{1,0:T(8,128)(2,1)} %ow_ref.1) | copy-start | bytes 5898244
  4.0 7.8 %copy-start.13 = (f32[1280]{0:T(1024)S(1)}, f32[1280]{0:T(1024)}, u32[]{:S(2)}) copy-start(f32[1280]{0:T(1024)} %param.13) | copy-start | bytes 15364
  4.0 7.8 %copy-start.12 = (bf16[4,257,1280]{2,0,1:T(4,128)(2,1)S(1)}, bf16[4,257,1280]{2,0,1:T(4,128)(2,1)}, u32[]{:S(2)}) copy-start(bf16[4,257,1280]{2,0,1:T(4,128)(2,1)} %param.12) | copy-start | bytes 7895044
  6.6 0.7 copy-start.8
  7.3 14.4 %collective-permute-start.3 = (bf16[256,256]{1,0:T(8,128)(2,1)S(1)}, bf16[256,256]{1,0:T(8,128)(2,1)S(1)}, u32[]{:S(2)}, u32[]{:S(2)}) collective-permute-start(bf16[256,256]{1,0:T(8,128)(2,1)S(1)} %get-tuple-element.22), channel_id=1, source_target_pairs={{0,64},{64,0},{128,192},{192,128},{1,65},{65,1},{129,193},{193,129... | collective-permute-start | bytes 393224 | tf_op jit(solution)/shard_map/ppermute | solution.py:264
  8.0 13.8 %collective-permute-start.4 = (bf16[256,256]{1,0:T(8,128)(2,1)S(1)}, bf16[256,256]{1,0:T(8,128)(2,1)S(1)}, u32[]{:S(2)}, u32[]{:S(2)}) collective-permute-start(bf16[256,256]{1,0:T(8,128)(2,1)S(1)} %get-tuple-element.23), channel_id=1, source_target_pairs={{0,128},{128,0},{64,192},{192,64},{1,129},{129,1},{65,193},{193,65... | collective-permute-start | bytes 393224 | tf_op jit(solution)/shard_map/ppermute | solution.py:264
  8.2 13.5 %collective-permute-start.5 = (bf16[256,256]{1,0:T(8,128)(2,1)S(1)}, bf16[256,256]{1,0:T(8,128)(2,1)S(1)}, u32[]{:S(2)}, u32[]{:S(2)}) collective-permute-start(bf16[256,256]{1,0:T(8,128)(2,1)S(1)} %get-tuple-element.24), channel_id=1, source_target_pairs={{0,192},{192,0},{64,128},{128,64},{1,193},{193,1},{65,129},{129,65... | collective-permute-start | bytes 393224 | tf_op jit(solution)/shard_map/ppermute | solution.py:264
  11.8 1.5 %copy-start.3 = (bf16[1280,768]{1,0:T(8,128)(2,1)S(1)}, bf16[1280,768]{1,0:T(8,128)(2,1)}, u32[]{:S(2)}) copy-start(bf16[1280,768]{1,0:T(8,128)(2,1)} %qw_ref.1) | copy-start | bytes 5898244
  11.9 1.7 %copy-start.6 = (bf16[4,64,1280]{2,1,0:T(8,128)(2,1)S(1)}, bf16[4,64,1280]{2,1,0:T(8,128)(2,1)}, u32[]{:S(2)}) copy-start(bf16[4,64,1280]{2,1,0:T(8,128)(2,1)} %lat_ref.3) | copy-start | bytes 1966084
  13.5 8.2 %copy-start.7 = (s32[1,4]{1,0:T(1,128)S(1)}, s32[1,4]{1,0:T(1,128)}, u32[]{:S(2)}) copy-start(s32[1,4]{1,0:T(1,128)} %sample_ref.3) | copy-start | bytes 52
  28.9 0.7 copy-start.9
  29.6 0.7 copy-start.10
  30.3 0.7 copy-start.11
  31.0 55.6 %copy-start.2 = (bf16[1,4,64,1280]{3,2,1,0:T(8,128)(2,1)S(1)}, bf16[1,4,64,1280]{3,2,1,0:T(8,128)(2,1)}, u32[]{:S(2)}) copy-start(bf16[1,4,64,1280]{3,2,1,0:T(8,128)(2,1)} %param.10) | copy-start | bytes 1966084
  31.0 19.0 %all-to-all-start = ((bf16[16,240,128]{2,1,0:T(8,128)(2,1)}), bf16[16,240,128]{2,1,0:T(8,128)(2,1)S(1)}, u32[]{:S(2)}, u32[]{:S(2)}) async-start(bf16[16,240,128]{2,1,0:T(8,128)(2,1)} %get-tuple-element.33), calls=%async_computation | async-start | bytes 1966080 | tf_op jit(solution)/shard_map/all_to_all | solution.py:306
  37.6 36.3 %collective-permute-start = (bf16[2,64,1280]{2,1,0:T(8,128)(2,1)}, bf16[2,64,1280]{2,1,0:T(8,128)(2,1)S(1)}, u32[]{:S(2)}, u32[]{:S(2)}) collective-permute-start(bf16[2,64,1280]{2,1,0:T(8,128)(2,1)} %get-tuple-element.18), channel_id=1, source_target_pairs={{0,64},{64,0},{128,192},{192,128},{1,65},{65,1},{129,193},{193,129... | collective-permute-start | bytes 983048 | tf_op jit(solution)/shard_map/ppermute | solution.py:264
  38.4 38.6 %collective-permute-start.1 = (bf16[2,64,1280]{2,1,0:T(8,128)(2,1)}, bf16[2,64,1280]{2,1,0:T(8,128)(2,1)S(1)}, u32[]{:S(2)}, u32[]{:S(2)}) collective-permute-start(bf16[2,64,1280]{2,1,0:T(8,128)(2,1)} %get-tuple-element.19), channel_id=1, source_target_pairs={{0,128},{128,0},{64,192},{192,64},{1,129},{129,1},{65,193},{193,65... | collective-permute-start | bytes 983048 | tf_op jit(solution)/shard_map/ppermute | solution.py:264
  38.7 38.3 %collective-permute-start.2 = (bf16[2,64,1280]{2,1,0:T(8,128)(2,1)}, bf16[2,64,1280]{2,1,0:T(8,128)(2,1)S(1)}, u32[]{:S(2)}, u32[]{:S(2)}) collective-permute-start(bf16[2,64,1280]{2,1,0:T(8,128)(2,1)} %copy-done.8), channel_id=1, source_target_pairs={{0,192},{192,0},{64,128},{128,64},{1,193},{193,1},{65,129},{129,65... | collective-permute-start | bytes 983048 | tf_op jit(solution)/shard_map/ppermute | solution.py:264
  50.9 43.6 %all-to-all-start.1 = ((bf16[8,32,384]{2,1,0:T(8,128)(2,1)}), bf16[8,32,384]{2,1,0:T(8,128)(2,1)S(1)}, u32[]{:S(2)}, u32[]{:S(2)}) async-start(bf16[8,32,384]{2,1,0:T(8,128)(2,1)} %first_sum.1), calls=%async_computation.1 | async-start | bytes 393216 | tf_op jit(solution)/shard_map/all_to_all | solution.py:315
  59.0 18.1 %collective-permute-start.6 = (bf16[128,768]{1,0:T(8,128)(2,1)}, bf16[128,768]{1,0:T(8,128)(2,1)S(1)}, u32[]{:S(2)}, u32[]{:S(2)}) collective-permute-start(bf16[128,768]{1,0:T(8,128)(2,1)} %copy-done.11), channel_id=1, source_target_pairs={{0,64},{64,0},{128,192},{192,128},{1,65},{65,1},{129,193},{193,129... | collective-permute-start | bytes 589832 | tf_op jit(solution)/shard_map/ppermute | solution.py:264
  73.9 8.3 %collective-permute-start.7 = (bf16[128,768]{1,0:T(8,128)(2,1)}, bf16[128,768]{1,0:T(8,128)(2,1)S(1)}, u32[]{:S(2)}, u32[]{:S(2)}) collective-permute-start(bf16[128,768]{1,0:T(8,128)(2,1)} %copy-done.10), channel_id=1, source_target_pairs={{0,128},{128,0},{64,192},{192,64},{1,129},{129,1},{65,193},{193,65... | collective-permute-start | bytes 589832 | tf_op jit(solution)/shard_map/ppermute | solution.py:264
  73.9 12.6 %collective-permute-start.8 = (bf16[128,768]{1,0:T(8,128)(2,1)}, bf16[128,768]{1,0:T(8,128)(2,1)S(1)}, u32[]{:S(2)}, u32[]{:S(2)}) collective-permute-start(bf16[128,768]{1,0:T(8,128)(2,1)} %copy-done.9), channel_id=1, source_target_pairs={{0,192},{192,0},{64,128},{128,64},{1,193},{193,1},{65,129},{129,65... | collective-permute-start | bytes 589832 | tf_op jit(solution)/shard_map/ppermute | solution.py:264
  86.5 2.1 %copy-start = (bf16[1280,1536]{1,0:T(8,128)(2,1)S(1)}, bf16[1280,1536]{1,0:T(8,128)(2,1)}, u32[]{:S(2)}) copy-start(bf16[1280,1536]{1,0:T(8,128)(2,1)} %kvw_ref.1) | copy-start | bytes 11796484
  88.6 1.5 %copy-start.4 = (bf16[1280,768]{1,0:T(8,128)(2,1)S(1)}, bf16[1280,768]{1,0:T(8,128)(2,1)}, u32[]{:S(2)}) copy-start(bf16[1280,768]{1,0:T(8,128)(2,1)} %qw_ref.1) | copy-start | bytes 5898244

commit v2 on v1

v2 whole, which is shorter than its diff:
```python
import functools
import jax
import jax.numpy as jnp
from jax import lax
from jax.experimental import pallas as pl
from jax.experimental.pallas import tpu as pltpu
from jax.sharding import Mesh, PartitionSpec as P

HEAD = 96
IMGS = 4
LAT = 64
PATCH = 257
TOK = 321
ROWS = 336
D = 1280
INNER = 768
EPS = 1e-05
BF = jnp.bfloat16
F32 = jnp.float32
FACTOR = HEAD ** (-0.5)
SHARE = 20


def dot(a, b, ca, cb):
    return lax.dot_general(a, b, (((ca,), (cb,)), ((), ())), preferred_element_type=F32)


def pair_of(xh, co):
    return co * 2 + xh


def window_of(pair):
    return (pair // 2) * 384 + (pair % 2) * 128


def head_lanes(pair, head, rows):
    lane = lax.broadcasted_iota(jnp.int32, (rows, 256), 1) - ((pair % 2) * 64 + head * HEAD)
    return (lane >= 0) & (lane < HEAD)


def by_head(x, pair):
    zero = jnp.zeros_like(x)
    return jnp.concatenate([jnp.where(head_lanes(pair, h, x.shape[0]), x, zero) for h in range(2)], axis=0)


def layer_stats(x):
    centred = x - jnp.mean(x, axis=-1, keepdims=True)
    inverse = lax.rsqrt(jnp.mean(centred * centred, axis=-1, keepdims=True) + EPS)
    return centred * inverse, inverse


def slot_image(owner_ref, section, slot):
    found = jnp.int32(0)
    index = jnp.int32(0)
    seen = jnp.int32(0)
    for i in range(IMGS):
        mine = (owner_ref[0, i] == section).astype(jnp.int32)
        take = (mine == 1) & (seen == slot)
        index = jnp.where(take, i, index)
        found = jnp.where(take, 1, found)
        seen = seen + mine
    return index, found


def scale_of(sample_ref, i):
    count = jnp.int32(0)
    for k in range(IMGS):
        count = count + (sample_ref[0, k] == sample_ref[0, i]).astype(jnp.int32)
    return count


AROUND = ((0, 0), (0, 1), (1, 0), (1, 1))


def attn_kernel(part_hbm, ow_hbm, a0, a1, a2, a3, part, wt, prod, sems):
    xh = lax.axis_index("xh")
    co = lax.axis_index("co")
    copies = [pltpu.make_async_copy(part_hbm, part, sems.at[0])]
    for k in range(4):
        rows = pl.ds(192 * k, 192)
        copies.append(pltpu.make_async_copy(ow_hbm.at[rows], wt.at[rows], sems.at[k + 1]))
    for c in copies:
        c.start()
    for c in copies:
        c.wait()
    prod[...] = dot(part[...].reshape(IMGS * LAT, D), wt[...], 1, 1).astype(BF)
    for out, (dx, dc) in zip((a0, a1, a2, a3), AROUND):
        start = pl.multiple_of(window_of(pair_of(xh ^ dx, co ^ dc)), 128)
        out[...] = prod[:, pl.ds(start, 256)]


def chip_sum_kernel(owner_ref, part_ref, c1_ref, u_ref):
    section = (lax.axis_index("xh") ^ 1) * 2 + lax.axis_index("co")
    for slot in range(2):
        index, _ = slot_image(owner_ref, section, slot)
        u_ref[slot] = (part_ref[index].astype(F32) + c1_ref[index].astype(F32)).astype(BF)


def forward_kernel(feat_ref, lat_ref, fg_ref, lg_ref, qw_hbm, kvw_hbm, ctx_ref, kv_ref, q_ref, pr_ref, win, sems):
    pair = pair_of(lax.axis_index("xh"), lax.axis_index("co"))
    start = pl.multiple_of(window_of(pair), 128)
    copies = [
        pltpu.make_async_copy(qw_hbm.at[:, pl.ds(start, 256)], win.at[0], sems.at[0]),
        pltpu.make_async_copy(kvw_hbm.at[:, pl.ds(start, 256)], win.at[1], sems.at[1]),
        pltpu.make_async_copy(kvw_hbm.at[:, pl.ds(pl.multiple_of(start + INNER, 128), 256)], win.at[2], sems.at[2]),
    ]
    for c in copies:
        c.start()
    fg = fg_ref[...].reshape(1, D)
    lg = lg_ref[...].reshape(1, D)
    live = lax.broadcasted_iota(jnp.int32, (2 * LAT, ROWS), 1) < TOK

    def norm(i):
        for c in range(4):
            hat, _ = layer_stats(feat_ref[i, 64 * c:64 * (c + 1)].astype(F32))
            ctx_ref[i, LAT + 64 * c:LAT + 64 * (c + 1)] = (hat * fg).astype(BF)
        hat, _ = layer_stats(lat_ref[i].astype(F32))
        ctx_ref[i, :LAT] = (hat * lg).astype(BF)
        hat, _ = layer_stats(feat_ref[i, 256:257].astype(F32))
        first = lax.broadcasted_iota(jnp.int32, (16, D), 0) == 0
        ctx_ref[i, 320:ROWS] = jnp.where(first, hat * fg, 0.0).astype(BF)

    def project(i):
        kv_ref[i, :, :256] = dot(ctx_ref[i], win[1], 1, 0).astype(BF)
        kv_ref[i, :, 256:] = dot(ctx_ref[i], win[2], 1, 0).astype(BF)
        q_ref[i] = by_head(dot(ctx_ref[i, :LAT], win[0], 1, 0), pair).astype(BF)

    def attend(i):
        scores = dot(q_ref[i], kv_ref[i, :, :256], 1, 1) * FACTOR
        scores = jnp.where(live, scores, -1e30)
        shifted = jnp.exp(scores - jnp.max(scores, axis=-1, keepdims=True))
        shifted = jnp.where(live, shifted, 0.0)
        pr_ref[i] = shifted / jnp.sum(shifted, axis=-1, keepdims=True)

    norm(0)
    for c in copies:
        c.wait()
    for i in range(IMGS):
        if i < IMGS - 1:
            norm(i + 1)
        project(i)
        if i > 0:
            attend(i - 1)
    attend(IMGS - 1)


def backward_kernel(owner_ref, sample_ref, a0, a1, a2, a3, kv_ref, q_ref, pr_ref,
                    kvg, g0, g1, g2, g3, lat):
    xh = lax.axis_index("xh")
    co = lax.axis_index("co")
    pair = pair_of(xh, co)
    left = lax.broadcasted_iota(jnp.int32, (ROWS, 128), 1) < 64
    for i in range(IMGS):
        rows = slice(LAT * i, LAT * (i + 1))
        count = scale_of(sample_ref, i).astype(F32)
        total = (a0[rows].astype(F32) + a1[rows].astype(F32)) + (a2[rows].astype(F32) + a3[rows].astype(F32))
        attn = by_head(total / count, pair).astype(BF)
        probs = pr_ref[i]
        value_grad = dot(probs.astype(BF), attn, 0, 0)
        prob_grad = dot(attn, kv_ref[i, :, 256:], 1, 1)
        inner = jnp.sum(probs * prob_grad, axis=-1, keepdims=True)
        score_grad = (probs * (prob_grad - inner) * FACTOR).astype(BF)
        query_grad = dot(score_grad, kv_ref[i, :, :256], 1, 0)
        query_grad = jnp.where(head_lanes(pair, 0, LAT), query_grad[:LAT],
                               jnp.where(head_lanes(pair, 1, LAT), query_grad[LAT:], 0.0))
        key_grad = dot(score_grad, q_ref[i], 0, 0)
        lat[rows, :256] = query_grad.astype(BF)
        lat[rows, 256:512] = key_grad[:LAT].astype(BF)
        lat[rows, 512:] = value_grad[:LAT].astype(BF)
        at = slice(ROWS * i, ROWS * (i + 1))
        kvg[at, :128] = jnp.where(xh == 0, key_grad[:, :128], key_grad[:, 128:]).astype(BF)
        kvg[at, 128:256] = jnp.where(xh == 0, value_grad[:, :128], value_grad[:, 128:]).astype(BF)
        even = jnp.where(left, key_grad[:, 128:], pltpu.roll(value_grad[:, 128:], 64, 1))
        odd = jnp.where(left, pltpu.roll(key_grad[:, :128], 64, 1), value_grad[:, :128])
        kvg[at, 256:] = jnp.where(xh == 0, even, odd).astype(BF)
    for out, (dx, dc) in zip((g0, g1, g2, g3), AROUND):
        section = (xh ^ dx) * 2 + (co ^ dc)
        for slot in range(2):
            index, _ = slot_image(owner_ref, section, slot)
            out[LAT * slot:LAT * (slot + 1)] = lat[pl.ds(pl.multiple_of(index * LAT, LAT), LAT)]


def weight_kernel(ctx_ref, kvg, w_ref, wide, order):
    ctx = ctx_ref[...].reshape(IMGS * ROWS, D)
    for c in range(5):
        wide[256 * c:256 * (c + 1)] = dot(ctx[:, 256 * c:256 * (c + 1)], kvg[...], 0, 0)
    for y in range(4):
        for xl in range(2):
            piece = xl * 4 + y
            for z in range(8):
                first = ((z * 4 + y) * 2 + xl) * SHARE
                order[piece, z * SHARE:(z + 1) * SHARE] = wide[first:first + SHARE]
            whole = order[piece]
            keys = whole[:, :128], whole[:, 256:320]
            vals = whole[:, 128:256], whole[:, 320:]
            for k, (main, tail) in enumerate((keys, vals)):
                w_ref[8 * k + piece, 0:160] = main.astype(BF)
                w_ref[8 * k + piece, 160:240] = jnp.concatenate([tail[:80], tail[80:]], axis=1).astype(BF)


def first_sum_kernel(r_ref, out_ref, full):
    tails = []
    for k in range(2):
        total = r_ref[8 * k].astype(F32)
        for p in range(1, 8):
            total = total + r_ref[8 * k + p].astype(F32)
        full[:, 256 * k:256 * k + 128] = total[:160]
        tail = total[160:]
        tails.append(jnp.concatenate([tail[:, :64], tail[:, 64:]], axis=0))
    full[:, 128:256] = jnp.concatenate(tails, axis=1)
    for z in range(8):
        out_ref[z, 0:SHARE] = full[SHARE * z:SHARE * (z + 1)].astype(BF)


def last_kernel(r_ref, out_ref):
    total = r_ref[0].astype(F32)
    for z in range(1, 8):
        total = total + r_ref[z].astype(F32)
    out_ref[...] = total[:SHARE] * (1.0 / 256.0)


def latent_kernel(owner_ref, sample_ref, part_ref, lat_ref, lg_ref, qw_hbm, kvw_hbm,
                  c1, u2, g0, g1, g2, g3, out_ref, win, sems):
    xh = lax.axis_index("xh")
    co = lax.axis_index("co")
    section = xh * 2 + co
    copies = []
    for dx, dc in AROUND:
        start = pl.multiple_of(window_of(pair_of(xh ^ dx, co ^ dc)), 128)
        further = pl.multiple_of(start + INNER, 128)
        for k, (source, lane) in enumerate(((qw_hbm, start), (kvw_hbm, start), (kvw_hbm, further))):
            n = len(copies)
            copies.append(pltpu.make_async_copy(source.at[:, pl.ds(lane, 256)], win.at[n], sems.at[n]))
    for c in copies:
        c.start()
    grad = jnp.zeros((2 * LAT, D), F32)
    for n, c in enumerate(copies):
        c.wait()
        k = n % 3
        grad = grad + dot((g0, g1, g2, g3)[n // 3][:, 256 * k:256 * (k + 1)], win[n], 1, 1)
    lg = lg_ref[...].reshape(1, D)
    for slot in range(2):
        index, found = slot_image(owner_ref, section, slot)
        count = scale_of(sample_ref, index).astype(F32)
        summed = (part_ref[index].astype(F32) + c1[index].astype(F32)) + u2[slot].astype(F32)
        upstream = (summed / count).astype(BF).astype(F32)
        hat, inverse = layer_stats(lat_ref[index].astype(F32))
        dy = grad[LAT * slot:LAT * (slot + 1)] * lg
        centred = dy - jnp.mean(dy, axis=-1, keepdims=True) - hat * jnp.mean(dy * hat, axis=-1, keepdims=True)
        out = (upstream + inverse * centred).astype(BF)
        out_ref[slot] = jnp.where(found == 1, out, jnp.zeros_like(out))


SMEM = pl.BlockSpec(memory_space=pltpu.SMEM)
VMEM = pl.BlockSpec(memory_space=pltpu.VMEM)
HBM = pl.BlockSpec(memory_space=pltpu.HBM)
CORE = [(0, 1), (1, 0), (2, 3), (3, 2)]
FAR = [(0, 2), (2, 0), (1, 3), (3, 1)]
DIAGONAL = [(0, 3), (3, 0), (1, 2), (2, 1)]
SECTION = ("xh", "co")


def call(body, name, outs, ins, scratch=(), flops=0, size=0, limit=24):
    return pl.pallas_call(
        body,
        out_shape=outs,
        in_specs=ins,
        out_specs=jax.tree.map(lambda _: VMEM, outs),
        scratch_shapes=list(scratch),
        cost_estimate=pl.CostEstimate(flops=flops, bytes_accessed=size, transcendentals=0),
        compiler_params=pltpu.CompilerParams(vmem_limit_bytes=limit * 2**20),
        name=name,
    )


def swap(x, pairs):
    return lax.ppermute(x, SECTION, pairs)


def bf(*shape):
    return jax.ShapeDtypeStruct(shape, BF)


DMA = pltpu.SemaphoreType.DMA
CALLS = dict(
    attn=call(
        attn_kernel, "attn_part", [bf(256, 256)] * 4, [HBM] * 2,
        [pltpu.VMEM((IMGS, LAT, D), BF), pltpu.VMEM((INNER, D), BF), pltpu.VMEM((256, INNER), BF), DMA((5,))],
        flops=600_000_000, size=3_000_000, limit=60),
    chip=call(chip_sum_kernel, "chip_sum", bf(2, LAT, D), [SMEM] + [VMEM] * 2, size=1_500_000),
    forward=call(
        forward_kernel, "forward_part",
        [bf(IMGS, ROWS, D), bf(IMGS, ROWS, 512), bf(IMGS, 2 * LAT, 256),
         jax.ShapeDtypeStruct((IMGS, 2 * LAT, ROWS), F32)],
        [VMEM] * 4 + [HBM] * 2,
        [pltpu.VMEM((3, D, 256), BF), DMA((3,))],
        flops=4_000_000_000, size=12_000_000),
    backward=call(
        backward_kernel, "backward_part", [bf(IMGS * ROWS, 384)] + [bf(2 * LAT, 768)] * 4,
        [SMEM, SMEM] + [VMEM] * 7, [pltpu.VMEM((256, 768), BF)],
        flops=2_000_000_000, size=5_000_000),
    weight=call(
        weight_kernel, "weight_part", bf(16, 240, 128), [VMEM] * 2,
        [pltpu.VMEM((D, 384), F32), pltpu.VMEM((8, 160, 384), F32)],
        flops=3_000_000_000, size=6_000_000),
    first=call(first_sum_kernel, "first_sum", bf(8, 32, 384), [VMEM], [pltpu.VMEM((160, 384), F32)],
               size=1_000_000),
    last=call(last_kernel, "last_sum", jax.ShapeDtypeStruct((SHARE, 384), F32), [VMEM], size=300_000),
    latent=call(
        latent_kernel, "latent_part", bf(2, LAT, D), [SMEM, SMEM] + [VMEM] * 3 + [HBM] * 2 + [VMEM] * 6,
        [pltpu.VMEM((12, D, 256), BF), DMA((12,))],
        flops=2_000_000_000, size=9_000_000, limit=60),
)


def per_device(partials, latents, features, feature_gain, latent_gain, query_weight, kv_weight, out_weight,
               sample_of, owner):
    part = partials[0]
    owner = owner.reshape(1, IMGS)
    c1 = swap(part, CORE)
    a0, a1, a2, a3 = CALLS["attn"](part, out_weight)
    a3 = swap(a3, DIAGONAL)
    a2 = swap(a2, FAR)
    a1 = swap(a1, CORE)
    u = swap(CALLS["chip"](owner, part, c1), FAR)
    ctx, kv, q, probs = CALLS["forward"](
        features, latents, feature_gain, latent_gain, query_weight, kv_weight)
    kvg, g0, g1, g2, g3 = CALLS["backward"](owner, sample_of, a0, a1, a2, a3, kv, q, probs)
    kvg, u = lax.optimization_barrier((kvg, u))
    g3 = swap(g3, DIAGONAL)
    g2 = swap(g2, FAR)
    g1 = swap(g1, CORE)
    w = CALLS["weight"](ctx, kvg)
    w, g1, g2, g3 = lax.optimization_barrier((w, g1, g2, g3))
    w = lax.all_to_all(w, ("xh", "xl", "y"), 0, 0, tiled=True)
    w = CALLS["first"](w)
    latent_grad = CALLS["latent"](
        owner, sample_of, part, latents, latent_gain, query_weight, kv_weight, c1, u, g0, g1, g2, g3)
    w, latent_grad = lax.optimization_barrier((w, latent_grad))
    w = lax.all_to_all(w, "z", 0, 0, tiled=True)
    kv_grad = CALLS["last"](w)
    return latent_grad[None], kv_grad


def solution(mesh):
    fine = Mesh(mesh.devices.reshape(2, 2, 8, 4, 2), ("xh", "co", "z", "y", "xl"))
    dp = ("z", "y", "xl")
    return jax.shard_map(
        per_device,
        mesh=fine,
        in_specs=(
            P(SECTION, dp, None, None),
            P(dp, None, None),
            P(dp, None, None),
            P(),
            P(),
            P(),
            P(),
            P(),
            P(dp, None),
            P(dp, None),
        ),
        out_specs=(P(SECTION, dp, None, None), P(dp, SECTION)),
        check_vma=False,
    )
```

time: 95.7 us -> 74.8 us (0.78)
  the two profiles are of different devices: /device:TPU:61 before, /device:TPU:8 now
where the time goes in v2:
time: 74.8 us; the launch traced here: 74.6 us
  Pallas kernels  22.8 us (30%)
  blocking collectives  18.1 us (24%)
  starting transfers between devices  16.2 us (22%)
  waiting for transfers between devices  13.7 us (18%)
  local copies, waits for them, and re-layouts  2.97 us (4%)
  between operations  0.86 us (1%)
    all_to_all x1, blocking collectives, per_device(): w = lax.all_to_all(w, 'z', 0, 0, tiled=True)  18.1 us
    ppermute x8, starting transfers between devices, swap(): return lax.ppermute(x, SECTION, pairs)  10 us
    all_to_all x1, waiting for transfers between devices, per_device(): w = lax.all_to_all(w, ('xh', 'xl', 'y'), 0, 0, tiled=True)  8.23 us
    pallas_call x1, Pallas kernels, per_device(): CALLS['latent']  8 us
    all_to_all x1, starting transfers between devices, per_device(): w = lax.all_to_all(w, ('xh', 'xl', 'y'), 0, 0, tiled=True)  6.22 us
    ppermute x8, waiting for transfers between devices, swap(): return lax.ppermute(x, SECTION, pairs)  5.43 us
    pallas_call x1, Pallas kernels, per_device(): CALLS['forward']  4.22 us
    pallas_call x1, Pallas kernels, per_device(): w = CALLS['weight'](ctx, kvg)  3.38 us
  transfers between devices with their start and end apart: 9, of which 3 were waited for; matrix products, arithmetic and copies ran while one was open for 3% of the time, Pallas kernels for 29%

profile of v2, /device:TPU:8, one launch (start us, length us, event | category | flops | bytes accessed | tf_op | source)
XLA Modules:
  0.0 74.6 jit_solution(13821953155002298126)
XLA Ops:
  0.6 0.1 collective-permute-start.3
  0.7 0.0 copy-start.4
  0.7 3.3 %attn_part.1 = (bf16[256,256]{1,0:T(8,128)(2,1)}, bf16[256,256]{1,0:T(8,128)(2,1)}, bf16[256,256]{1,0:T(8,128)(2,1)}, bf16[256,256]{1,0:T(8,128)(2,1)}) custom-call(bf16[4,64,1280]{2,1,0:T(8,128)(2,1)} %bitcast.4, bf16[768,1280]{1,0:T(8,128)(2,1)} %ow_hbm.1), custom_call_target="tpu_custom_call" | custom-call | flops 600000000 | bytes 3000000 | tf_op jit(solution)/shard_map/attn_part/pallas_call | solution.py:321
  4.0 0.6 collective-permute-start
  4.6 3.0 %collective-permute-start.1 = (bf16[256,256]{1,0:T(8,128)(2,1)}, bf16[256,256]{1,0:T(8,128)(2,1)S(1)}, u32[]{:S(2)}, u32[]{:S(2)}) collective-permute-start(bf16[256,256]{1,0:T(8,128)(2,1)} %get-tuple-element.26), channel_id=1, source_target_pairs={{0,128},{128,0},{64,192},{192,64},{1,129},{129,1},{65,193},{193,65... | collective-permute-start | bytes 393224 | tf_op jit(solution)/shard_map/ppermute | solution.py:277
  7.6 0.0 copy-start.7
  7.6 0.0 copy-start
  7.6 0.0 copy-start.1
  7.6 0.0 copy-start.3
  7.6 0.0 copy-start.6
  7.6 0.0 copy-start.10
  7.7 0.1 collective-permute-start.2
  7.8 2.2 %copy.12.feat_ref = bf16[4,257,1280]{2,1,0:T(8,128)(2,1)S(1)} copy(bf16[4,257,1280]{2,0,1:T(4,128)(2,1)} %param.12) | data formatting | bytes 5263360 | tf_op args[2]
  10.0 0.0 collective-permute-done.3.c1_ref.c1
  10.0 0.0 copy-start.2
  10.0 0.0 copy-done.7
  10.0 0.0 copy-done
  10.0 0.6 chip_sum.1
  10.7 0.0 copy-start.8
  10.7 0.0 copy-start.9
  10.7 2.9 %collective-permute-start.4 = (bf16[2,64,1280]{2,1,0:T(8,128)(2,1)S(1)}, bf16[2,64,1280]{2,1,0:T(8,128)(2,1)S(1)}, u32[]{:S(2)}, u32[]{:S(2)}) collective-permute-start(bf16[2,64,1280]{2,1,0:T(8,128)(2,1)S(1)} %chip_sum.1), channel_id=1, source_target_pairs={{0,128},{128,0},{64,192},{192,64},{1,129},{129,1},{65,193},{193,65... | collective-permute-start | bytes 983048 | tf_op jit(solution)/shard_map/ppermute | solution.py:277
  13.6 0.0 copy-done.4
  13.6 0.0 copy-done.1
  13.6 0.0 copy-done.3
  13.6 0.0 copy-done.6
  13.6 0.0 copy-done.10
  13.6 4.2 %forward_part.1 = (bf16[4,336,1280]{2,1,0:T(8,128)(2,1)S(1)}, bf16[4,336,512]{2,1,0:T(8,128)(2,1)S(1)}, bf16[4,128,256]{2,1,0:T(8,128)(2,1)S(1)}, f32[4,128,336]{2,1,0:T(8,128)S(1)}) custom-call(bf16[4,257,1280]{2,1,0:T(8,128)(2,1)S(1)} %copy.12.feat_ref, bf16[4,64,1280]{2,1,0:T(8,128)(2,1)S(1)} %copy-done.4, f32[1280]{0:T(1024)S(1)} %copy-done.10, ...), custom_call_target="tpu_custom_call" | custom-call | flops 4000000000 | bytes 12000000 | tf_op jit(solution)/shard_map/forward_part/pallas_call | solution.py:326
  17.8 0.0 copy-done.2
  17.8 0.0 collective-permute-done.a1
  17.8 0.0 collective-permute-done.1.a2
  17.9 0.0 collective-permute-done.2.a3
  17.9 0.0 copy-done.8
  17.9 0.0 copy-done.9
  17.9 2.4 %backward_part.1 = (bf16[1344,384]{1,0:T(8,128)(2,1)S(1)}, bf16[128,768]{1,0:T(8,128)(2,1)S(1)}, bf16[128,768]{1,0:T(8,128)(2,1)S(1)}, bf16[128,768]{1,0:T(8,128)(2,1)S(1)}, bf16[128,768]{1,0:T(8,128)(2,1)S(1)}) custom-call(s32[1,4]{1,0:T(1,128)S(1)} %bitcast.9, s32[1,4]{1,0:T(1,128)S(1)} %copy-done.8, bf16[256,256]{1,0:T(8,128)(2,1)S(1)} %copy-done.9, ...), custom_call_target="tpu_custom_call" | custom-call | flops 2000000000 | bytes 5000000 | tf_op jit(solution)/shard_map/backward_part/pallas_call | solution.py:328
  20.3 0.0 copy-start.5
  20.4 0.7 copy-done.5
  21.0 0.4 collective-permute-start.5
  21.4 1.0 %collective-permute-start.6 = (bf16[128,768]{1,0:T(8,128)(2,1)S(1)}, bf16[128,768]{1,0:T(8,128)(2,1)S(1)}, u32[]{:S(2)}, u32[]{:S(2)}) collective-permute-start(bf16[128,768]{1,0:T(8,128)(2,1)S(1)} %get-tuple-element.34), channel_id=1, source_target_pairs={{0,128},{128,0},{64,192},{192,64},{1,129},{129,1},{65,193},{193,65... | collective-permute-start | bytes 589832 | tf_op jit(solution)/shard_map/ppermute | solution.py:277
  22.4 2.0 %collective-permute-start.7 = (bf16[128,768]{1,0:T(8,128)(2,1)S(1)}, bf16[128,768]{1,0:T(8,128)(2,1)S(1)}, u32[]{:S(2)}, u32[]{:S(2)}) collective-permute-start(bf16[128,768]{1,0:T(8,128)(2,1)S(1)} %get-tuple-element.35), channel_id=1, source_target_pairs={{0,192},{192,0},{64,128},{128,64},{1,193},{193,1},{65,129},{129,65... | collective-permute-start | bytes 589832 | tf_op jit(solution)/shard_map/ppermute | solution.py:277
  24.4 0.0 collective-permute-done.4.u2
  24.4 0.0 copy-start.11
  24.4 3.4 %weight_part.1 = bf16[16,240,128]{2,1,0:T(8,128)(2,1)} custom-call(bf16[4,336,1280]{2,1,0:T(8,128)(2,1)S(1)} %get-tuple-element.23.ctx_ref, bf16[1344,384]{1,0:T(8,128)(2,1)S(1)} %get-tuple-element.32.kvg), custom_call_target="tpu_custom_call" | custom-call | flops 3000000000 | bytes 6000000 | tf_op jit(solution)/shard_map/weight_part/pallas_call | solution.py:333
  27.8 0.0 copy-done.11
  27.8 0.0 collective-permute-done.5.g1
  27.8 0.0 copy-start.12
  27.8 2.9 %collective-permute-done.6.g2 = bf16[128,768]{1,0:T(8,128)(2,1)S(1)} collective-permute-done((bf16[128,768]{1,0:T(8,128)(2,1)S(1)}, bf16[128,768]{1,0:T(8,128)(2,1)S(1)}, u32[]{:S(2)}, u32[]{:S(2)}) %collective-permute-start.6) | collective-permute-done | bytes 196640 | tf_op jit(solution)/shard_map/ppermute | solution.py:277
  30.7 0.0 copy-start.13
  30.7 2.5 %collective-permute-done.7.g3 = bf16[128,768]{1,0:T(8,128)(2,1)S(1)} collective-permute-done((bf16[128,768]{1,0:T(8,128)(2,1)S(1)}, bf16[128,768]{1,0:T(8,128)(2,1)S(1)}, u32[]{:S(2)}, u32[]{:S(2)}) %collective-permute-start.7) | collective-permute-done | bytes 196640 | tf_op jit(solution)/shard_map/ppermute | solution.py:277
  33.2 0.0 copy-start.14
  33.2 6.2 %all-to-all-start = ((bf16[16,240,128]{2,1,0:T(8,128)(2,1)}), bf16[16,240,128]{2,1,0:T(8,128)(2,1)S(1)}, u32[]{:S(2)}, u32[]{:S(2)}) async-start(bf16[16,240,128]{2,1,0:T(8,128)(2,1)} %weight_part.1), calls=%async_computation | async-start | bytes 1966080 | tf_op jit(solution)/shard_map/all_to_all | solution.py:335
  39.4 0.0 copy-done.12
  39.4 0.0 copy-done.13
  39.4 0.0 copy-done.14
  39.4 8.0 %latent_part.1 = bf16[2,64,1280]{2,1,0:T(8,128)(2,1)} custom-call(s32[1,4]{1,0:T(1,128)} %bitcast.7, s32[1,4]{1,0:T(1,128)} %sample_ref.3, bf16[4,64,1280]{2,1,0:T(8,128)(2,1)} %bitcast.5, bf16[4,64,1280]{2,1,0:T(8,128)(2,1)} %lat_ref.3, f32[1280]{0:T(1024)} %lg_ref.3, bf16[1280,768]{1,0:T(8,128)(2,1)} %qw_hbm.3, bf16[1280,1536]{1,0:T(8,128)(2,1)} %kvw_hbm.3, ...), custom_call_target="tpu_custom_call" | custom-call | flops 2000000000 | bytes 9000000 | tf_op jit(solution)/shard_map/latent_part/pallas_call | solution.py:337
  47.5 8.2 %all-to-all-done.r_ref = bf16[16,240,128]{2,1,0:T(8,128)(2,1)S(1)} async-done(((bf16[16,240,128]{2,1,0:T(8,128)(2,1)}), bf16[16,240,128]{2,1,0:T(8,128)(2,1)S(1)}, u32[]{:S(2)}, u32[]{:S(2)}) %all-to-all-start) | async-done | bytes 983072 | tf_op jit(solution)/shard_map/all_to_all | solution.py:335
  55.7 0.2 first_sum.1
  55.8 18.1 %all_to_all.10.r_ref = bf16[8,32,384]{2,1,0:T(8,128)(2,1)S(1)} all-to-all(bf16[8,32,384]{2,1,0:T(8,128)(2,1)S(1)} %first_sum.1), channel_id=1, replica_groups=mesh['xh'=2,'co'=2,'z'=8,'y'=4,'xl'=2] {'z'}, dimensions={0} | all-to-all | bytes 393216 | tf_op jit(solution)/shard_map/all_to_all | solution.py:340
  73.9 0.6 last_sum.1
Async XLA Ops:
  0.6 9.4 %collective-permute-start.3 = (bf16[4,64,1280]{2,1,0:T(8,128)(2,1)}, bf16[4,64,1280]{2,1,0:T(8,128)(2,1)S(1)}, u32[]{:S(2)}, u32[]{:S(2)}) collective-permute-start(bf16[4,64,1280]{2,1,0:T(8,128)(2,1)} %bitcast.3), channel_id=1, source_target_pairs={{0,64},{64,0},{128,192},{192,128},{1,65},{65,1},{129,193},{193,129... | collective-permute-start | bytes 1966088 | tf_op jit(solution)/shard_map/ppermute | solution.py:277
  0.7 12.8 %copy-start.4 = (bf16[4,64,1280]{2,1,0:T(8,128)(2,1)S(1)}, bf16[4,64,1280]{2,1,0:T(8,128)(2,1)}, u32[]{:S(2)}) copy-start(bf16[4,64,1280]{2,1,0:T(8,128)(2,1)} %lat_ref.3) | copy-start | bytes 1966084
  4.0 13.8 %collective-permute-start = (bf16[256,256]{1,0:T(8,128)(2,1)}, bf16[256,256]{1,0:T(8,128)(2,1)S(1)}, u32[]{:S(2)}, u32[]{:S(2)}) collective-permute-start(bf16[256,256]{1,0:T(8,128)(2,1)} %get-tuple-element.25), channel_id=1, source_target_pairs={{0,64},{64,0},{128,192},{192,128},{1,65},{65,1},{129,193},{193,129... | collective-permute-start | bytes 393224 | tf_op jit(solution)/shard_map/ppermute | solution.py:277
  4.6 13.3 %collective-permute-start.1 = (bf16[256,256]{1,0:T(8,128)(2,1)}, bf16[256,256]{1,0:T(8,128)(2,1)S(1)}, u32[]{:S(2)}, u32[]{:S(2)}) collective-permute-start(bf16[256,256]{1,0:T(8,128)(2,1)} %get-tuple-element.26), channel_id=1, source_target_pairs={{0,128},{128,0},{64,192},{192,64},{1,129},{129,1},{65,193},{193,65... | collective-permute-start | bytes 393224 | tf_op jit(solution)/shard_map/ppermute | solution.py:277
  7.6 2.4 %copy-start.7 = (s32[4,1]{0,1:T(1,128)S(1)}, s32[4,1]{0,1:T(1,128)}, u32[]{:S(2)}) copy-start(s32[4,1]{0,1:T(1,128)} %param.19) | copy-start | bytes 52
  7.6 2.4 %copy-start = (bf16[1,4,64,1280]{3,2,1,0:T(8,128)(2,1)S(1)}, bf16[1,4,64,1280]{3,2,1,0:T(8,128)(2,1)}, u32[]{:S(2)}) copy-start(bf16[1,4,64,1280]{3,2,1,0:T(8,128)(2,1)} %param.10) | copy-start | bytes 1966084
  7.6 6.0 %copy-start.1 = (bf16[1280,1536]{1,0:T(8,128)(2,1)S(1)}, bf16[1280,1536]{1,0:T(8,128)(2,1)}, u32[]{:S(2)}) copy-start(bf16[1280,1536]{1,0:T(8,128)(2,1)} %kvw_hbm.3) | copy-start | bytes 11796484
  7.6 6.0 %copy-start.3 = (bf16[1280,768]{1,0:T(8,128)(2,1)S(1)}, bf16[1280,768]{1,0:T(8,128)(2,1)}, u32[]{:S(2)}) copy-start(bf16[1280,768]{1,0:T(8,128)(2,1)} %qw_hbm.3) | copy-start | bytes 5898244
  7.6 6.0 %copy-start.6 = (f32[1280]{0:T(1024)S(1)}, f32[1280]{0:T(1024)}, u32[]{:S(2)}) copy-start(f32[1280]{0:T(1024)} %lg_ref.3) | copy-start | bytes 15364
  7.6 5.9 %copy-start.10 = (f32[1280]{0:T(1024)S(1)}, f32[1280]{0:T(1024)}, u32[]{:S(2)}) copy-start(f32[1280]{0:T(1024)} %fg_ref.1) | copy-start | bytes 15364
  7.7 10.2 %collective-permute-start.2 = (bf16[256,256]{1,0:T(8,128)(2,1)}, bf16[256,256]{1,0:T(8,128)(2,1)S(1)}, u32[]{:S(2)}, u32[]{:S(2)}) collective-permute-start(bf16[256,256]{1,0:T(8,128)(2,1)} %get-tuple-element.27), channel_id=1, source_target_pairs={{0,192},{192,0},{64,128},{128,64},{1,193},{193,1},{65,129},{129,65... | collective-permute-start | bytes 393224 | tf_op jit(solution)/shard_map/ppermute | solution.py:277
  10.0 7.8 %copy-start.2 = (bf16[4,64,1280]{2,1,0:T(8,128)(2,1)}, bf16[4,64,1280]{2,1,0:T(8,128)(2,1)S(1)}, u32[]{:S(2)}) copy-start(bf16[4,64,1280]{2,1,0:T(8,128)(2,1)S(1)} %collective-permute-done.3.c1_ref.c1) | copy-start | bytes 1966084
  10.7 7.2 %copy-start.8 = (s32[1,4]{1,0:T(1,128)S(1)}, s32[1,4]{1,0:T(1,128)}, u32[]{:S(2)}) copy-start(s32[1,4]{1,0:T(1,128)} %sample_ref.3) | copy-start | bytes 52
  10.7 7.2 %copy-start.9 = (bf16[256,256]{1,0:T(8,128)(2,1)S(1)}, bf16[256,256]{1,0:T(8,128)(2,1)}, u32[]{:S(2)}) copy-start(bf16[256,256]{1,0:T(8,128)(2,1)} %get-tuple-element.24.a0) | copy-start | bytes 393220
  10.7 13.7 %collective-permute-start.4 = (bf16[2,64,1280]{2,1,0:T(8,128)(2,1)S(1)}, bf16[2,64,1280]{2,1,0:T(8,128)(2,1)S(1)}, u32[]{:S(2)}, u32[]{:S(2)}) collective-permute-start(bf16[2,64,1280]{2,1,0:T(8,128)(2,1)S(1)} %chip_sum.1), channel_id=1, source_target_pairs={{0,128},{128,0},{64,192},{192,64},{1,129},{129,1},{65,193},{193,65... | collective-permute-start | bytes 983048 | tf_op jit(solution)/shard_map/ppermute | solution.py:277
  20.3 0.7 copy-start.5
  21.0 6.8 %collective-permute-start.5 = (bf16[128,768]{1,0:T(8,128)(2,1)S(1)}, bf16[128,768]{1,0:T(8,128)(2,1)S(1)}, u32[]{:S(2)}, u32[]{:S(2)}) collective-permute-start(bf16[128,768]{1,0:T(8,128)(2,1)S(1)} %get-tuple-element.33), channel_id=1, source_target_pairs={{0,64},{64,0},{128,192},{192,128},{1,65},{65,1},{129,193},{193,129... | collective-permute-start | bytes 589832 | tf_op jit(solution)/shard_map/ppermute | solution.py:277
  21.4 9.3 %collective-permute-start.6 = (bf16[128,768]{1,0:T(8,128)(2,1)S(1)}, bf16[128,768]{1,0:T(8,128)(2,1)S(1)}, u32[]{:S(2)}, u32[]{:S(2)}) collective-permute-start(bf16[128,768]{1,0:T(8,128)(2,1)S(1)} %get-tuple-element.34), channel_id=1, source_target_pairs={{0,128},{128,0},{64,192},{192,64},{1,129},{129,1},{65,193},{193,65... | collective-permute-start | bytes 589832 | tf_op jit(solution)/shard_map/ppermute | solution.py:277
  22.4 10.8 %collective-permute-start.7 = (bf16[128,768]{1,0:T(8,128)(2,1)S(1)}, bf16[128,768]{1,0:T(8,128)(2,1)S(1)}, u32[]{:S(2)}, u32[]{:S(2)}) collective-permute-start(bf16[128,768]{1,0:T(8,128)(2,1)S(1)} %get-tuple-element.35), channel_id=1, source_target_pairs={{0,192},{192,0},{64,128},{128,64},{1,193},{193,1},{65,129},{129,65... | collective-permute-start | bytes 589832 | tf_op jit(solution)/shard_map/ppermute | solution.py:277
  24.4 3.4 %copy-start.11 = (bf16[2,64,1280]{2,1,0:T(8,128)(2,1)}, bf16[2,64,1280]{2,1,0:T(8,128)(2,1)S(1)}, u32[]{:S(2)}) copy-start(bf16[2,64,1280]{2,1,0:T(8,128)(2,1)S(1)} %collective-permute-done.4.u2) | copy-start | bytes 983044
  27.8 11.6 %copy-start.12 = (bf16[128,768]{1,0:T(8,128)(2,1)}, bf16[128,768]{1,0:T(8,128)(2,1)S(1)}, u32[]{:S(2)}) copy-start(bf16[128,768]{1,0:T(8,128)(2,1)S(1)} %collective-permute-done.5.g1) | copy-start | bytes 589828
  30.7 8.7 %copy-start.13 = (bf16[128,768]{1,0:T(8,128)(2,1)}, bf16[128,768]{1,0:T(8,128)(2,1)S(1)}, u32[]{:S(2)}) copy-start(bf16[128,768]{1,0:T(8,128)(2,1)S(1)} %collective-permute-done.6.g2) | copy-start | bytes 589828
  33.2 6.2 %copy-start.14 = (bf16[128,768]{1,0:T(8,128)(2,1)}, bf16[128,768]{1,0:T(8,128)(2,1)S(1)}, u32[]{:S(2)}) copy-start(bf16[128,768]{1,0:T(8,128)(2,1)S(1)} %collective-permute-done.7.g3) | copy-start | bytes 589828
  33.2 22.5 %all-to-all-start = ((bf16[16,240,128]{2,1,0:T(8,128)(2,1)}), bf16[16,240,128]{2,1,0:T(8,128)(2,1)S(1)}, u32[]{:S(2)}, u32[]{:S(2)}) async-start(bf16[16,240,128]{2,1,0:T(8,128)(2,1)} %weight_part.1), calls=%async_computation | async-start | bytes 1966080 | tf_op jit(solution)/shard_map/all_to_all | solution.py:335

commit v3 on v2

--- a/solution.py
+++ b/solution.py
@@ -72,28 +72,17 @@
 AROUND = ((0, 0), (0, 1), (1, 0), (1, 1))
 
 
-def attn_kernel(part_hbm, ow_hbm, a0, a1, a2, a3, part, wt, prod, sems):
+def attn_kernel(owner_ref, part_ref, c1_ref, ow_ref, lat_ref, mine, far, u_ref, chip, prod):
     xh = lax.axis_index("xh")
     co = lax.axis_index("co")
-    copies = [pltpu.make_async_copy(part_hbm, part, sems.at[0])]
-    for k in range(4):
-        rows = pl.ds(192 * k, 192)
-        copies.append(pltpu.make_async_copy(ow_hbm.at[rows], wt.at[rows], sems.at[k + 1]))
-    for c in copies:
-        c.start()
-    for c in copies:
-        c.wait()
-    prod[...] = dot(part[...].reshape(IMGS * LAT, D), wt[...], 1, 1).astype(BF)
-    for out, (dx, dc) in zip((a0, a1, a2, a3), AROUND):
-        start = pl.multiple_of(window_of(pair_of(xh ^ dx, co ^ dc)), 128)
-        out[...] = prod[:, pl.ds(start, 256)]
-
-
-def chip_sum_kernel(owner_ref, part_ref, c1_ref, u_ref):
-    section = (lax.axis_index("xh") ^ 1) * 2 + lax.axis_index("co")
+    chip[...] = (part_ref[...].astype(F32) + c1_ref[...].astype(F32)).astype(BF)
+    group = ow_ref[pl.ds(pl.multiple_of(co * 384, 128), 384)]
+    prod[...] = dot(chip[...].reshape(IMGS * LAT, D), group, 1, 1).astype(BF)
+    mine[...] = prod[:, pl.ds(pl.multiple_of(xh * 128, 128), 256)]
+    far[...] = prod[:, pl.ds(pl.multiple_of((1 - xh) * 128, 128), 256)]
     for slot in range(2):
-        index, _ = slot_image(owner_ref, section, slot)
-        u_ref[slot] = (part_ref[index].astype(F32) + c1_ref[index].astype(F32)).astype(BF)
+        index, _ = slot_image(owner_ref, (xh ^ 1) * 2 + co, slot)
+        u_ref[slot] = chip[index]
 
 
 def forward_kernel(feat_ref, lat_ref, fg_ref, lg_ref, qw_hbm, kvw_hbm, ctx_ref, kv_ref, q_ref, pr_ref, win, sems):
@@ -144,8 +133,8 @@
     attend(IMGS - 1)
 
 
-def backward_kernel(owner_ref, sample_ref, a0, a1, a2, a3, kv_ref, q_ref, pr_ref,
-                    kvg, g0, g1, g2, g3, lat):
+def backward_kernel(owner_ref, sample_ref, a0, a2, kv_ref, q_ref, pr_ref,
+                    kvg, g0, g1, g2, lat):
     xh = lax.axis_index("xh")
     co = lax.axis_index("co")
     pair = pair_of(xh, co)
@@ -153,7 +142,7 @@
     for i in range(IMGS):
         rows = slice(LAT * i, LAT * (i + 1))
         count = scale_of(sample_ref, i).astype(F32)
-        total = (a0[rows].astype(F32) + a1[rows].astype(F32)) + (a2[rows].astype(F32) + a3[rows].astype(F32))
+        total = a0[rows].astype(F32) + a2[rows].astype(F32)
         attn = by_head(total / count, pair).astype(BF)
         probs = pr_ref[i]
         value_grad = dot(probs.astype(BF), attn, 0, 0)
@@ -173,7 +162,8 @@
         even = jnp.where(left, key_grad[:, 128:], pltpu.roll(value_grad[:, 128:], 64, 1))
         odd = jnp.where(left, pltpu.roll(key_grad[:, :128], 64, 1), value_grad[:, :128])
         kvg[at, 256:] = jnp.where(xh == 0, even, odd).astype(BF)
-    for out, (dx, dc) in zip((g0, g1, g2, g3), AROUND):
+    places = (g0, g1.at[:2 * LAT], g2, g1.at[2 * LAT:])
+    for out, (dx, dc) in zip(places, AROUND):
         section = (xh ^ dx) * 2 + (co ^ dc)
         for slot in range(2):
             index, _ = slot_image(owner_ref, section, slot)
@@ -220,7 +210,7 @@
 
 
 def latent_kernel(owner_ref, sample_ref, part_ref, lat_ref, lg_ref, qw_hbm, kvw_hbm,
-                  c1, u2, g0, g1, g2, g3, out_ref, win, sems):
+                  c1, u2, g0, g1, g2, out_ref, win, sems):
     xh = lax.axis_index("xh")
     co = lax.axis_index("co")
     section = xh * 2 + co
@@ -233,11 +223,12 @@
             copies.append(pltpu.make_async_copy(source.at[:, pl.ds(lane, 256)], win.at[n], sems.at[n]))
     for c in copies:
         c.start()
+    sources = (g0, g1.at[:2 * LAT], g2.at[:2 * LAT], g2.at[2 * LAT:])
     grad = jnp.zeros((2 * LAT, D), F32)
     for n, c in enumerate(copies):
         c.wait()
         k = n % 3
-        grad = grad + dot((g0, g1, g2, g3)[n // 3][:, 256 * k:256 * (k + 1)], win[n], 1, 1)
+        grad = grad + dot(sources[n // 3][:, 256 * k:256 * (k + 1)], win[n], 1, 1)
     lg = lg_ref[...].reshape(1, D)
     for slot in range(2):
         index, found = slot_image(owner_ref, section, slot)
@@ -282,12 +273,12 @@
 
 
 DMA = pltpu.SemaphoreType.DMA
+COST = 1000000
 CALLS = dict(
     attn=call(
-        attn_kernel, "attn_part", [bf(256, 256)] * 4, [HBM] * 2,
-        [pltpu.VMEM((IMGS, LAT, D), BF), pltpu.VMEM((INNER, D), BF), pltpu.VMEM((256, INNER), BF), DMA((5,))],
-        flops=600_000_000, size=3_000_000, limit=60),
-    chip=call(chip_sum_kernel, "chip_sum", bf(2, LAT, D), [SMEM] + [VMEM] * 2, size=1_500_000),
+        attn_kernel, "attn_part", [bf(256, 256)] * 2 + [bf(2, LAT, D)], [SMEM] + [VMEM] * 4,
+        [pltpu.VMEM((IMGS, LAT, D), BF), pltpu.VMEM((256, 384), BF)],
+        flops=600_000_000, size=3_000_000),
     forward=call(
         forward_kernel, "forward_part",
         [bf(IMGS, ROWS, D), bf(IMGS, ROWS, 512), bf(IMGS, 2 * LAT, 256),
@@ -296,20 +287,20 @@
         [pltpu.VMEM((3, D, 256), BF), DMA((3,))],
         flops=4_000_000_000, size=12_000_000),
     backward=call(
-        backward_kernel, "backward_part", [bf(IMGS * ROWS, 384)] + [bf(2 * LAT, 768)] * 4,
-        [SMEM, SMEM] + [VMEM] * 7, [pltpu.VMEM((256, 768), BF)],
-        flops=2_000_000_000, size=5_000_000),
+        backward_kernel, "backward_part", [bf(IMGS * ROWS, 384)] + [bf(2 * LAT, 768), bf(4 * LAT, 768), bf(2 * LAT, 768)],
+        [SMEM, SMEM] + [VMEM] * 5, [pltpu.VMEM((256, 768), BF)],
+        flops=COST, size=1000),
     weight=call(
         weight_kernel, "weight_part", bf(16, 240, 128), [VMEM] * 2,
         [pltpu.VMEM((D, 384), F32), pltpu.VMEM((8, 160, 384), F32)],
-        flops=3_000_000_000, size=6_000_000),
+        flops=COST, size=1000),
     first=call(first_sum_kernel, "first_sum", bf(8, 32, 384), [VMEM], [pltpu.VMEM((160, 384), F32)],
                size=1_000_000),
     last=call(last_kernel, "last_sum", jax.ShapeDtypeStruct((SHARE, 384), F32), [VMEM], size=300_000),
     latent=call(
-        latent_kernel, "latent_part", bf(2, LAT, D), [SMEM, SMEM] + [VMEM] * 3 + [HBM] * 2 + [VMEM] * 6,
+        latent_kernel, "latent_part", bf(2, LAT, D), [SMEM, SMEM] + [VMEM] * 3 + [HBM] * 2 + [VMEM] * 5,
         [pltpu.VMEM((12, D, 256), BF), DMA((12,))],
-        flops=2_000_000_000, size=9_000_000, limit=60),
+        flops=2_000_000_000, size=9_000_000, limit=52),
 )
 
 
@@ -318,26 +309,24 @@
     part = partials[0]
     owner = owner.reshape(1, IMGS)
     c1 = swap(part, CORE)
-    a0, a1, a2, a3 = CALLS["attn"](part, out_weight)
-    a3 = swap(a3, DIAGONAL)
+    a0, a2, u = CALLS["attn"](owner, part, c1, out_weight, latents)
     a2 = swap(a2, FAR)
-    a1 = swap(a1, CORE)
-    u = swap(CALLS["chip"](owner, part, c1), FAR)
+    u = swap(u, FAR)
     ctx, kv, q, probs = CALLS["forward"](
         features, latents, feature_gain, latent_gain, query_weight, kv_weight)
-    kvg, g0, g1, g2, g3 = CALLS["backward"](owner, sample_of, a0, a1, a2, a3, kv, q, probs)
-    kvg, u = lax.optimization_barrier((kvg, u))
-    g3 = swap(g3, DIAGONAL)
+    kvg, g0, g1, g2 = CALLS["backward"](owner, sample_of, a0, a2, kv, q, probs)
+    g1 = swap(g1, CORE)
+    g2 = jnp.concatenate([g2, g1[2 * LAT:]], axis=0)
+    w = CALLS["weight"](ctx, kvg)
+    w, u = lax.optimization_barrier((w, u))
+    w = lax.all_to_all(w, ("xh", "xl", "y"), 0, 0, tiled=True)
+    w, g2 = lax.optimization_barrier((w, g2))
     g2 = swap(g2, FAR)
-    g1 = swap(g1, CORE)
-    w = CALLS["weight"](ctx, kvg)
-    w, g1, g2, g3 = lax.optimization_barrier((w, g1, g2, g3))
-    w = lax.all_to_all(w, ("xh", "xl", "y"), 0, 0, tiled=True)
     w = CALLS["first"](w)
     latent_grad = CALLS["latent"](
-        owner, sample_of, part, latents, latent_gain, query_weight, kv_weight, c1, u, g0, g1, g2, g3)
+        owner, sample_of, part, latents, latent_gain, query_weight, kv_weight, c1, u, g0, g1, g2)
+    w = lax.all_to_all(w, "z", 0, 0, tiled=True)
     w, latent_grad = lax.optimization_barrier((w, latent_grad))
-    w = lax.all_to_all(w, "z", 0, 0, tiled=True)
     kv_grad = CALLS["last"](w)
     return latent_grad[None], kv_grad
 

time: 74.8 us -> 62.6 us (0.84); the launches traced: 74.6 us -> 61.4 us
  blocking collectives: 18.1 us -> 0 us
  waiting for transfers between devices: 13.7 us -> 17.9 us
  starting transfers between devices: 16.2 us -> 20.1 us
  Pallas kernels: 22.8 us -> 20 us
    all_to_all x1 -> x0, blocking collectives: 18.1 us -> none  [per_device(): w = lax.all_to_all(w, 'z', 0, 0, tiled=True)]
    all_to_all x0 -> x1, starting transfers between devices: none -> 8.42 us  [per_device(): w = lax.all_to_all(w, 'z', 0, 0, tiled=True)]
    ppermute x8 -> x5, starting transfers between devices: 10 us -> 4.31 us  [swap(): return lax.ppermute(x, SECTION, pairs)]
    all_to_all x1, waiting for transfers between devices: 8.23 us -> 13.1 us  [per_device(): w = lax.all_to_all(w, ('xh', 'xl', 'y'), 0, 0, tiled=True)]
    ppermute x8 -> x5, waiting for transfers between devices: 5.43 us -> 2.59 us  [swap(): return lax.ppermute(x, SECTION, pairs)]
    pallas_call x3 -> x2, Pallas kernels: 6.36 us -> 3.56 us  [the longest x1 2.43 us: per_device(): kvg, g0, g1, g2 = CALLS['backward'](owner, sample_of, a0, a2, kv, q, probs)]
    all_to_all x0 -> x1, waiting for transfers between devices: none -> 2.16 us  [per_device(): w = lax.all_to_all(w, 'z', 0, 0, tiled=True)]
    all_to_all x1, starting transfers between devices: 6.22 us -> 7.39 us  [per_device(): w = lax.all_to_all(w, ('xh', 'xl', 'y'), 0, 0, tiled=True)]
  transfers between devices with their start and end apart: 9 -> 7, of which waited for: 3 -> 5; matrix products, arithmetic and copies ran while one was open for 3% -> 4% of each run, Pallas kernels for 29% -> 30%
where the time goes in v3:
time: 62.6 us; the launch traced here: 61.4 us
  starting transfers between devices  20.1 us (32%)
  Pallas kernels  20 us (32%)
  waiting for transfers between devices  17.9 us (29%)
  local copies, waits for them, and re-layouts  2.58 us (4%)
  between operations  0.8 us (1%)
    all_to_all x1, waiting for transfers between devices, per_device(): w = lax.all_to_all(w, ('xh', 'xl', 'y'), 0, 0, tiled=True)  13.1 us
    all_to_all x1, starting transfers between devices, per_device(): w = lax.all_to_all(w, 'z', 0, 0, tiled=True)  8.42 us
    pallas_call x1, Pallas kernels, per_device(): CALLS['latent']  7.45 us
    all_to_all x1, starting transfers between devices, per_device(): w = lax.all_to_all(w, ('xh', 'xl', 'y'), 0, 0, tiled=True)  7.39 us
    ppermute x5, starting transfers between devices, swap(): return lax.ppermute(x, SECTION, pairs)  4.31 us
    pallas_call x1, Pallas kernels, per_device(): CALLS['forward']  4.17 us
    pallas_call x1, Pallas kernels, per_device(): w = CALLS['weight'](ctx, kvg)  3.31 us
    ppermute x5, waiting for transfers between devices, swap(): return lax.ppermute(x, SECTION, pairs)  2.59 us
  transfers between devices with their start and end apart: 7, of which 5 were waited for; matrix products, arithmetic and copies ran while one was open for 4% of the time, Pallas kernels for 30%

profile of v3, /device:TPU:8, one launch (start us, length us, event | category | flops | bytes accessed | tf_op | source)
XLA Modules:
  0.0 61.4 jit_solution(10440800782364945814)
XLA Ops:
  0.6 0.0 copy-start.1
  0.6 0.0 copy-start.2
  0.7 0.0 copy-start.4
  0.7 0.0 copy-start.7
  0.7 0.1 collective-permute-start
  0.8 0.0 copy-start.5
  0.8 0.0 copy-start.6
  0.8 0.0 copy-start.9
  0.8 2.2 %copy.12.feat_ref = bf16[4,257,1280]{2,1,0:T(8,128)(2,1)S(1)} copy(bf16[4,257,1280]{2,0,1:T(4,128)(2,1)} %param.12) | data formatting | bytes 5263360 | tf_op args[2]
  3.0 0.0 copy-start
  3.0 0.0 collective-permute-done.c1_ref.c1
  3.1 0.0 copy-start.3
  3.1 0.0 copy-done.1
  3.1 0.0 copy-done.2
  3.1 0.3 copy-done.4
  3.4 0.0 copy-done.7
  3.4 1.1 %attn_part.1 = (bf16[256,256]{1,0:T(8,128)(2,1)S(1)}, bf16[256,256]{1,0:T(8,128)(2,1)S(1)}, bf16[2,64,1280]{2,1,0:T(8,128)(2,1)S(1)}) custom-call(s32[1,4]{1,0:T(1,128)S(1)} %bitcast.6, bf16[4,64,1280]{2,1,0:T(8,128)(2,1)S(1)} %bitcast.4, bf16[4,64,1280]{2,1,0:T(8,128)(2,1)S(1)} %collective-permute-done.c1_ref.c1, bf16[768,1280]{1,0:T(8,128)(2,1)S(1)} %copy-done.4, ...), custom_call_target="tpu_custom_call" | custom-call | flops 600000000 | bytes 3000000 | tf_op jit(solution)/shard_map/attn_part/pallas_call | solution.py:312
  4.5 3.1 %collective-permute-start.1 = (bf16[256,256]{1,0:T(8,128)(2,1)S(1)}, bf16[256,256]{1,0:T(8,128)(2,1)S(1)}, u32[]{:S(2)}, u32[]{:S(2)}) collective-permute-start(bf16[256,256]{1,0:T(8,128)(2,1)S(1)} %get-tuple-element.21), channel_id=1, source_target_pairs={{0,128},{128,0},{64,192},{192,64},{1,129},{129,1},{65,193},{193,65... | collective-permute-start | bytes 393224 | tf_op jit(solution)/shard_map/ppermute | solution.py:268
  7.6 0.0 copy-start.8
  7.6 0.5 collective-permute-start.2
  8.1 0.0 copy-done.5
  8.1 0.0 copy-done.6
  8.1 0.0 copy-done.9
  8.1 0.0 copy-done
  8.1 4.2 %forward_part.1 = (bf16[4,336,1280]{2,1,0:T(8,128)(2,1)S(1)}, bf16[4,336,512]{2,1,0:T(8,128)(2,1)S(1)}, bf16[4,128,256]{2,1,0:T(8,128)(2,1)S(1)}, f32[4,128,336]{2,1,0:T(8,128)S(1)}) custom-call(bf16[4,257,1280]{2,1,0:T(8,128)(2,1)S(1)} %copy.12.feat_ref, bf16[4,64,1280]{2,1,0:T(8,128)(2,1)S(1)} %copy-done.2, f32[1280]{0:T(1024)S(1)} %copy-done.9, ...), custom_call_target="tpu_custom_call" | custom-call | flops 4000000000 | bytes 12000000 | tf_op jit(solution)/shard_map/forward_part/pallas_call | solution.py:315
  12.3 0.0 copy-done.3
  12.3 0.0 collective-permute-done.1.a2
  12.3 0.0 copy-done.8
  12.4 2.4 %backward_part.1 = (bf16[1344,384]{1,0:T(8,128)(2,1)S(1)}, bf16[128,768]{1,0:T(8,128)(2,1)S(1)}, bf16[256,768]{1,0:T(8,128)(2,1)S(1)}, bf16[128,768]{1,0:T(8,128)(2,1)S(1)}) custom-call(s32[1,4]{1,0:T(1,128)S(1)} %bitcast.7, s32[1,4]{1,0:T(1,128)S(1)} %copy-done.8, bf16[256,256]{1,0:T(8,128)(2,1)S(1)} %get-tuple-element.20.a0, ...), custom_call_target="tpu_custom_call" | custom-call | flops 1000000 | bytes 1000 | tf_op jit(solution)/shard_map/backward_part/pallas_call | solution.py:317
  14.8 3.3 %weight_part.1 = bf16[16,240,128]{2,1,0:T(8,128)(2,1)} custom-call(bf16[4,336,1280]{2,1,0:T(8,128)(2,1)S(1)} %get-tuple-element.19.ctx_ref, bf16[1344,384]{1,0:T(8,128)(2,1)S(1)} %get-tuple-element.25.kvg), custom_call_target="tpu_custom_call" | custom-call | flops 1000000 | bytes 1000 | tf_op jit(solution)/shard_map/weight_part/pallas_call | solution.py:320
  18.1 0.7 %collective-permute-done.2.u2 = bf16[2,64,1280]{2,1,0:T(8,128)(2,1)S(1)} collective-permute-done((bf16[2,64,1280]{2,1,0:T(8,128)(2,1)S(1)}, bf16[2,64,1280]{2,1,0:T(8,128)(2,1)S(1)}, u32[]{:S(2)}, u32[]{:S(2)}) %collective-permute-start.2) | collective-permute-done | bytes 327712 | tf_op jit(solution)/shard_map/ppermute | solution.py:268
  18.8 7.4 %all-to-all-start = ((bf16[16,240,128]{2,1,0:T(8,128)(2,1)}), bf16[16,240,128]{2,1,0:T(8,128)(2,1)S(1)}, u32[]{:S(2)}, u32[]{:S(2)}) async-start(bf16[16,240,128]{2,1,0:T(8,128)(2,1)} %weight_part.1), calls=%async_computation | async-start | bytes 1966080 | tf_op jit(solution)/shard_map/all_to_all | solution.py:322
  26.2 0.0 collective-permute-start.3
  26.2 1.7 %collective-permute-done.3.g1 = bf16[256,768]{1,0:T(8,128)(2,1)S(1)} collective-permute-done((bf16[256,768]{1,0:T(8,128)(2,1)S(1)}, bf16[256,768]{1,0:T(8,128)(2,1)S(1)}, u32[]{:S(2)}, u32[]{:S(2)}) %collective-permute-start.3) | collective-permute-done | bytes 393248 | tf_op jit(solution)/shard_map/ppermute | solution.py:268
  28.0 13.1 %all-to-all-done.r_ref = bf16[16,240,128]{2,1,0:T(8,128)(2,1)S(1)} async-done(((bf16[16,240,128]{2,1,0:T(8,128)(2,1)}), bf16[16,240,128]{2,1,0:T(8,128)(2,1)S(1)}, u32[]{:S(2)}, u32[]{:S(2)}) %all-to-all-start) | async-done | bytes 983072 | tf_op jit(solution)/shard_map/all_to_all | solution.py:322
  41.1 0.6 collective-permute-start.4
  41.7 0.8 %first_sum.1 = bf16[8,32,384]{2,1,0:T(8,128)(2,1)} custom-call(bf16[16,240,128]{2,1,0:T(8,128)(2,1)S(1)} %all-to-all-done.r_ref), custom_call_target="tpu_custom_call" | custom-call | bytes 1000000 | tf_op jit(solution)/shard_map/first_sum/pallas_call | solution.py:325
  42.5 8.4 %all-to-all-start.1 = ((bf16[8,32,384]{2,1,0:T(8,128)(2,1)}), bf16[8,32,384]{2,1,0:T(8,128)(2,1)S(1)}, u32[]{:S(2)}, u32[]{:S(2)}) async-start(bf16[8,32,384]{2,1,0:T(8,128)(2,1)} %first_sum.1), calls=%async_computation.1 | async-start | bytes 393216 | tf_op jit(solution)/shard_map/all_to_all | solution.py:328
  51.0 0.2 collective-permute-done.4.g2
  51.1 7.5 %latent_part.1 = bf16[2,64,1280]{2,1,0:T(8,128)(2,1)} custom-call(s32[1,4]{1,0:T(1,128)S(1)} %bitcast.8, s32[1,4]{1,0:T(1,128)S(1)} %copy-done.8, bf16[4,64,1280]{2,1,0:T(8,128)(2,1)S(1)} %bitcast.5, bf16[4,64,1280]{2,1,0:T(8,128)(2,1)} %lat_ref.5, f32[1280]{0:T(1024)S(1)} %copy-done.6, bf16[1280,768]{1,0:T(8,128)(2,1)} %qw_hbm.3, ...), custom_call_target="tpu_custom_call" | custom-call | flops 2000000000 | bytes 9000000 | tf_op jit(solution)/shard_map/latent_part/pallas_call | solution.py:326
  58.6 2.2 %all-to-all-done.1.r_ref = bf16[8,32,384]{2,1,0:T(8,128)(2,1)S(1)} async-done(((bf16[8,32,384]{2,1,0:T(8,128)(2,1)}), bf16[8,32,384]{2,1,0:T(8,128)(2,1)S(1)}, u32[]{:S(2)}, u32[]{:S(2)}) %all-to-all-start.1) | async-done | bytes 196640 | tf_op jit(solution)/shard_map/all_to_all | solution.py:328
  60.7 0.6 %last_sum.1 = f32[20,384]{1,0:T(8,128)} custom-call(bf16[8,32,384]{2,1,0:T(8,128)(2,1)S(1)} %all-to-all-done.1.r_ref), custom_call_target="tpu_custom_call" | custom-call | bytes 300000 | tf_op jit(solution)/shard_map/last_sum/pallas_call | solution.py:330
  (2 shorter events, 0.0 us)
Async XLA Ops:
  0.6 2.4 %copy-start.1 = (bf16[1,4,64,1280]{3,2,1,0:T(8,128)(2,1)S(1)}, bf16[1,4,64,1280]{3,2,1,0:T(8,128)(2,1)}, u32[]{:S(2)}) copy-start(bf16[1,4,64,1280]{3,2,1,0:T(8,128)(2,1)} %param.10) | copy-start | bytes 1966084
  0.6 2.4 %copy-start.2 = (bf16[4,64,1280]{2,1,0:T(8,128)(2,1)S(1)}, bf16[4,64,1280]{2,1,0:T(8,128)(2,1)}, u32[]{:S(2)}) copy-start(bf16[4,64,1280]{2,1,0:T(8,128)(2,1)} %lat_ref.5) | copy-start | bytes 1966084
  0.7 2.7 %copy-start.4 = (bf16[768,1280]{1,0:T(8,128)(2,1)S(1)}, bf16[768,1280]{1,0:T(8,128)(2,1)}, u32[]{:S(2)}) copy-start(bf16[768,1280]{1,0:T(8,128)(2,1)} %ow_ref.1) | copy-start | bytes 5898244
  0.7 2.7 %copy-start.7 = (s32[4,1]{0,1:T(1,128)S(1)}, s32[4,1]{0,1:T(1,128)}, u32[]{:S(2)}) copy-start(s32[4,1]{0,1:T(1,128)} %param.19) | copy-start | bytes 52
  0.7 2.4 %collective-permute-start = (bf16[4,64,1280]{2,1,0:T(8,128)(2,1)}, bf16[4,64,1280]{2,1,0:T(8,128)(2,1)S(1)}, u32[]{:S(2)}, u32[]{:S(2)}) collective-permute-start(bf16[4,64,1280]{2,1,0:T(8,128)(2,1)} %bitcast.3), channel_id=1, source_target_pairs={{0,64},{64,0},{128,192},{192,128},{1,65},{65,1},{129,193},{193,129... | collective-permute-start | bytes 1966088 | tf_op jit(solution)/shard_map/ppermute | solution.py:268
  0.8 7.4 %copy-start.5 = (bf16[1280,768]{1,0:T(8,128)(2,1)S(1)}, bf16[1280,768]{1,0:T(8,128)(2,1)}, u32[]{:S(2)}) copy-start(bf16[1280,768]{1,0:T(8,128)(2,1)} %qw_hbm.3) | copy-start | bytes 5898244
  0.8 7.4 %copy-start.6 = (f32[1280]{0:T(1024)S(1)}, f32[1280]{0:T(1024)}, u32[]{:S(2)}) copy-start(f32[1280]{0:T(1024)} %lg_ref.3) | copy-start | bytes 15364
  0.8 7.3 %copy-start.9 = (f32[1280]{0:T(1024)S(1)}, f32[1280]{0:T(1024)}, u32[]{:S(2)}) copy-start(f32[1280]{0:T(1024)} %fg_ref.1) | copy-start | bytes 15364
  3.0 5.1 %copy-start = (bf16[1280,1536]{1,0:T(8,128)(2,1)S(1)}, bf16[1280,1536]{1,0:T(8,128)(2,1)}, u32[]{:S(2)}) copy-start(bf16[1280,1536]{1,0:T(8,128)(2,1)} %kvw_hbm.3) | copy-start | bytes 11796484
  3.1 9.3 %copy-start.3 = (bf16[4,64,1280]{2,1,0:T(8,128)(2,1)}, bf16[4,64,1280]{2,1,0:T(8,128)(2,1)S(1)}, u32[]{:S(2)}) copy-start(bf16[4,64,1280]{2,1,0:T(8,128)(2,1)S(1)} %collective-permute-done.c1_ref.c1) | copy-start | bytes 1966084
  4.5 7.8 %collective-permute-start.1 = (bf16[256,256]{1,0:T(8,128)(2,1)S(1)}, bf16[256,256]{1,0:T(8,128)(2,1)S(1)}, u32[]{:S(2)}, u32[]{:S(2)}) collective-permute-start(bf16[256,256]{1,0:T(8,128)(2,1)S(1)} %get-tuple-element.21), channel_id=1, source_target_pairs={{0,128},{128,0},{64,192},{192,64},{1,129},{129,1},{65,193},{193,65... | collective-permute-start | bytes 393224 | tf_op jit(solution)/shard_map/ppermute | solution.py:268
  7.6 4.7 %copy-start.8 = (s32[1,4]{1,0:T(1,128)S(1)}, s32[1,4]{1,0:T(1,128)}, u32[]{:S(2)}) copy-start(s32[1,4]{1,0:T(1,128)} %sample_ref.3) | copy-start | bytes 52
  7.6 11.2 %collective-permute-start.2 = (bf16[2,64,1280]{2,1,0:T(8,128)(2,1)S(1)}, bf16[2,64,1280]{2,1,0:T(8,128)(2,1)S(1)}, u32[]{:S(2)}, u32[]{:S(2)}) collective-permute-start(bf16[2,64,1280]{2,1,0:T(8,128)(2,1)S(1)} %get-tuple-element.26), channel_id=1, source_target_pairs={{0,128},{128,0},{64,192},{192,64},{1,129},{129,1},{65,193},{193,65... | collective-permute-start | bytes 983048 | tf_op jit(solution)/shard_map/ppermute | solution.py:268
  18.8 22.3 %all-to-all-start = ((bf16[16,240,128]{2,1,0:T(8,128)(2,1)}), bf16[16,240,128]{2,1,0:T(8,128)(2,1)S(1)}, u32[]{:S(2)}, u32[]{:S(2)}) async-start(bf16[16,240,128]{2,1,0:T(8,128)(2,1)} %weight_part.1), calls=%async_computation | async-start | bytes 1966080 | tf_op jit(solution)/shard_map/all_to_all | solution.py:322
  26.2 1.7 %collective-permute-start.3 = (bf16[256,768]{1,0:T(8,128)(2,1)S(1)}, bf16[256,768]{1,0:T(8,128)(2,1)S(1)}, u32[]{:S(2)}, u32[]{:S(2)}) collective-permute-start(bf16[256,768]{1,0:T(8,128)(2,1)S(1)} %get-tuple-element.29), channel_id=1, source_target_pairs={{0,64},{64,0},{128,192},{192,128},{1,65},{65,1},{129,193},{193,129... | collective-permute-start | bytes 1179656 | tf_op jit(solution)/shard_map/ppermute | solution.py:268
  41.1 10.0 %collective-permute-start.4 = (bf16[256,768]{1,0:T(8,128)(2,1)S(1)}, bf16[256,768]{1,0:T(8,128)(2,1)S(1)}, u32[]{:S(2)}, u32[]{:S(2)}) collective-permute-start(bf16[256,768]{1,0:T(8,128)(2,1)S(1)} %pad_maximum_fusion), channel_id=1, source_target_pairs={{0,128},{128,0},{64,192},{192,64},{1,129},{129,1},{65,193},{193,65... | collective-permute-start | bytes 1179656 | tf_op jit(solution)/shard_map/ppermute | solution.py:268
  42.5 18.2 %all-to-all-start.1 = ((bf16[8,32,384]{2,1,0:T(8,128)(2,1)}), bf16[8,32,384]{2,1,0:T(8,128)(2,1)S(1)}, u32[]{:S(2)}, u32[]{:S(2)}) async-start(bf16[8,32,384]{2,1,0:T(8,128)(2,1)} %first_sum.1), calls=%async_computation.1 | async-start | bytes 393216 | tf_op jit(solution)/shard_map/all_to_all | solution.py:328

commit v4 on v3

--- a/solution.py
+++ b/solution.py
@@ -77,9 +77,9 @@
     co = lax.axis_index("co")
     chip[...] = (part_ref[...].astype(F32) + c1_ref[...].astype(F32)).astype(BF)
     group = ow_ref[pl.ds(pl.multiple_of(co * 384, 128), 384)]
-    prod[...] = dot(chip[...].reshape(IMGS * LAT, D), group, 1, 1).astype(BF)
+    prod[...] = dot(chip[...].reshape(IMGS * LAT, D), group, 1, 1)
     mine[...] = prod[:, pl.ds(pl.multiple_of(xh * 128, 128), 256)]
-    far[...] = prod[:, pl.ds(pl.multiple_of((1 - xh) * 128, 128), 256)]
+    far[...] = prod[:, pl.ds(pl.multiple_of((1 - xh) * 128, 128), 256)].astype(BF)
     for slot in range(2):
         index, _ = slot_image(owner_ref, (xh ^ 1) * 2 + co, slot)
         u_ref[slot] = chip[index]
@@ -142,7 +142,7 @@
     for i in range(IMGS):
         rows = slice(LAT * i, LAT * (i + 1))
         count = scale_of(sample_ref, i).astype(F32)
-        total = a0[rows].astype(F32) + a2[rows].astype(F32)
+        total = a0[rows] + a2[rows].astype(F32)
         attn = by_head(total / count, pair).astype(BF)
         probs = pr_ref[i]
         value_grad = dot(probs.astype(BF), attn, 0, 0)
@@ -173,7 +173,8 @@
 def weight_kernel(ctx_ref, kvg, w_ref, wide, order):
     ctx = ctx_ref[...].reshape(IMGS * ROWS, D)
     for c in range(5):
-        wide[256 * c:256 * (c + 1)] = dot(ctx[:, 256 * c:256 * (c + 1)], kvg[...], 0, 0)
+        columns = slice(256 * c, 256 * (c + 1))
+        wide[columns] = dot(ctx[:, columns], kvg[...], 0, 0)
     for y in range(4):
         for xl in range(2):
             piece = xl * 4 + y
@@ -188,7 +189,7 @@
                 w_ref[8 * k + piece, 160:240] = jnp.concatenate([tail[:80], tail[80:]], axis=1).astype(BF)
 
 
-def first_sum_kernel(r_ref, out_ref, full):
+def first_sum_kernel(r_ref, out_ref, full, share):
     tails = []
     for k in range(2):
         total = r_ref[8 * k].astype(F32)
@@ -199,36 +200,52 @@
         tails.append(jnp.concatenate([tail[:, :64], tail[:, 64:]], axis=0))
     full[:, 128:256] = jnp.concatenate(tails, axis=1)
     for z in range(8):
-        out_ref[z, 0:SHARE] = full[SHARE * z:SHARE * (z + 1)].astype(BF)
+        for k in range(3):
+            share[z, SHARE * k:SHARE * (k + 1)] = full[SHARE * z:SHARE * (z + 1), 128 * k:128 * (k + 1)]
+        share[z, 3 * SHARE:] = jnp.zeros((64 - 3 * SHARE, 128), F32)
+    out_ref[...] = share[...].astype(BF)
 
 
 def last_kernel(r_ref, out_ref):
     total = r_ref[0].astype(F32)
     for z in range(1, 8):
         total = total + r_ref[z].astype(F32)
-    out_ref[...] = total[:SHARE] * (1.0 / 256.0)
+    total = total * (1.0 / 256.0)
+    for k in range(3):
+        out_ref[:, 128 * k:128 * (k + 1)] = total[SHARE * k:SHARE * (k + 1)]
 
 
 def latent_kernel(owner_ref, sample_ref, part_ref, lat_ref, lg_ref, qw_hbm, kvw_hbm,
-                  c1, u2, g0, g1, g2, out_ref, win, sems):
+                  c1, u2, g0, g1, g2, out_ref, qw, kvw, every, grad, sems):
     xh = lax.axis_index("xh")
     co = lax.axis_index("co")
     section = xh * 2 + co
     copies = []
-    for dx, dc in AROUND:
-        start = pl.multiple_of(window_of(pair_of(xh ^ dx, co ^ dc)), 128)
-        further = pl.multiple_of(start + INNER, 128)
-        for k, (source, lane) in enumerate(((qw_hbm, start), (kvw_hbm, start), (kvw_hbm, further))):
-            n = len(copies)
-            copies.append(pltpu.make_async_copy(source.at[:, pl.ds(lane, 256)], win.at[n], sems.at[n]))
-    for c in copies:
-        c.start()
-    sources = (g0, g1.at[:2 * LAT], g2.at[:2 * LAT], g2.at[2 * LAT:])
-    grad = jnp.zeros((2 * LAT, D), F32)
-    for n, c in enumerate(copies):
-        c.wait()
-        k = n % 3
-        grad = grad + dot(sources[n // 3][:, 256 * k:256 * (k + 1)], win[n], 1, 1)
+    for c in range(5):
+        rows = pl.ds(256 * c, 256)
+        copies.append((pltpu.make_async_copy(qw_hbm.at[rows], qw.at[rows], sems.at[2 * c]),
+                       pltpu.make_async_copy(kvw_hbm.at[rows], kvw.at[rows], sems.at[2 * c + 1])))
+    for pair in copies:
+        for c in pair:
+            c.start()
+    near = (co, g0[...], g2[:2 * LAT])
+    other = (1 - co, g1[:2 * LAT], g2[2 * LAT:])
+    for group, same, across in (near, other):
+        even = jnp.where(xh == 0, same, across)
+        odd = jnp.where(xh == 0, across, same)
+        for k in range(3):
+            first = pl.multiple_of(group * 384 + INNER * k, 128)
+            e = even[:, 256 * k:256 * (k + 1)]
+            o = odd[:, 256 * k:256 * (k + 1)]
+            every[:, pl.ds(first, 128)] = e[:, :128]
+            every[:, pl.ds(pl.multiple_of(first + 128, 128), 128)] = e[:, 128:] + o[:, :128]
+            every[:, pl.ds(pl.multiple_of(first + 256, 128), 128)] = o[:, 128:]
+    for c, pair in enumerate(copies):
+        for one in pair:
+            one.wait()
+        rows = slice(256 * c, 256 * (c + 1))
+        block = dot(qw[rows], every[:, :INNER], 1, 1) + dot(kvw[rows], every[:, INNER:], 1, 1)
+        grad[:, rows] = jnp.transpose(block)
     lg = lg_ref[...].reshape(1, D)
     for slot in range(2):
         index, found = slot_image(owner_ref, section, slot)
@@ -276,8 +293,8 @@
 COST = 1000000
 CALLS = dict(
     attn=call(
-        attn_kernel, "attn_part", [bf(256, 256)] * 2 + [bf(2, LAT, D)], [SMEM] + [VMEM] * 4,
-        [pltpu.VMEM((IMGS, LAT, D), BF), pltpu.VMEM((256, 384), BF)],
+        attn_kernel, "attn_part", [jax.ShapeDtypeStruct((256, 256), F32), bf(256, 256), bf(2, LAT, D)], [SMEM] + [VMEM] * 4,
+        [pltpu.VMEM((IMGS, LAT, D), BF), pltpu.VMEM((256, 384), F32)],
         flops=600_000_000, size=3_000_000),
     forward=call(
         forward_kernel, "forward_part",
@@ -287,19 +304,22 @@
         [pltpu.VMEM((3, D, 256), BF), DMA((3,))],
         flops=4_000_000_000, size=12_000_000),
     backward=call(
-        backward_kernel, "backward_part", [bf(IMGS * ROWS, 384)] + [bf(2 * LAT, 768), bf(4 * LAT, 768), bf(2 * LAT, 768)],
+        backward_kernel, "backward_part",
+        [bf(IMGS * ROWS, 384), bf(2 * LAT, 768), bf(4 * LAT, 768), bf(2 * LAT, 768)],
         [SMEM, SMEM] + [VMEM] * 5, [pltpu.VMEM((256, 768), BF)],
         flops=COST, size=1000),
     weight=call(
         weight_kernel, "weight_part", bf(16, 240, 128), [VMEM] * 2,
         [pltpu.VMEM((D, 384), F32), pltpu.VMEM((8, 160, 384), F32)],
         flops=COST, size=1000),
-    first=call(first_sum_kernel, "first_sum", bf(8, 32, 384), [VMEM], [pltpu.VMEM((160, 384), F32)],
+    first=call(first_sum_kernel, "first_sum", bf(8, 64, 128), [VMEM],
+               [pltpu.VMEM((160, 384), F32), pltpu.VMEM((8, 64, 128), F32)],
                size=1_000_000),
     last=call(last_kernel, "last_sum", jax.ShapeDtypeStruct((SHARE, 384), F32), [VMEM], size=300_000),
     latent=call(
         latent_kernel, "latent_part", bf(2, LAT, D), [SMEM, SMEM] + [VMEM] * 3 + [HBM] * 2 + [VMEM] * 5,
-        [pltpu.VMEM((12, D, 256), BF), DMA((12,))],
+        [pltpu.VMEM((D, INNER), BF), pltpu.VMEM((D, 2 * INNER), BF), pltpu.VMEM((2 * LAT, 3 * INNER), BF),
+         pltpu.VMEM((2 * LAT, D), F32), DMA((10,))],
         flops=2_000_000_000, size=9_000_000, limit=52),
 )
 

time: 62.6 us -> 61.9 us (0.989)
  waiting for transfers between devices: 17.9 us -> 17.1 us
    all_to_all x1, waiting for transfers between devices: 2.16 us -> 1.35 us  [per_device(): w = lax.all_to_all(w, 'z', 0, 0, tiled=True)]
where the time goes in v4:
time: 61.9 us; the launch traced here: 60.7 us
  starting transfers between devices  20.1 us (32%)
  Pallas kernels  20.1 us (32%)
  waiting for transfers between devices  17.1 us (28%)
  local copies, waits for them, and re-layouts  2.58 us (4%)
  between operations  0.8 us (1%)
    all_to_all x1, waiting for transfers between devices, per_device(): w = lax.all_to_all(w, ('xh', 'xl', 'y'), 0, 0, tiled=True)  13.1 us
    all_to_all x1, starting transfers between devices, per_device(): w = lax.all_to_all(w, 'z', 0, 0, tiled=True)  8.42 us
    pallas_call x1, Pallas kernels, per_device(): CALLS['latent']  7.56 us
    all_to_all x1, starting transfers between devices, per_device(): w = lax.all_to_all(w, ('xh', 'xl', 'y'), 0, 0, tiled=True)  7.4 us
    ppermute x5, starting transfers between devices, swap(): return lax.ppermute(x, SECTION, pairs)  4.32 us
    pallas_call x1, Pallas kernels, per_device(): CALLS['forward']  4.16 us
    pallas_call x1, Pallas kernels, per_device(): w = CALLS['weight'](ctx, kvg)  3.31 us
    ppermute x5, waiting for transfers between devices, swap(): return lax.ppermute(x, SECTION, pairs)  2.6 us
  transfers between devices with their start and end apart: 7, of which 5 were waited for; matrix products, arithmetic and copies ran while one was open for 4% of the time, Pallas kernels for 30%

profile of v4, /device:TPU:8, one launch (start us, length us, event | category | flops | bytes accessed | tf_op | source)
XLA Modules:
  0.0 60.7 jit_solution(7780212376486795927)
XLA Ops:
  0.6 0.0 copy-start.1
  0.6 0.0 copy-start.2
  0.7 0.0 copy-start.4
  0.7 0.0 copy-start.7
  0.7 0.1 collective-permute-start
  0.8 0.0 copy-start.5
  0.8 0.0 copy-start.6
  0.8 0.0 copy-start.9
  0.8 2.2 %copy.12.feat_ref = bf16[4,257,1280]{2,1,0:T(8,128)(2,1)S(1)} copy(bf16[4,257,1280]{2,0,1:T(4,128)(2,1)} %param.12) | data formatting | bytes 5263360 | tf_op args[2]
  3.0 0.0 copy-start
  3.0 0.0 collective-permute-done.c1_ref.c1
  3.1 0.0 copy-start.3
  3.1 0.0 copy-done.1
  3.1 0.0 copy-done.2
  3.1 0.3 copy-done.4
  3.4 0.0 copy-done.7
  3.4 1.2 %attn_part.1 = (f32[256,256]{1,0:T(8,128)S(1)}, bf16[256,256]{1,0:T(8,128)(2,1)S(1)}, bf16[2,64,1280]{2,1,0:T(8,128)(2,1)S(1)}) custom-call(s32[1,4]{1,0:T(1,128)S(1)} %bitcast.6, bf16[4,64,1280]{2,1,0:T(8,128)(2,1)S(1)} %bitcast.4, bf16[4,64,1280]{2,1,0:T(8,128)(2,1)S(1)} %collective-permute-done.c1_ref.c1, bf16[768,1280]{1,0:T(8,128)(2,1)S(1)} %copy-done.4, ...), custom_call_target="tpu_custom_call" | custom-call | flops 600000000 | bytes 3000000 | tf_op jit(solution)/shard_map/attn_part/pallas_call | solution.py:332
  4.5 3.1 %collective-permute-start.1 = (bf16[256,256]{1,0:T(8,128)(2,1)S(1)}, bf16[256,256]{1,0:T(8,128)(2,1)S(1)}, u32[]{:S(2)}, u32[]{:S(2)}) collective-permute-start(bf16[256,256]{1,0:T(8,128)(2,1)S(1)} %get-tuple-element.21), channel_id=1, source_target_pairs={{0,128},{128,0},{64,192},{192,64},{1,129},{129,1},{65,193},{193,65... | collective-permute-start | bytes 393224 | tf_op jit(solution)/shard_map/ppermute | solution.py:285
  7.7 0.0 copy-start.8
  7.7 0.5 collective-permute-start.2
  8.2 0.0 copy-done.5
  8.2 0.0 copy-done.6
  8.2 0.0 copy-done.9
  8.2 0.0 copy-done
  8.2 4.2 %forward_part.1 = (bf16[4,336,1280]{2,1,0:T(8,128)(2,1)S(1)}, bf16[4,336,512]{2,1,0:T(8,128)(2,1)S(1)}, bf16[4,128,256]{2,1,0:T(8,128)(2,1)S(1)}, f32[4,128,336]{2,1,0:T(8,128)S(1)}) custom-call(bf16[4,257,1280]{2,1,0:T(8,128)(2,1)S(1)} %copy.12.feat_ref, bf16[4,64,1280]{2,1,0:T(8,128)(2,1)S(1)} %copy-done.2, f32[1280]{0:T(1024)S(1)} %copy-done.9, ...), custom_call_target="tpu_custom_call" | custom-call | flops 4000000000 | bytes 12000000 | tf_op jit(solution)/shard_map/forward_part/pallas_call | solution.py:335
  12.3 0.0 copy-done.3
  12.4 0.0 collective-permute-done.1.a2
  12.4 0.0 copy-done.8
  12.4 2.4 %backward_part.1 = (bf16[1344,384]{1,0:T(8,128)(2,1)S(1)}, bf16[128,768]{1,0:T(8,128)(2,1)S(1)}, bf16[256,768]{1,0:T(8,128)(2,1)S(1)}, bf16[128,768]{1,0:T(8,128)(2,1)S(1)}) custom-call(s32[1,4]{1,0:T(1,128)S(1)} %bitcast.7, s32[1,4]{1,0:T(1,128)S(1)} %copy-done.8, f32[256,256]{1,0:T(8,128)S(1)} %get-tuple-element.20.a0, ...), custom_call_target="tpu_custom_call" | custom-call | flops 1000000 | bytes 1000 | tf_op jit(solution)/shard_map/backward_part/pallas_call | solution.py:337
  14.8 3.3 %weight_part.1 = bf16[16,240,128]{2,1,0:T(8,128)(2,1)} custom-call(bf16[4,336,1280]{2,1,0:T(8,128)(2,1)S(1)} %get-tuple-element.19.ctx_ref, bf16[1344,384]{1,0:T(8,128)(2,1)S(1)} %get-tuple-element.25.kvg), custom_call_target="tpu_custom_call" | custom-call | flops 1000000 | bytes 1000 | tf_op jit(solution)/shard_map/weight_part/pallas_call | solution.py:340
  18.1 0.7 %collective-permute-done.2.u2 = bf16[2,64,1280]{2,1,0:T(8,128)(2,1)S(1)} collective-permute-done((bf16[2,64,1280]{2,1,0:T(8,128)(2,1)S(1)}, bf16[2,64,1280]{2,1,0:T(8,128)(2,1)S(1)}, u32[]{:S(2)}, u32[]{:S(2)}) %collective-permute-start.2) | collective-permute-done | bytes 327712 | tf_op jit(solution)/shard_map/ppermute | solution.py:285
  18.8 7.4 %all-to-all-start = ((bf16[16,240,128]{2,1,0:T(8,128)(2,1)}), bf16[16,240,128]{2,1,0:T(8,128)(2,1)S(1)}, u32[]{:S(2)}, u32[]{:S(2)}) async-start(bf16[16,240,128]{2,1,0:T(8,128)(2,1)} %weight_part.1), calls=%async_computation | async-start | bytes 1966080 | tf_op jit(solution)/shard_map/all_to_all | solution.py:342
  26.2 0.0 collective-permute-start.3
  26.2 1.7 %collective-permute-done.3.g1 = bf16[256,768]{1,0:T(8,128)(2,1)S(1)} collective-permute-done((bf16[256,768]{1,0:T(8,128)(2,1)S(1)}, bf16[256,768]{1,0:T(8,128)(2,1)S(1)}, u32[]{:S(2)}, u32[]{:S(2)}) %collective-permute-start.3) | collective-permute-done | bytes 393248 | tf_op jit(solution)/shard_map/ppermute | solution.py:285
  28.0 13.1 %all-to-all-done.r_ref = bf16[16,240,128]{2,1,0:T(8,128)(2,1)S(1)} async-done(((bf16[16,240,128]{2,1,0:T(8,128)(2,1)}), bf16[16,240,128]{2,1,0:T(8,128)(2,1)S(1)}, u32[]{:S(2)}, u32[]{:S(2)}) %all-to-all-start) | async-done | bytes 983072 | tf_op jit(solution)/shard_map/all_to_all | solution.py:342
  41.1 0.6 collective-permute-start.4
  41.7 0.8 %first_sum.1 = bf16[8,64,128]{2,1,0:T(8,128)(2,1)} custom-call(bf16[16,240,128]{2,1,0:T(8,128)(2,1)S(1)} %all-to-all-done.r_ref), custom_call_target="tpu_custom_call" | custom-call | bytes 1000000 | tf_op jit(solution)/shard_map/first_sum/pallas_call | solution.py:345
  42.6 8.4 %all-to-all-start.1 = ((bf16[8,64,128]{2,1,0:T(8,128)(2,1)}), bf16[8,64,128]{2,1,0:T(8,128)(2,1)S(1)}, u32[]{:S(2)}, u32[]{:S(2)}) async-start(bf16[8,64,128]{2,1,0:T(8,128)(2,1)} %first_sum.1), calls=%async_computation.1 | async-start | bytes 262144 | tf_op jit(solution)/shard_map/all_to_all | solution.py:348
  51.0 0.2 collective-permute-done.4.g2
  51.2 7.6 %latent_part.1 = bf16[2,64,1280]{2,1,0:T(8,128)(2,1)} custom-call(s32[1,4]{1,0:T(1,128)S(1)} %bitcast.8, s32[1,4]{1,0:T(1,128)S(1)} %copy-done.8, bf16[4,64,1280]{2,1,0:T(8,128)(2,1)S(1)} %bitcast.5, bf16[4,64,1280]{2,1,0:T(8,128)(2,1)} %lat_ref.5, f32[1280]{0:T(1024)S(1)} %copy-done.6, bf16[1280,768]{1,0:T(8,128)(2,1)} %qw_hbm.3, ...), custom_call_target="tpu_custom_call" | custom-call | flops 2000000000 | bytes 9000000 | tf_op jit(solution)/shard_map/latent_part/pallas_call | solution.py:346
  58.7 1.4 %all-to-all-done.1.r_ref = bf16[8,64,128]{2,1,0:T(8,128)(2,1)S(1)} async-done(((bf16[8,64,128]{2,1,0:T(8,128)(2,1)}), bf16[8,64,128]{2,1,0:T(8,128)(2,1)S(1)}, u32[]{:S(2)}, u32[]{:S(2)}) %all-to-all-start.1) | async-done | bytes 131104 | tf_op jit(solution)/shard_map/all_to_all | solution.py:348
  60.1 0.6 %last_sum.1 = f32[20,384]{1,0:T(8,128)} custom-call(bf16[8,64,128]{2,1,0:T(8,128)(2,1)S(1)} %all-to-all-done.1.r_ref), custom_call_target="tpu_custom_call" | custom-call | bytes 300000 | tf_op jit(solution)/shard_map/last_sum/pallas_call | solution.py:350
  (2 shorter events, 0.0 us)
Async XLA Ops:
  0.6 2.4 %copy-start.1 = (bf16[1,4,64,1280]{3,2,1,0:T(8,128)(2,1)S(1)}, bf16[1,4,64,1280]{3,2,1,0:T(8,128)(2,1)}, u32[]{:S(2)}) copy-start(bf16[1,4,64,1280]{3,2,1,0:T(8,128)(2,1)} %param.10) | copy-start | bytes 1966084
  0.6 2.4 %copy-start.2 = (bf16[4,64,1280]{2,1,0:T(8,128)(2,1)S(1)}, bf16[4,64,1280]{2,1,0:T(8,128)(2,1)}, u32[]{:S(2)}) copy-start(bf16[4,64,1280]{2,1,0:T(8,128)(2,1)} %lat_ref.5) | copy-start | bytes 1966084
  0.7 2.7 %copy-start.4 = (bf16[768,1280]{1,0:T(8,128)(2,1)S(1)}, bf16[768,1280]{1,0:T(8,128)(2,1)}, u32[]{:S(2)}) copy-start(bf16[768,1280]{1,0:T(8,128)(2,1)} %ow_ref.1) | copy-start | bytes 5898244
  0.7 2.7 %copy-start.7 = (s32[4,1]{0,1:T(1,128)S(1)}, s32[4,1]{0,1:T(1,128)}, u32[]{:S(2)}) copy-start(s32[4,1]{0,1:T(1,128)} %param.19) | copy-start | bytes 52
  0.7 2.4 %collective-permute-start = (bf16[4,64,1280]{2,1,0:T(8,128)(2,1)}, bf16[4,64,1280]{2,1,0:T(8,128)(2,1)S(1)}, u32[]{:S(2)}, u32[]{:S(2)}) collective-permute-start(bf16[4,64,1280]{2,1,0:T(8,128)(2,1)} %bitcast.3), channel_id=1, source_target_pairs={{0,64},{64,0},{128,192},{192,128},{1,65},{65,1},{129,193},{193,129... | collective-permute-start | bytes 1966088 | tf_op jit(solution)/shard_map/ppermute | solution.py:285
  0.8 7.4 %copy-start.5 = (bf16[1280,768]{1,0:T(8,128)(2,1)S(1)}, bf16[1280,768]{1,0:T(8,128)(2,1)}, u32[]{:S(2)}) copy-start(bf16[1280,768]{1,0:T(8,128)(2,1)} %qw_hbm.3) | copy-start | bytes 5898244
  0.8 7.4 %copy-start.6 = (f32[1280]{0:T(1024)S(1)}, f32[1280]{0:T(1024)}, u32[]{:S(2)}) copy-start(f32[1280]{0:T(1024)} %lg_ref.3) | copy-start | bytes 15364
  0.8 7.4 %copy-start.9 = (f32[1280]{0:T(1024)S(1)}, f32[1280]{0:T(1024)}, u32[]{:S(2)}) copy-start(f32[1280]{0:T(1024)} %fg_ref.1) | copy-start | bytes 15364
  3.0 5.1 %copy-start = (bf16[1280,1536]{1,0:T(8,128)(2,1)S(1)}, bf16[1280,1536]{1,0:T(8,128)(2,1)}, u32[]{:S(2)}) copy-start(bf16[1280,1536]{1,0:T(8,128)(2,1)} %kvw_hbm.3) | copy-start | bytes 11796484
  3.1 9.3 %copy-start.3 = (bf16[4,64,1280]{2,1,0:T(8,128)(2,1)}, bf16[4,64,1280]{2,1,0:T(8,128)(2,1)S(1)}, u32[]{:S(2)}) copy-start(bf16[4,64,1280]{2,1,0:T(8,128)(2,1)S(1)} %collective-permute-done.c1_ref.c1) | copy-start | bytes 1966084
  4.5 7.8 %collective-permute-start.1 = (bf16[256,256]{1,0:T(8,128)(2,1)S(1)}, bf16[256,256]{1,0:T(8,128)(2,1)S(1)}, u32[]{:S(2)}, u32[]{:S(2)}) collective-permute-start(bf16[256,256]{1,0:T(8,128)(2,1)S(1)} %get-tuple-element.21), channel_id=1, source_target_pairs={{0,128},{128,0},{64,192},{192,64},{1,129},{129,1},{65,193},{193,65... | collective-permute-start | bytes 393224 | tf_op jit(solution)/shard_map/ppermute | solution.py:285
  7.7 4.7 %copy-start.8 = (s32[1,4]{1,0:T(1,128)S(1)}, s32[1,4]{1,0:T(1,128)}, u32[]{:S(2)}) copy-start(s32[1,4]{1,0:T(1,128)} %sample_ref.3) | copy-start | bytes 52
  7.7 11.2 %collective-permute-start.2 = (bf16[2,64,1280]{2,1,0:T(8,128)(2,1)S(1)}, bf16[2,64,1280]{2,1,0:T(8,128)(2,1)S(1)}, u32[]{:S(2)}, u32[]{:S(2)}) collective-permute-start(bf16[2,64,1280]{2,1,0:T(8,128)(2,1)S(1)} %get-tuple-element.26), channel_id=1, source_target_pairs={{0,128},{128,0},{64,192},{192,64},{1,129},{129,1},{65,193},{193,65... | collective-permute-start | bytes 983048 | tf_op jit(solution)/shard_map/ppermute | solution.py:285
  18.8 22.3 %all-to-all-start = ((bf16[16,240,128]{2,1,0:T(8,128)(2,1)}), bf16[16,240,128]{2,1,0:T(8,128)(2,1)S(1)}, u32[]{:S(2)}, u32[]{:S(2)}) async-start(bf16[16,240,128]{2,1,0:T(8,128)(2,1)} %weight_part.1), calls=%async_computation | async-start | bytes 1966080 | tf_op jit(solution)/shard_map/all_to_all | solution.py:342
  26.2 1.7 %collective-permute-start.3 = (bf16[256,768]{1,0:T(8,128)(2,1)S(1)}, bf16[256,768]{1,0:T(8,128)(2,1)S(1)}, u32[]{:S(2)}, u32[]{:S(2)}) collective-permute-start(bf16[256,768]{1,0:T(8,128)(2,1)S(1)} %get-tuple-element.29), channel_id=1, source_target_pairs={{0,64},{64,0},{128,192},{192,128},{1,65},{65,1},{129,193},{193,129... | collective-permute-start | bytes 1179656 | tf_op jit(solution)/shard_map/ppermute | solution.py:285
  41.1 10.0 %collective-permute-start.4 = (bf16[256,768]{1,0:T(8,128)(2,1)S(1)}, bf16[256,768]{1,0:T(8,128)(2,1)S(1)}, u32[]{:S(2)}, u32[]{:S(2)}) collective-permute-start(bf16[256,768]{1,0:T(8,128)(2,1)S(1)} %pad_maximum_fusion), channel_id=1, source_target_pairs={{0,128},{128,0},{64,192},{192,64},{1,129},{129,1},{65,193},{193,65... | collective-permute-start | bytes 1179656 | tf_op jit(solution)/shard_map/ppermute | solution.py:285
  42.6 17.5 %all-to-all-start.1 = ((bf16[8,64,128]{2,1,0:T(8,128)(2,1)}), bf16[8,64,128]{2,1,0:T(8,128)(2,1)S(1)}, u32[]{:S(2)}, u32[]{:S(2)}) async-start(bf16[8,64,128]{2,1,0:T(8,128)(2,1)} %first_sum.1), calls=%async_computation.1 | async-start | bytes 262144 | tf_op jit(solution)/shard_map/all_to_all | solution.py:348

commit v5 on v4

--- a/solution.py
+++ b/solution.py
@@ -215,47 +215,57 @@
         out_ref[:, 128 * k:128 * (k + 1)] = total[SHARE * k:SHARE * (k + 1)]
 
 
-def latent_kernel(owner_ref, sample_ref, part_ref, lat_ref, lg_ref, qw_hbm, kvw_hbm,
-                  c1, u2, g0, g1, g2, out_ref, qw, kvw, every, grad, sems):
+def near_kernel(owner_ref, part_ref, lat_ref, qw_hbm, kvw_hbm, c1, g0, g1,
+                acc_ref, up_ref, hat_ref, inv_ref, far_ref, win, sems):
     xh = lax.axis_index("xh")
     co = lax.axis_index("co")
-    section = xh * 2 + co
     copies = []
+    for dx, place in ((0, win), (1, far_ref)):
+        for dc in range(2):
+            start = pl.multiple_of(window_of(pair_of(xh ^ dx, co ^ dc)), 128)
+            further = pl.multiple_of(start + INNER, 128)
+            for k, (source, lane) in enumerate(((qw_hbm, start), (kvw_hbm, start), (kvw_hbm, further))):
+                copies.append(pltpu.make_async_copy(
+                    source.at[:, pl.ds(lane, 256)], place.at[3 * dc + k], sems.at[len(copies)]))
+    for c in copies:
+        c.start()
+    for slot in range(2):
+        rows = slice(LAT * slot, LAT * (slot + 1))
+        index, _ = slot_image(owner_ref, xh * 2 + co, slot)
+        up_ref[rows] = part_ref[index].astype(F32) + c1[index].astype(F32)
+        hat, inverse = layer_stats(lat_ref[index].astype(F32))
+        hat_ref[rows] = hat
+        inv_ref[rows] = jnp.broadcast_to(inverse, (LAT, 128))
+    total = jnp.zeros((D, 2 * LAT), F32)
+    for n in range(6):
+        copies[n].wait()
+        lanes = slice(256 * (n % 3), 256 * (n % 3 + 1))
+        total = total + dot(win[n], (g0, g1)[n // 3][:2 * LAT, lanes], 1, 1)
+    acc_ref[...] = total
+    for c in copies[6:]:
+        c.wait()
+
+
+def latent_kernel(owner_ref, sample_ref, lg_ref, acc_ref, up_ref, hat_ref, inv_ref, far_ref, u2, g2, out_ref, grad):
+    section = lax.axis_index("xh") * 2 + lax.axis_index("co")
     for c in range(5):
-        rows = pl.ds(256 * c, 256)
-        copies.append((pltpu.make_async_copy(qw_hbm.at[rows], qw.at[rows], sems.at[2 * c]),
-                       pltpu.make_async_copy(kvw_hbm.at[rows], kvw.at[rows], sems.at[2 * c + 1])))
-    for pair in copies:
-        for c in pair:
-            c.start()
-    near = (co, g0[...], g2[:2 * LAT])
-    other = (1 - co, g1[:2 * LAT], g2[2 * LAT:])
-    for group, same, across in (near, other):
-        even = jnp.where(xh == 0, same, across)
-        odd = jnp.where(xh == 0, across, same)
-        for k in range(3):
-            first = pl.multiple_of(group * 384 + INNER * k, 128)
-            e = even[:, 256 * k:256 * (k + 1)]
-            o = odd[:, 256 * k:256 * (k + 1)]
-            every[:, pl.ds(first, 128)] = e[:, :128]
-            every[:, pl.ds(pl.multiple_of(first + 128, 128), 128)] = e[:, 128:] + o[:, :128]
-            every[:, pl.ds(pl.multiple_of(first + 256, 128), 128)] = o[:, 128:]
-    for c, pair in enumerate(copies):
-        for one in pair:
-            one.wait()
         rows = slice(256 * c, 256 * (c + 1))
-        block = dot(qw[rows], every[:, :INNER], 1, 1) + dot(kvw[rows], every[:, INNER:], 1, 1)
+        block = acc_ref[rows]
+        for n in range(6):
+            first = 2 * LAT * (n // 3)
+            block = block + dot(
+                far_ref[n, rows], g2[first:first + 2 * LAT, 256 * (n % 3):256 * (n % 3 + 1)], 1, 1)
         grad[:, rows] = jnp.transpose(block)
     lg = lg_ref[...].reshape(1, D)
     for slot in range(2):
+        rows = slice(LAT * slot, LAT * (slot + 1))
         index, found = slot_image(owner_ref, section, slot)
         count = scale_of(sample_ref, index).astype(F32)
-        summed = (part_ref[index].astype(F32) + c1[index].astype(F32)) + u2[slot].astype(F32)
-        upstream = (summed / count).astype(BF).astype(F32)
-        hat, inverse = layer_stats(lat_ref[index].astype(F32))
-        dy = grad[LAT * slot:LAT * (slot + 1)] * lg
+        upstream = ((up_ref[rows] + u2[slot].astype(F32)) / count).astype(BF).astype(F32)
+        hat = hat_ref[rows]
+        dy = grad[rows] * lg
         centred = dy - jnp.mean(dy, axis=-1, keepdims=True) - hat * jnp.mean(dy * hat, axis=-1, keepdims=True)
-        out = (upstream + inverse * centred).astype(BF)
+        out = (upstream + inv_ref[rows, :1] * centred).astype(BF)
         out_ref[slot] = jnp.where(found == 1, out, jnp.zeros_like(out))
 
 
@@ -287,6 +297,10 @@
 
 def bf(*shape):
     return jax.ShapeDtypeStruct(shape, BF)
+
+
+def wide(*shape):
+    return jax.ShapeDtypeStruct(shape, F32)
 
 
 DMA = pltpu.SemaphoreType.DMA
@@ -316,11 +330,16 @@
                [pltpu.VMEM((160, 384), F32), pltpu.VMEM((8, 64, 128), F32)],
                size=1_000_000),
     last=call(last_kernel, "last_sum", jax.ShapeDtypeStruct((SHARE, 384), F32), [VMEM], size=300_000),
+    near=call(
+        near_kernel, "near_part", [wide(D, 2 * LAT), wide(2 * LAT, D), wide(2 * LAT, D), wide(2 * LAT, 128),
+                                   bf(6, D, 256)],
+        [SMEM] + [VMEM] * 2 + [HBM] * 2 + [VMEM] * 3,
+        [pltpu.VMEM((6, D, 256), BF), DMA((12,))],
+        flops=COST, size=1000, limit=60),
     latent=call(
-        latent_kernel, "latent_part", bf(2, LAT, D), [SMEM, SMEM] + [VMEM] * 3 + [HBM] * 2 + [VMEM] * 5,
-        [pltpu.VMEM((D, INNER), BF), pltpu.VMEM((D, 2 * INNER), BF), pltpu.VMEM((2 * LAT, 3 * INNER), BF),
-         pltpu.VMEM((2 * LAT, D), F32), DMA((10,))],
-        flops=2_000_000_000, size=9_000_000, limit=52),
+        latent_kernel, "latent_part", bf(2, LAT, D), [SMEM, SMEM] + [VMEM] * 8,
+        [pltpu.VMEM((2 * LAT, D), F32)],
+        flops=2_000_000_000, size=9_000_000, limit=60),
 )
 
 
@@ -340,11 +359,12 @@
     w = CALLS["weight"](ctx, kvg)
     w, u = lax.optimization_barrier((w, u))
     w = lax.all_to_all(w, ("xh", "xl", "y"), 0, 0, tiled=True)
-    w, g2 = lax.optimization_barrier((w, g2))
+    near = CALLS["near"](owner, part, latents, query_weight, kv_weight, c1, g0, g1)
+    g2, near = lax.optimization_barrier((g2, near))
+    w, near = lax.optimization_barrier((w, near))
     g2 = swap(g2, FAR)
     w = CALLS["first"](w)
-    latent_grad = CALLS["latent"](
-        owner, sample_of, part, latents, latent_gain, query_weight, kv_weight, c1, u, g0, g1, g2)
+    latent_grad = CALLS["latent"](owner, sample_of, latent_gain, *near, u, g2)
     w = lax.all_to_all(w, "z", 0, 0, tiled=True)
     w, latent_grad = lax.optimization_barrier((w, latent_grad))
     kv_grad = CALLS["last"](w)

time: 61.9 us -> 60.3 us (0.974); the launches traced: 60.7 us -> 60.1 us
  waiting for transfers between devices: 17.1 us -> 6.35 us
  Pallas kernels: 20.1 us -> 26.2 us
  starting transfers between devices: 20.1 us -> 22.6 us
  local copies, waits for them, and re-layouts: 2.58 us -> 4.09 us
    all_to_all x1, waiting for transfers between devices: 13.1 us -> 0.91 us  [per_device(): w = lax.all_to_all(w, ('xh', 'xl', 'y'), 0, 0, tiled=True)]
    pallas_call x1 -> x2, Pallas kernels: 7.56 us -> 13.5 us  [the longest x1 8.34 us: per_device(): CALLS['near'](owner, part, latents, query_weight, kv_weight, c1, g0, g1)]
    ppermute x5, starting transfers between devices: 4.32 us -> 6.78 us  [swap(): return lax.ppermute(x, SECTION, pairs)]
    all_to_all x1, waiting for transfers between devices: 1.35 us -> 3.15 us  [per_device(): w = lax.all_to_all(w, 'z', 0, 0, tiled=True)]
    unnamed x21 -> x29, local copies, waits for them, and re-layouts: 2.57 us -> 4.08 us
  transfers between devices with their start and end apart: 7 -> 7, of which waited for: 5 -> 4; matrix products, arithmetic and copies ran while one was open for 4% -> 4% of each run, Pallas kernels for 30% -> 41%
where the time goes in v5:
time: 60.3 us; the launch traced here: 60.1 us
  Pallas kernels  26.2 us (43%)
  starting transfers between devices  22.6 us (37%)
  waiting for transfers between devices  6.35 us (11%)
  local copies, waits for them, and re-layouts  4.09 us (7%)
  between operations  0.84 us (1%)
    all_to_all x1, starting transfers between devices, per_device(): w = lax.all_to_all(w, 'z', 0, 0, tiled=True)  8.43 us
    pallas_call x1, Pallas kernels, per_device(): CALLS['near'](owner, part, latents, query_weight, kv_weight, c1, g0, g1)  8.34 us
    all_to_all x1, starting transfers between devices, per_device(): w = lax.all_to_all(w, ('xh', 'xl', 'y'), 0, 0, tiled=True)  7.38 us
    ppermute x5, starting transfers between devices, swap(): return lax.ppermute(x, SECTION, pairs)  6.78 us
    pallas_call x1, Pallas kernels, per_device(): latent_grad = CALLS['latent'](owner, sample_of, latent_gain, *near, u, g2)  5.17 us
    pallas_call x1, Pallas kernels, per_device(): CALLS['forward']  4.17 us
    unnamed x29, local copies, waits for them, and re-layouts  4.08 us
    pallas_call x1, Pallas kernels, per_device(): w = CALLS['weight'](ctx, kvg)  3.38 us
  transfers between devices with their start and end apart: 7, of which 4 were waited for; matrix products, arithmetic and copies ran while one was open for 4% of the time, Pallas kernels for 41%

profile of v5, /device:TPU:8, one launch (start us, length us, event | category | flops | bytes accessed | tf_op | source)
XLA Modules:
  0.0 60.1 jit_solution(12612446904691078664)
XLA Ops:
  0.6 0.0 copy-start.1
  0.6 0.0 copy-start.2
  0.7 0.0 copy-start.7
  0.7 0.0 copy-start.4
  0.7 0.1 collective-permute-start
  0.8 0.0 copy-start.5
  0.8 0.0 copy-start.9
  0.8 0.0 copy-start.10
  0.8 2.2 %copy.12.feat_ref = bf16[4,257,1280]{2,1,0:T(8,128)(2,1)S(1)} copy(bf16[4,257,1280]{2,0,1:T(4,128)(2,1)} %param.12) | data formatting | bytes 5263360 | tf_op args[2]
  3.0 0.0 copy-start
  3.1 0.0 collective-permute-done.c1_ref.c1
  3.1 0.0 copy-start.3
  3.1 0.0 copy-done.1
  3.1 0.0 copy-done.2
  3.1 0.0 copy-done.7
  3.1 0.3 copy-done.4
  3.4 1.2 %attn_part.1 = (f32[256,256]{1,0:T(8,128)S(1)}, bf16[256,256]{1,0:T(8,128)(2,1)S(1)}, bf16[2,64,1280]{2,1,0:T(8,128)(2,1)S(1)}) custom-call(s32[1,4]{1,0:T(1,128)S(1)} %bitcast.8, bf16[4,64,1280]{2,1,0:T(8,128)(2,1)S(1)} %bitcast.5, bf16[4,64,1280]{2,1,0:T(8,128)(2,1)S(1)} %collective-permute-done.c1_ref.c1, bf16[768,1280]{1,0:T(8,128)(2,1)S(1)} %copy-done.4, ...), custom_call_target="tpu_custom_call" | custom-call | flops 600000000 | bytes 3000000 | tf_op jit(solution)/shard_map/attn_part/pallas_call | solution.py:351
  4.6 3.1 %collective-permute-start.1 = (bf16[256,256]{1,0:T(8,128)(2,1)S(1)}, bf16[256,256]{1,0:T(8,128)(2,1)S(1)}, u32[]{:S(2)}, u32[]{:S(2)}) collective-permute-start(bf16[256,256]{1,0:T(8,128)(2,1)S(1)} %get-tuple-element.36), channel_id=1, source_target_pairs={{0,128},{128,0},{64,192},{192,64},{1,129},{129,1},{65,193},{193,65... | collective-permute-start | bytes 393224 | tf_op jit(solution)/shard_map/ppermute | solution.py:295
  7.7 0.0 copy-start.8
  7.7 0.5 collective-permute-start.2
  8.2 0.0 copy-done.5
  8.2 0.0 copy-done.9
  8.2 0.0 copy-done.10
  8.2 0.0 copy-done
  8.2 4.2 %forward_part.1 = (bf16[4,336,1280]{2,1,0:T(8,128)(2,1)S(1)}, bf16[4,336,512]{2,1,0:T(8,128)(2,1)S(1)}, bf16[4,128,256]{2,1,0:T(8,128)(2,1)S(1)}, f32[4,128,336]{2,1,0:T(8,128)S(1)}) custom-call(bf16[4,257,1280]{2,1,0:T(8,128)(2,1)S(1)} %copy.12.feat_ref, bf16[4,64,1280]{2,1,0:T(8,128)(2,1)S(1)} %copy-done.2, f32[1280]{0:T(1024)S(1)} %copy-done.9, ...), custom_call_target="tpu_custom_call" | custom-call | flops 4000000000 | bytes 12000000 | tf_op jit(solution)/shard_map/forward_part/pallas_call | solution.py:354
  12.4 0.0 copy-done.3
  12.4 0.0 collective-permute-done.1.a2
  12.4 0.0 copy-done.8
  12.4 2.5 %backward_part.1 = (bf16[1344,384]{1,0:T(8,128)(2,1)S(1)}, bf16[128,768]{1,0:T(8,128)(2,1)S(1)}, bf16[256,768]{1,0:T(8,128)(2,1)S(1)}, bf16[128,768]{1,0:T(8,128)(2,1)S(1)}) custom-call(s32[1,4]{1,0:T(1,128)S(1)} %bitcast.9, s32[1,4]{1,0:T(1,128)S(1)} %copy-done.8, f32[256,256]{1,0:T(8,128)S(1)} %get-tuple-element.35.a0, ...), custom_call_target="tpu_custom_call" | custom-call | flops 1000000 | bytes 1000 | tf_op jit(solution)/shard_map/backward_part/pallas_call | solution.py:356
  14.9 0.0 copy-start.6
  14.9 3.4 %weight_part.1 = bf16[16,240,128]{2,1,0:T(8,128)(2,1)} custom-call(bf16[4,336,1280]{2,1,0:T(8,128)(2,1)S(1)} %get-tuple-element.34.ctx_ref, bf16[1344,384]{1,0:T(8,128)(2,1)S(1)} %get-tuple-element.40.kvg), custom_call_target="tpu_custom_call" | custom-call | flops 1000000 | bytes 1000 | tf_op jit(solution)/shard_map/weight_part/pallas_call | solution.py:359
  18.3 0.0 copy-done.6
  18.3 0.6 collective-permute-done.2.u2
  18.8 0.0 copy-start.13
  18.8 7.4 %all-to-all-start = ((bf16[16,240,128]{2,1,0:T(8,128)(2,1)}), bf16[16,240,128]{2,1,0:T(8,128)(2,1)S(1)}, u32[]{:S(2)}, u32[]{:S(2)}) async-start(bf16[16,240,128]{2,1,0:T(8,128)(2,1)} %weight_part.1), calls=%async_computation | async-start | bytes 1966080 | tf_op jit(solution)/shard_map/all_to_all | solution.py:361
  26.2 0.0 collective-permute-start.3
  26.2 1.7 %collective-permute-done.3.g1 = bf16[256,768]{1,0:T(8,128)(2,1)S(1)} collective-permute-done((bf16[256,768]{1,0:T(8,128)(2,1)S(1)}, bf16[256,768]{1,0:T(8,128)(2,1)S(1)}, u32[]{:S(2)}, u32[]{:S(2)}) %collective-permute-start.3) | collective-permute-done | bytes 393248 | tf_op jit(solution)/shard_map/ppermute | solution.py:295
  27.9 0.0 copy-start.11
  28.0 0.7 %copy-done.11 = bf16[256,768]{1,0:T(8,128)(2,1)} copy-done((bf16[256,768]{1,0:T(8,128)(2,1)}, bf16[256,768]{1,0:T(8,128)(2,1)S(1)}, u32[]{:S(2)}) %copy-start.11) | copy-done | bytes 393240
  28.7 8.3 %near_part.1 = (f32[1280,128]{1,0:T(8,128)}, f32[128,1280]{1,0:T(8,128)}, f32[128,1280]{1,0:T(8,128)}, f32[128,128]{1,0:T(8,128)}, bf16[6,1280,256]{2,1,0:T(8,128)(2,1)}) custom-call(s32[1,4]{1,0:T(1,128)} %bitcast.6, bf16[4,64,1280]{2,1,0:T(8,128)(2,1)} %bitcast.4, bf16[4,64,1280]{2,1,0:T(8,128)(2,1)} %lat_ref.5, bf16[1280,768]{1,0:T(8,128)(2,1)} %qw_hbm.3, ...), custom_call_target="tpu_custom_call" | custom-call | flops 1000000 | bytes 1000 | tf_op jit(solution)/shard_map/near_part/pallas_call | solution.py:362
  37.0 0.0 copy-done.13
  37.1 3.1 %collective-permute-start.4 = (bf16[256,768]{1,0:T(8,128)(2,1)S(1)}, bf16[256,768]{1,0:T(8,128)(2,1)S(1)}, u32[]{:S(2)}, u32[]{:S(2)}) collective-permute-start(bf16[256,768]{1,0:T(8,128)(2,1)S(1)} %pad_maximum_fusion), channel_id=1, source_target_pairs={{0,128},{128,0},{64,192},{192,64},{1,129},{129,1},{65,193},{193,65... | collective-permute-start | bytes 1179656 | tf_op jit(solution)/shard_map/ppermute | solution.py:295
  40.2 0.9 %all-to-all-done.r_ref = bf16[16,240,128]{2,1,0:T(8,128)(2,1)S(1)} async-done(((bf16[16,240,128]{2,1,0:T(8,128)(2,1)}), bf16[16,240,128]{2,1,0:T(8,128)(2,1)S(1)}, u32[]{:S(2)}, u32[]{:S(2)}) %all-to-all-start) | async-done | bytes 983072 | tf_op jit(solution)/shard_map/all_to_all | solution.py:361
  41.1 0.8 %first_sum.1 = bf16[8,64,128]{2,1,0:T(8,128)(2,1)} custom-call(bf16[16,240,128]{2,1,0:T(8,128)(2,1)S(1)} %all-to-all-done.r_ref), custom_call_target="tpu_custom_call" | custom-call | bytes 1000000 | tf_op jit(solution)/shard_map/first_sum/pallas_call | solution.py:366
  41.9 8.4 %all-to-all-start.1 = ((bf16[8,64,128]{2,1,0:T(8,128)(2,1)}), bf16[8,64,128]{2,1,0:T(8,128)(2,1)S(1)}, u32[]{:S(2)}, u32[]{:S(2)}) async-start(bf16[8,64,128]{2,1,0:T(8,128)(2,1)} %first_sum.1), calls=%async_computation.1 | async-start | bytes 262144 | tf_op jit(solution)/shard_map/all_to_all | solution.py:368
  50.3 0.0 collective-permute-done.4.g2
  50.3 0.0 copy-start.12
  50.4 0.7 %copy-done.12 = bf16[256,768]{1,0:T(8,128)(2,1)} copy-done((bf16[256,768]{1,0:T(8,128)(2,1)}, bf16[256,768]{1,0:T(8,128)(2,1)S(1)}, u32[]{:S(2)}) %copy-start.12) | copy-done | bytes 393240
  51.1 5.2 %latent_part.1 = bf16[2,64,1280]{2,1,0:T(8,128)(2,1)} custom-call(s32[1,4]{1,0:T(1,128)} %bitcast.7, s32[1,4]{1,0:T(1,128)} %sample_ref.3, f32[1280]{0:T(1024)} %lg_ref.3, f32[1280,128]{1,0:T(8,128)} %get-tuple-element.57.acc_ref, f32[128,1280]{1,0:T(8,128)} %get-tuple-element.58.up_ref, f32[128,1280]{1,0:T(8,128)} %get-tuple-element.59.hat_ref, ...), custom_call_target="tpu_custom_call" | custom-call | flops 2000000000 | bytes 9000000 | tf_op jit(solution)/shard_map/latent_part/pallas_call | solution.py:367
  56.3 3.2 %all-to-all-done.1.r_ref = bf16[8,64,128]{2,1,0:T(8,128)(2,1)S(1)} async-done(((bf16[8,64,128]{2,1,0:T(8,128)(2,1)}), bf16[8,64,128]{2,1,0:T(8,128)(2,1)S(1)}, u32[]{:S(2)}, u32[]{:S(2)}) %all-to-all-start.1) | async-done | bytes 131104 | tf_op jit(solution)/shard_map/all_to_all | solution.py:368
  59.4 0.6 %last_sum.1 = f32[20,384]{1,0:T(8,128)} custom-call(bf16[8,64,128]{2,1,0:T(8,128)(2,1)S(1)} %all-to-all-done.1.r_ref), custom_call_target="tpu_custom_call" | custom-call | bytes 300000 | tf_op jit(solution)/shard_map/last_sum/pallas_call | solution.py:370
  (2 shorter events, 0.0 us)
Async XLA Ops:
  0.6 2.5 %copy-start.1 = (bf16[1,4,64,1280]{3,2,1,0:T(8,128)(2,1)S(1)}, bf16[1,4,64,1280]{3,2,1,0:T(8,128)(2,1)}, u32[]{:S(2)}) copy-start(bf16[1,4,64,1280]{3,2,1,0:T(8,128)(2,1)} %param.10) | copy-start | bytes 1966084
  0.6 2.4 %copy-start.2 = (bf16[4,64,1280]{2,1,0:T(8,128)(2,1)S(1)}, bf16[4,64,1280]{2,1,0:T(8,128)(2,1)}, u32[]{:S(2)}) copy-start(bf16[4,64,1280]{2,1,0:T(8,128)(2,1)} %lat_ref.5) | copy-start | bytes 1966084
  0.7 2.4 %copy-start.7 = (s32[4,1]{0,1:T(1,128)S(1)}, s32[4,1]{0,1:T(1,128)}, u32[]{:S(2)}) copy-start(s32[4,1]{0,1:T(1,128)} %param.19) | copy-start | bytes 52
  0.7 2.7 %copy-start.4 = (bf16[768,1280]{1,0:T(8,128)(2,1)S(1)}, bf16[768,1280]{1,0:T(8,128)(2,1)}, u32[]{:S(2)}) copy-start(bf16[768,1280]{1,0:T(8,128)(2,1)} %ow_ref.1) | copy-start | bytes 5898244
  0.7 2.4 %collective-permute-start = (bf16[4,64,1280]{2,1,0:T(8,128)(2,1)}, bf16[4,64,1280]{2,1,0:T(8,128)(2,1)S(1)}, u32[]{:S(2)}, u32[]{:S(2)}) collective-permute-start(bf16[4,64,1280]{2,1,0:T(8,128)(2,1)} %bitcast.3), channel_id=1, source_target_pairs={{0,64},{64,0},{128,192},{192,128},{1,65},{65,1},{129,193},{193,129... | collective-permute-start | bytes 1966088 | tf_op jit(solution)/shard_map/ppermute | solution.py:295
  0.8 7.4 %copy-start.5 = (bf16[1280,768]{1,0:T(8,128)(2,1)S(1)}, bf16[1280,768]{1,0:T(8,128)(2,1)}, u32[]{:S(2)}) copy-start(bf16[1280,768]{1,0:T(8,128)(2,1)} %qw_hbm.3) | copy-start | bytes 5898244
  0.8 7.4 %copy-start.9 = (f32[1280]{0:T(1024)S(1)}, f32[1280]{0:T(1024)}, u32[]{:S(2)}) copy-start(f32[1280]{0:T(1024)} %fg_ref.1) | copy-start | bytes 15364
  0.8 7.4 %copy-start.10 = (f32[1280]{0:T(1024)S(1)}, f32[1280]{0:T(1024)}, u32[]{:S(2)}) copy-start(f32[1280]{0:T(1024)} %lg_ref.3) | copy-start | bytes 15364
  3.0 5.1 %copy-start = (bf16[1280,1536]{1,0:T(8,128)(2,1)S(1)}, bf16[1280,1536]{1,0:T(8,128)(2,1)}, u32[]{:S(2)}) copy-start(bf16[1280,1536]{1,0:T(8,128)(2,1)} %kvw_hbm.3) | copy-start | bytes 11796484
  3.1 9.3 %copy-start.3 = (bf16[4,64,1280]{2,1,0:T(8,128)(2,1)}, bf16[4,64,1280]{2,1,0:T(8,128)(2,1)S(1)}, u32[]{:S(2)}) copy-start(bf16[4,64,1280]{2,1,0:T(8,128)(2,1)S(1)} %collective-permute-done.c1_ref.c1) | copy-start | bytes 1966084
  4.6 7.8 %collective-permute-start.1 = (bf16[256,256]{1,0:T(8,128)(2,1)S(1)}, bf16[256,256]{1,0:T(8,128)(2,1)S(1)}, u32[]{:S(2)}, u32[]{:S(2)}) collective-permute-start(bf16[256,256]{1,0:T(8,128)(2,1)S(1)} %get-tuple-element.36), channel_id=1, source_target_pairs={{0,128},{128,0},{64,192},{192,64},{1,129},{129,1},{65,193},{193,65... | collective-permute-start | bytes 393224 | tf_op jit(solution)/shard_map/ppermute | solution.py:295
  7.7 4.7 %copy-start.8 = (s32[1,4]{1,0:T(1,128)S(1)}, s32[1,4]{1,0:T(1,128)}, u32[]{:S(2)}) copy-start(s32[1,4]{1,0:T(1,128)} %sample_ref.3) | copy-start | bytes 52
  7.7 11.1 %collective-permute-start.2 = (bf16[2,64,1280]{2,1,0:T(8,128)(2,1)S(1)}, bf16[2,64,1280]{2,1,0:T(8,128)(2,1)S(1)}, u32[]{:S(2)}, u32[]{:S(2)}) collective-permute-start(bf16[2,64,1280]{2,1,0:T(8,128)(2,1)S(1)} %get-tuple-element.41), channel_id=1, source_target_pairs={{0,128},{128,0},{64,192},{192,64},{1,129},{129,1},{65,193},{193,65... | collective-permute-start | bytes 983048 | tf_op jit(solution)/shard_map/ppermute | solution.py:295
  14.9 3.4 %copy-start.6 = (bf16[128,768]{1,0:T(8,128)(2,1)}, bf16[128,768]{1,0:T(8,128)(2,1)S(1)}, u32[]{:S(2)}) copy-start(bf16[128,768]{1,0:T(8,128)(2,1)S(1)} %get-tuple-element.45.g0) | copy-start | bytes 589828
  18.8 18.2 %copy-start.13 = (bf16[2,64,1280]{2,1,0:T(8,128)(2,1)}, bf16[2,64,1280]{2,1,0:T(8,128)(2,1)S(1)}, u32[]{:S(2)}) copy-start(bf16[2,64,1280]{2,1,0:T(8,128)(2,1)S(1)} %collective-permute-done.2.u2) | copy-start | bytes 983044
  18.8 22.2 %all-to-all-start = ((bf16[16,240,128]{2,1,0:T(8,128)(2,1)}), bf16[16,240,128]{2,1,0:T(8,128)(2,1)S(1)}, u32[]{:S(2)}, u32[]{:S(2)}) async-start(bf16[16,240,128]{2,1,0:T(8,128)(2,1)} %weight_part.1), calls=%async_computation | async-start | bytes 1966080 | tf_op jit(solution)/shard_map/all_to_all | solution.py:361
  26.2 1.7 %collective-permute-start.3 = (bf16[256,768]{1,0:T(8,128)(2,1)S(1)}, bf16[256,768]{1,0:T(8,128)(2,1)S(1)}, u32[]{:S(2)}, u32[]{:S(2)}) collective-permute-start(bf16[256,768]{1,0:T(8,128)(2,1)S(1)} %get-tuple-element.44), channel_id=1, source_target_pairs={{0,64},{64,0},{128,192},{192,128},{1,65},{65,1},{129,193},{193,129... | collective-permute-start | bytes 1179656 | tf_op jit(solution)/shard_map/ppermute | solution.py:295
  27.9 0.8 %copy-start.11 = (bf16[256,768]{1,0:T(8,128)(2,1)}, bf16[256,768]{1,0:T(8,128)(2,1)S(1)}, u32[]{:S(2)}) copy-start(bf16[256,768]{1,0:T(8,128)(2,1)S(1)} %collective-permute-done.3.g1) | copy-start | bytes 1179652
  37.1 13.2 %collective-permute-start.4 = (bf16[256,768]{1,0:T(8,128)(2,1)S(1)}, bf16[256,768]{1,0:T(8,128)(2,1)S(1)}, u32[]{:S(2)}, u32[]{:S(2)}) collective-permute-start(bf16[256,768]{1,0:T(8,128)(2,1)S(1)} %pad_maximum_fusion), channel_id=1, source_target_pairs={{0,128},{128,0},{64,192},{192,64},{1,129},{129,1},{65,193},{193,65... | collective-permute-start | bytes 1179656 | tf_op jit(solution)/shard_map/ppermute | solution.py:295
  41.9 17.5 %all-to-all-start.1 = ((bf16[8,64,128]{2,1,0:T(8,128)(2,1)}), bf16[8,64,128]{2,1,0:T(8,128)(2,1)S(1)}, u32[]{:S(2)}, u32[]{:S(2)}) async-start(bf16[8,64,128]{2,1,0:T(8,128)(2,1)} %first_sum.1), calls=%async_computation.1 | async-start | bytes 262144 | tf_op jit(solution)/shard_map/all_to_all | solution.py:368
  50.3 0.8 %copy-start.12 = (bf16[256,768]{1,0:T(8,128)(2,1)}, bf16[256,768]{1,0:T(8,128)(2,1)S(1)}, u32[]{:S(2)}) copy-start(bf16[256,768]{1,0:T(8,128)(2,1)S(1)} %collective-permute-done.4.g2) | copy-start | bytes 1179652

commit v6 on v5

--- a/solution.py
+++ b/solution.py
@@ -170,11 +170,12 @@
             out[LAT * slot:LAT * (slot + 1)] = lat[pl.ds(pl.multiple_of(index * LAT, LAT), LAT)]
 
 
-def weight_kernel(ctx_ref, kvg, w_ref, wide, order):
+def weight_kernel(ctx_ref, kvg, w_hbm, wide, order, w_ref, sems):
     ctx = ctx_ref[...].reshape(IMGS * ROWS, D)
     for c in range(5):
         columns = slice(256 * c, 256 * (c + 1))
         wide[columns] = dot(ctx[:, columns], kvg[...], 0, 0)
+    copies = []
     for y in range(4):
         for xl in range(2):
             piece = xl * 4 + y
@@ -186,7 +187,12 @@
             vals = whole[:, 128:256], whole[:, 320:]
             for k, (main, tail) in enumerate((keys, vals)):
                 w_ref[8 * k + piece, 0:160] = main.astype(BF)
-                w_ref[8 * k + piece, 160:240] = jnp.concatenate([tail[:80], tail[80:]], axis=1).astype(BF)
+                at = 8 * k + piece
+                w_ref[at, 160:240] = jnp.concatenate([tail[:80], tail[80:]], axis=1).astype(BF)
+                copies.append(pltpu.make_async_copy(w_ref.at[at], w_hbm.at[at], sems.at[at]))
+                copies[-1].start()
+    for c in copies:
+        c.wait()
 
 
 def first_sum_kernel(r_ref, out_ref, full, share):
@@ -278,12 +284,12 @@
 SECTION = ("xh", "co")
 
 
-def call(body, name, outs, ins, scratch=(), flops=0, size=0, limit=24):
+def call(body, name, outs, ins, scratch=(), flops=0, size=0, limit=24, place=VMEM):
     return pl.pallas_call(
         body,
         out_shape=outs,
         in_specs=ins,
-        out_specs=jax.tree.map(lambda _: VMEM, outs),
+        out_specs=jax.tree.map(lambda _: place, outs),
         scratch_shapes=list(scratch),
         cost_estimate=pl.CostEstimate(flops=flops, bytes_accessed=size, transcendentals=0),
         compiler_params=pltpu.CompilerParams(vmem_limit_bytes=limit * 2**20),
@@ -324,7 +330,8 @@
         flops=COST, size=1000),
     weight=call(
         weight_kernel, "weight_part", bf(16, 240, 128), [VMEM] * 2,
-        [pltpu.VMEM((D, 384), F32), pltpu.VMEM((8, 160, 384), F32)],
+        [pltpu.VMEM((D, 384), F32), pltpu.VMEM((8, 160, 384), F32), pltpu.VMEM((16, 240, 128), BF), DMA((16,))],
+        place=HBM,
         flops=COST, size=1000),
     first=call(first_sum_kernel, "first_sum", bf(8, 64, 128), [VMEM],
                [pltpu.VMEM((160, 384), F32), pltpu.VMEM((8, 64, 128), F32)],

time: 60.3 us -> 60.4 us (level)
  no operation moved by 1% of the time
where the time goes in v6:
time: 60.4 us; the launch traced here: 60.2 us
  Pallas kernels  26.3 us (44%)
  starting transfers between devices  22.7 us (38%)
  waiting for transfers between devices  6.21 us (10%)
  local copies, waits for them, and re-layouts  4.09 us (7%)
  between operations  0.86 us (1%)
    all_to_all x1, starting transfers between devices, per_device(): w = lax.all_to_all(w, 'z', 0, 0, tiled=True)  8.52 us
    pallas_call x1, Pallas kernels, per_device(): CALLS['near'](owner, part, latents, query_weight, kv_weight, c1, g0, g1)  8.34 us
    all_to_all x1, starting transfers between devices, per_device(): w = lax.all_to_all(w, ('xh', 'xl', 'y'), 0, 0, tiled=True)  7.4 us
    ppermute x5, starting transfers between devices, swap(): return lax.ppermute(x, SECTION, pairs)  6.78 us
    pallas_call x1, Pallas kernels, per_device(): latent_grad = CALLS['latent'](owner, sample_of, latent_gain, *near, u, g2)  5.17 us
    pallas_call x1, Pallas kernels, per_device(): CALLS['forward']  4.17 us
    unnamed x29, local copies, waits for them, and re-layouts  4.08 us
    pallas_call x1, Pallas kernels, per_device(): w = CALLS['weight'](ctx, kvg)  3.49 us
  transfers between devices with their start and end apart: 7, of which 4 were waited for; matrix products, arithmetic and copies ran while one was open for 4% of the time, Pallas kernels for 41%

profile of v6, /device:TPU:8, one launch (start us, length us, event | category | flops | bytes accessed | tf_op | source)
XLA Modules:
  0.0 60.2 jit_solution(6532919115307901747)
XLA Ops:
  0.6 0.0 copy-start.1
  0.6 0.0 copy-start.2
  0.7 0.0 copy-start.7
  0.7 0.0 copy-start.4
  0.7 0.1 collective-permute-start
  0.8 0.0 copy-start.5
  0.8 0.0 copy-start.9
  0.8 0.0 copy-start.10
  0.8 2.2 %copy.12.feat_ref = bf16[4,257,1280]{2,1,0:T(8,128)(2,1)S(1)} copy(bf16[4,257,1280]{2,0,1:T(4,128)(2,1)} %param.12) | data formatting | bytes 5263360 | tf_op args[2]
  3.0 0.0 copy-start
  3.1 0.0 collective-permute-done.c1_ref.c1
  3.1 0.0 copy-start.3
  3.1 0.0 copy-done.1
  3.1 0.0 copy-done.2
  3.1 0.0 copy-done.7
  3.1 0.3 copy-done.4
  3.4 1.2 %attn_part.1 = (f32[256,256]{1,0:T(8,128)S(1)}, bf16[256,256]{1,0:T(8,128)(2,1)S(1)}, bf16[2,64,1280]{2,1,0:T(8,128)(2,1)S(1)}) custom-call(s32[1,4]{1,0:T(1,128)S(1)} %bitcast.8, bf16[4,64,1280]{2,1,0:T(8,128)(2,1)S(1)} %bitcast.5, bf16[4,64,1280]{2,1,0:T(8,128)(2,1)S(1)} %collective-permute-done.c1_ref.c1, bf16[768,1280]{1,0:T(8,128)(2,1)S(1)} %copy-done.4, ...), custom_call_target="tpu_custom_call" | custom-call | flops 600000000 | bytes 3000000 | tf_op jit(solution)/shard_map/attn_part/pallas_call | solution.py:358
  4.6 3.1 %collective-permute-start.1 = (bf16[256,256]{1,0:T(8,128)(2,1)S(1)}, bf16[256,256]{1,0:T(8,128)(2,1)S(1)}, u32[]{:S(2)}, u32[]{:S(2)}) collective-permute-start(bf16[256,256]{1,0:T(8,128)(2,1)S(1)} %get-tuple-element.36), channel_id=1, source_target_pairs={{0,128},{128,0},{64,192},{192,64},{1,129},{129,1},{65,193},{193,65... | collective-permute-start | bytes 393224 | tf_op jit(solution)/shard_map/ppermute | solution.py:301
  7.7 0.0 copy-start.8
  7.7 0.5 collective-permute-start.2
  8.2 0.0 copy-done.5
  8.2 0.0 copy-done.9
  8.2 0.0 copy-done.10
  8.2 0.0 copy-done
  8.2 4.2 %forward_part.1 = (bf16[4,336,1280]{2,1,0:T(8,128)(2,1)S(1)}, bf16[4,336,512]{2,1,0:T(8,128)(2,1)S(1)}, bf16[4,128,256]{2,1,0:T(8,128)(2,1)S(1)}, f32[4,128,336]{2,1,0:T(8,128)S(1)}) custom-call(bf16[4,257,1280]{2,1,0:T(8,128)(2,1)S(1)} %copy.12.feat_ref, bf16[4,64,1280]{2,1,0:T(8,128)(2,1)S(1)} %copy-done.2, f32[1280]{0:T(1024)S(1)} %copy-done.9, ...), custom_call_target="tpu_custom_call" | custom-call | flops 4000000000 | bytes 12000000 | tf_op jit(solution)/shard_map/forward_part/pallas_call | solution.py:361
  12.4 0.0 copy-done.3
  12.4 0.0 collective-permute-done.1.a2
  12.4 0.0 copy-done.8
  12.4 2.5 %backward_part.1 = (bf16[1344,384]{1,0:T(8,128)(2,1)S(1)}, bf16[128,768]{1,0:T(8,128)(2,1)S(1)}, bf16[256,768]{1,0:T(8,128)(2,1)S(1)}, bf16[128,768]{1,0:T(8,128)(2,1)S(1)}) custom-call(s32[1,4]{1,0:T(1,128)S(1)} %bitcast.9, s32[1,4]{1,0:T(1,128)S(1)} %copy-done.8, f32[256,256]{1,0:T(8,128)S(1)} %get-tuple-element.35.a0, ...), custom_call_target="tpu_custom_call" | custom-call | flops 1000000 | bytes 1000 | tf_op jit(solution)/shard_map/backward_part/pallas_call | solution.py:363
  14.9 0.0 copy-start.6
  14.9 3.5 %weight_part.1 = bf16[16,240,128]{2,1,0:T(8,128)(2,1)} custom-call(bf16[4,336,1280]{2,1,0:T(8,128)(2,1)S(1)} %get-tuple-element.34.ctx_ref, bf16[1344,384]{1,0:T(8,128)(2,1)S(1)} %get-tuple-element.40.kvg), custom_call_target="tpu_custom_call" | custom-call | flops 1000000 | bytes 1000 | tf_op jit(solution)/shard_map/weight_part/pallas_call | solution.py:366
  18.4 0.0 copy-done.6
  18.4 0.4 collective-permute-done.2.u2
  18.8 0.0 copy-start.13
  18.8 7.4 %all-to-all-start = ((bf16[16,240,128]{2,1,0:T(8,128)(2,1)}), bf16[16,240,128]{2,1,0:T(8,128)(2,1)S(1)}, u32[]{:S(2)}, u32[]{:S(2)}) async-start(bf16[16,240,128]{2,1,0:T(8,128)(2,1)} %weight_part.1), calls=%async_computation | async-start | bytes 1966080 | tf_op jit(solution)/shard_map/all_to_all | solution.py:368
  26.2 0.0 collective-permute-start.3
  26.2 1.7 %collective-permute-done.3.g1 = bf16[256,768]{1,0:T(8,128)(2,1)S(1)} collective-permute-done((bf16[256,768]{1,0:T(8,128)(2,1)S(1)}, bf16[256,768]{1,0:T(8,128)(2,1)S(1)}, u32[]{:S(2)}, u32[]{:S(2)}) %collective-permute-start.3) | collective-permute-done | bytes 393248 | tf_op jit(solution)/shard_map/ppermute | solution.py:301
  27.9 0.0 copy-start.11
  28.0 0.7 %copy-done.11 = bf16[256,768]{1,0:T(8,128)(2,1)} copy-done((bf16[256,768]{1,0:T(8,128)(2,1)}, bf16[256,768]{1,0:T(8,128)(2,1)S(1)}, u32[]{:S(2)}) %copy-start.11) | copy-done | bytes 393240
  28.7 8.3 %near_part.1 = (f32[1280,128]{1,0:T(8,128)}, f32[128,1280]{1,0:T(8,128)}, f32[128,1280]{1,0:T(8,128)}, f32[128,128]{1,0:T(8,128)}, bf16[6,1280,256]{2,1,0:T(8,128)(2,1)}) custom-call(s32[1,4]{1,0:T(1,128)} %bitcast.6, bf16[4,64,1280]{2,1,0:T(8,128)(2,1)} %bitcast.4, bf16[4,64,1280]{2,1,0:T(8,128)(2,1)} %lat_ref.5, bf16[1280,768]{1,0:T(8,128)(2,1)} %qw_hbm.3, ...), custom_call_target="tpu_custom_call" | custom-call | flops 1000000 | bytes 1000 | tf_op jit(solution)/shard_map/near_part/pallas_call | solution.py:369
  37.0 0.0 copy-done.13
  37.1 3.1 %collective-permute-start.4 = (bf16[256,768]{1,0:T(8,128)(2,1)S(1)}, bf16[256,768]{1,0:T(8,128)(2,1)S(1)}, u32[]{:S(2)}, u32[]{:S(2)}) collective-permute-start(bf16[256,768]{1,0:T(8,128)(2,1)S(1)} %pad_maximum_fusion), channel_id=1, source_target_pairs={{0,128},{128,0},{64,192},{192,64},{1,129},{129,1},{65,193},{193,65... | collective-permute-start | bytes 1179656 | tf_op jit(solution)/shard_map/ppermute | solution.py:301
  40.2 0.9 %all-to-all-done.r_ref = bf16[16,240,128]{2,1,0:T(8,128)(2,1)S(1)} async-done(((bf16[16,240,128]{2,1,0:T(8,128)(2,1)}), bf16[16,240,128]{2,1,0:T(8,128)(2,1)S(1)}, u32[]{:S(2)}, u32[]{:S(2)}) %all-to-all-start) | async-done | bytes 983072 | tf_op jit(solution)/shard_map/all_to_all | solution.py:368
  41.1 0.8 %first_sum.1 = bf16[8,64,128]{2,1,0:T(8,128)(2,1)} custom-call(bf16[16,240,128]{2,1,0:T(8,128)(2,1)S(1)} %all-to-all-done.r_ref), custom_call_target="tpu_custom_call" | custom-call | bytes 1000000 | tf_op jit(solution)/shard_map/first_sum/pallas_call | solution.py:373
  41.9 8.5 %all-to-all-start.1 = ((bf16[8,64,128]{2,1,0:T(8,128)(2,1)}), bf16[8,64,128]{2,1,0:T(8,128)(2,1)S(1)}, u32[]{:S(2)}, u32[]{:S(2)}) async-start(bf16[8,64,128]{2,1,0:T(8,128)(2,1)} %first_sum.1), calls=%async_computation.1 | async-start | bytes 262144 | tf_op jit(solution)/shard_map/all_to_all | solution.py:375
  50.4 0.0 collective-permute-done.4.g2
  50.4 0.0 copy-start.12
  50.4 0.7 %copy-done.12 = bf16[256,768]{1,0:T(8,128)(2,1)} copy-done((bf16[256,768]{1,0:T(8,128)(2,1)}, bf16[256,768]{1,0:T(8,128)(2,1)S(1)}, u32[]{:S(2)}) %copy-start.12) | copy-done | bytes 393240
  51.2 5.2 %latent_part.1 = bf16[2,64,1280]{2,1,0:T(8,128)(2,1)} custom-call(s32[1,4]{1,0:T(1,128)} %bitcast.7, s32[1,4]{1,0:T(1,128)} %sample_ref.3, f32[1280]{0:T(1024)} %lg_ref.3, f32[1280,128]{1,0:T(8,128)} %get-tuple-element.57.acc_ref, f32[128,1280]{1,0:T(8,128)} %get-tuple-element.58.up_ref, f32[128,1280]{1,0:T(8,128)} %get-tuple-element.59.hat_ref, ...), custom_call_target="tpu_custom_call" | custom-call | flops 2000000000 | bytes 9000000 | tf_op jit(solution)/shard_map/latent_part/pallas_call | solution.py:374
  56.4 3.2 %all-to-all-done.1.r_ref = bf16[8,64,128]{2,1,0:T(8,128)(2,1)S(1)} async-done(((bf16[8,64,128]{2,1,0:T(8,128)(2,1)}), bf16[8,64,128]{2,1,0:T(8,128)(2,1)S(1)}, u32[]{:S(2)}, u32[]{:S(2)}) %all-to-all-start.1) | async-done | bytes 131104 | tf_op jit(solution)/shard_map/all_to_all | solution.py:375
  59.5 0.6 %last_sum.1 = f32[20,384]{1,0:T(8,128)} custom-call(bf16[8,64,128]{2,1,0:T(8,128)(2,1)S(1)} %all-to-all-done.1.r_ref), custom_call_target="tpu_custom_call" | custom-call | bytes 300000 | tf_op jit(solution)/shard_map/last_sum/pallas_call | solution.py:377
  (2 shorter events, 0.0 us)
Async XLA Ops:
  0.6 2.5 %copy-start.1 = (bf16[1,4,64,1280]{3,2,1,0:T(8,128)(2,1)S(1)}, bf16[1,4,64,1280]{3,2,1,0:T(8,128)(2,1)}, u32[]{:S(2)}) copy-start(bf16[1,4,64,1280]{3,2,1,0:T(8,128)(2,1)} %param.10) | copy-start | bytes 1966084
  0.6 2.4 %copy-start.2 = (bf16[4,64,1280]{2,1,0:T(8,128)(2,1)S(1)}, bf16[4,64,1280]{2,1,0:T(8,128)(2,1)}, u32[]{:S(2)}) copy-start(bf16[4,64,1280]{2,1,0:T(8,128)(2,1)} %lat_ref.5) | copy-start | bytes 1966084
  0.7 2.4 %copy-start.7 = (s32[4,1]{0,1:T(1,128)S(1)}, s32[4,1]{0,1:T(1,128)}, u32[]{:S(2)}) copy-start(s32[4,1]{0,1:T(1,128)} %param.19) | copy-start | bytes 52
  0.7 2.7 %copy-start.4 = (bf16[768,1280]{1,0:T(8,128)(2,1)S(1)}, bf16[768,1280]{1,0:T(8,128)(2,1)}, u32[]{:S(2)}) copy-start(bf16[768,1280]{1,0:T(8,128)(2,1)} %ow_ref.1) | copy-start | bytes 5898244
  0.7 2.4 %collective-permute-start = (bf16[4,64,1280]{2,1,0:T(8,128)(2,1)}, bf16[4,64,1280]{2,1,0:T(8,128)(2,1)S(1)}, u32[]{:S(2)}, u32[]{:S(2)}) collective-permute-start(bf16[4,64,1280]{2,1,0:T(8,128)(2,1)} %bitcast.3), channel_id=1, source_target_pairs={{0,64},{64,0},{128,192},{192,128},{1,65},{65,1},{129,193},{193,129... | collective-permute-start | bytes 1966088 | tf_op jit(solution)/shard_map/ppermute | solution.py:301
  0.8 7.4 %copy-start.5 = (bf16[1280,768]{1,0:T(8,128)(2,1)S(1)}, bf16[1280,768]{1,0:T(8,128)(2,1)}, u32[]{:S(2)}) copy-start(bf16[1280,768]{1,0:T(8,128)(2,1)} %qw_hbm.3) | copy-start | bytes 5898244
  0.8 7.4 %copy-start.9 = (f32[1280]{0:T(1024)S(1)}, f32[1280]{0:T(1024)}, u32[]{:S(2)}) copy-start(f32[1280]{0:T(1024)} %fg_ref.1) | copy-start | bytes 15364
  0.8 7.4 %copy-start.10 = (f32[1280]{0:T(1024)S(1)}, f32[1280]{0:T(1024)}, u32[]{:S(2)}) copy-start(f32[1280]{0:T(1024)} %lg_ref.3) | copy-start | bytes 15364
  3.0 5.1 %copy-start = (bf16[1280,1536]{1,0:T(8,128)(2,1)S(1)}, bf16[1280,1536]{1,0:T(8,128)(2,1)}, u32[]{:S(2)}) copy-start(bf16[1280,1536]{1,0:T(8,128)(2,1)} %kvw_hbm.3) | copy-start | bytes 11796484
  3.1 9.3 %copy-start.3 = (bf16[4,64,1280]{2,1,0:T(8,128)(2,1)}, bf16[4,64,1280]{2,1,0:T(8,128)(2,1)S(1)}, u32[]{:S(2)}) copy-start(bf16[4,64,1280]{2,1,0:T(8,128)(2,1)S(1)} %collective-permute-done.c1_ref.c1) | copy-start | bytes 1966084
  4.6 7.8 %collective-permute-start.1 = (bf16[256,256]{1,0:T(8,128)(2,1)S(1)}, bf16[256,256]{1,0:T(8,128)(2,1)S(1)}, u32[]{:S(2)}, u32[]{:S(2)}) collective-permute-start(bf16[256,256]{1,0:T(8,128)(2,1)S(1)} %get-tuple-element.36), channel_id=1, source_target_pairs={{0,128},{128,0},{64,192},{192,64},{1,129},{129,1},{65,193},{193,65... | collective-permute-start | bytes 393224 | tf_op jit(solution)/shard_map/ppermute | solution.py:301
  7.7 4.7 %copy-start.8 = (s32[1,4]{1,0:T(1,128)S(1)}, s32[1,4]{1,0:T(1,128)}, u32[]{:S(2)}) copy-start(s32[1,4]{1,0:T(1,128)} %sample_ref.3) | copy-start | bytes 52
  7.7 11.1 %collective-permute-start.2 = (bf16[2,64,1280]{2,1,0:T(8,128)(2,1)S(1)}, bf16[2,64,1280]{2,1,0:T(8,128)(2,1)S(1)}, u32[]{:S(2)}, u32[]{:S(2)}) collective-permute-start(bf16[2,64,1280]{2,1,0:T(8,128)(2,1)S(1)} %get-tuple-element.41), channel_id=1, source_target_pairs={{0,128},{128,0},{64,192},{192,64},{1,129},{129,1},{65,193},{193,65... | collective-permute-start | bytes 983048 | tf_op jit(solution)/shard_map/ppermute | solution.py:301
  14.9 3.5 %copy-start.6 = (bf16[128,768]{1,0:T(8,128)(2,1)}, bf16[128,768]{1,0:T(8,128)(2,1)S(1)}, u32[]{:S(2)}) copy-start(bf16[128,768]{1,0:T(8,128)(2,1)S(1)} %get-tuple-element.45.g0) | copy-start | bytes 589828
  18.8 18.2 %copy-start.13 = (bf16[2,64,1280]{2,1,0:T(8,128)(2,1)}, bf16[2,64,1280]{2,1,0:T(8,128)(2,1)S(1)}, u32[]{:S(2)}) copy-start(bf16[2,64,1280]{2,1,0:T(8,128)(2,1)S(1)} %collective-permute-done.2.u2) | copy-start | bytes 983044
  18.8 22.3 %all-to-all-start = ((bf16[16,240,128]{2,1,0:T(8,128)(2,1)}), bf16[16,240,128]{2,1,0:T(8,128)(2,1)S(1)}, u32[]{:S(2)}, u32[]{:S(2)}) async-start(bf16[16,240,128]{2,1,0:T(8,128)(2,1)} %weight_part.1), calls=%async_computation | async-start | bytes 1966080 | tf_op jit(solution)/shard_map/all_to_all | solution.py:368
  26.2 1.7 %collective-permute-start.3 = (bf16[256,768]{1,0:T(8,128)(2,1)S(1)}, bf16[256,768]{1,0:T(8,128)(2,1)S(1)}, u32[]{:S(2)}, u32[]{:S(2)}) collective-permute-start(bf16[256,768]{1,0:T(8,128)(2,1)S(1)} %get-tuple-element.44), channel_id=1, source_target_pairs={{0,64},{64,0},{128,192},{192,128},{1,65},{65,1},{129,193},{193,129... | collective-permute-start | bytes 1179656 | tf_op jit(solution)/shard_map/ppermute | solution.py:301
  27.9 0.8 %copy-start.11 = (bf16[256,768]{1,0:T(8,128)(2,1)}, bf16[256,768]{1,0:T(8,128)(2,1)S(1)}, u32[]{:S(2)}) copy-start(bf16[256,768]{1,0:T(8,128)(2,1)S(1)} %collective-permute-done.3.g1) | copy-start | bytes 1179652
  37.1 13.3 %collective-permute-start.4 = (bf16[256,768]{1,0:T(8,128)(2,1)S(1)}, bf16[256,768]{1,0:T(8,128)(2,1)S(1)}, u32[]{:S(2)}, u32[]{:S(2)}) collective-permute-start(bf16[256,768]{1,0:T(8,128)(2,1)S(1)} %pad_maximum_fusion), channel_id=1, source_target_pairs={{0,128},{128,0},{64,192},{192,64},{1,129},{129,1},{65,193},{193,65... | collective-permute-start | bytes 1179656 | tf_op jit(solution)/shard_map/ppermute | solution.py:301
  41.9 17.6 %all-to-all-start.1 = ((bf16[8,64,128]{2,1,0:T(8,128)(2,1)}), bf16[8,64,128]{2,1,0:T(8,128)(2,1)S(1)}, u32[]{:S(2)}, u32[]{:S(2)}) async-start(bf16[8,64,128]{2,1,0:T(8,128)(2,1)} %first_sum.1), calls=%async_computation.1 | async-start | bytes 262144 | tf_op jit(solution)/shard_map/all_to_all | solution.py:375
  50.4 0.8 %copy-start.12 = (bf16[256,768]{1,0:T(8,128)(2,1)}, bf16[256,768]{1,0:T(8,128)(2,1)S(1)}, u32[]{:S(2)}) copy-start(bf16[256,768]{1,0:T(8,128)(2,1)S(1)} %collective-permute-done.4.g2) | copy-start | bytes 1179652
